TPU v7x, 32 devices: a whole 2x2x4 slice. The times are simulated.
32 devices in a mesh: tm: 16 (over z, y, x), dp: 2 (over core).
Axes of the slice: x: 2, y: 2, z: 4, core: 2. Of those that a mesh axis runs over, the one named last changes fastest.
Arguments:
- movie: bfloat16 [2, 64, 8, 16, 128], P('dp', 'tm'), may hold values from -6 to 6
- kernel_one: bfloat16 [3456, 128], replicated, may hold values from -0.15625 to 0.15625
- kernel_two: bfloat16 [3456, 128], replicated, may hold values from -0.15625 to 0.15625
- upstream: bfloat16 [2, 64, 8, 16, 128], P('dp', 'tm'), may hold values from -6 to 6
Outputs:
- output: bfloat16 [2, 64, 8, 16, 128], P('dp', 'tm')
- movie_grad: bfloat16 [2, 64, 8, 16, 128], P('dp', 'tm')
- grad_one: float32 [3456, 128], P('tm')
- grad_two: float32 [3456, 128], P('tm')
All inputs are finite; a program needn't handle non-finite values.
Results may differ from a plain program's by a relative error of at most 0.0053.
Values may be sent and summed in bfloat16 or wider, within the bound.
No kernel may reach another device: no remote copies, remote signals or barrier semaphores. Data moves between devices by JAX's collectives and lax.ppermute only.
A program may use at most 64 MiB of HBM per device.

v0:
```python
import jax
import jax.numpy as jnp
from jax import lax
from jax.sharding import PartitionSpec as P


def passed_along(block, axis, distance):
    devices = range(lax.axis_size(axis))
    route = [(i - distance, i) for i in devices if i - distance in devices]
    return lax.ppermute(block, axis, route)


def silu_grad(value):
    sig = jax.nn.sigmoid(value)
    return sig * (1.0 + value * (1.0 - sig))


def conv_valid(field, weights):
    return lax.conv_general_dilated(
        field,
        weights,
        (1, 1, 1),
        ((0, 0), (1, 1), (1, 1)),
        dimension_numbers=("NDHWC", "DHWIO", "NDHWC"),
        preferred_element_type=jnp.float32,
    )


def forward_kernel(kernel):
    chans = kernel.shape[1]
    return kernel.reshape(3, 3, 3, chans, chans)


def backward_kernel(kernel):
    chans = kernel.shape[1]
    return kernel.reshape(3, 3, 3, chans, chans)[::-1, ::-1, ::-1].swapaxes(3, 4)


def kernel_grad(extended, grads):
    frames, height, width = (grads.shape[1], grads.shape[2], grads.shape[3])
    padded = jnp.pad(extended, ((0, 0), (0, 0), (1, 1), (1, 1), (0, 0)))
    flat_grad = grads.reshape(-1, grads.shape[4])
    blocks = []
    for offset_t in range(3):
        for offset_i in range(3):
            for offset_j in range(3):
                piece = padded[
                    :,
                    offset_t : offset_t + frames,
                    offset_i : offset_i + height,
                    offset_j : offset_j + width,
                ]
                piece = piece.reshape(-1, piece.shape[4])
                blocks.append(
                    lax.dot_general(
                        piece,
                        flat_grad,
                        (((0,), (0,)), ((), ())),
                        preferred_element_type=jnp.float32,
                    )
                )
    return jnp.concatenate(blocks, axis=0)


def body(movie, kernel_one, kernel_two, upstream):
    frames = movie.shape[1]
    movie_f = movie.astype(jnp.float32)
    act_in = jax.nn.silu(movie_f).astype(jnp.bfloat16)
    first_fwd = forward_kernel(kernel_one)
    second_fwd = forward_kernel(kernel_two)
    first_back = backward_kernel(kernel_one)
    second_back = backward_kernel(kernel_two)
    before = passed_along(act_in[:, frames - 2 :], "tm", 1)
    act_in_ext = jnp.concatenate([before, act_in], axis=1)
    pre = conv_valid(act_in_ext, first_fwd)
    act_mid = jax.nn.silu(pre).astype(jnp.bfloat16)
    mid_before = passed_along(act_mid[:, frames - 2 :], "tm", 1)
    act_mid_ext = jnp.concatenate([mid_before, act_mid], axis=1)
    output = (movie_f + conv_valid(act_mid_ext, second_fwd)).astype(jnp.bfloat16)
    after = passed_along(upstream[:, :2], "tm", -1)
    mid_grad = conv_valid(jnp.concatenate([upstream, after], axis=1), second_back)
    pre_grad = (mid_grad * silu_grad(pre)).astype(jnp.bfloat16)
    grad_after = passed_along(pre_grad[:, :2], "tm", -1)
    pre_grad_ext = jnp.concatenate([pre_grad, grad_after], axis=1)
    in_grad = conv_valid(pre_grad_ext, first_back)
    movie_grad = (upstream.astype(jnp.float32) + in_grad * silu_grad(movie_f)).astype(jnp.bfloat16)
    grad_two_term = kernel_grad(act_mid_ext, upstream)
    grad_one_term = kernel_grad(act_in_ext, pre_grad)
    both_terms = jnp.concatenate([grad_one_term, grad_two_term], axis=1)
    chans = kernel_one.shape[1]
    partial_rows = lax.psum_scatter(both_terms, "tm", scatter_dimension=0, tiled=True)
    mine = lax.psum(partial_rows, "dp")
    return (output, movie_grad, mine[:, :chans], mine[:, chans:])


def solution(mesh):
    in_specs = (P("dp", "tm", None, None, None), P(), P(), P("dp", "tm", None, None, None))
    out_specs = (
        P("dp", "tm", None, None, None),
        P("dp", "tm", None, None, None),
        P("tm", None),
        P("tm", None),
    )
    return jax.shard_map(body, mesh=mesh, in_specs=in_specs, out_specs=out_specs, check_vma=False)
```

profile of v0, /device:TPU:0, one launch (start us, length us, event | category | flops | bytes accessed | tf_op | source)
XLA Modules:
  0.0 207.8 jit_solution(17254498826794649063)
XLA Ops:
  7.2 1.0 copy.21
  8.3 1.3 collective-permute-start.2
  9.6 1.0 fusion.87
  10.6 5.5 %collective-permute-start = (bf16[1,2,8,16,128]{4,3,2,1,0:T(8,128)(2,1)S(1)}, bf16[1,2,8,16,128]{4,3,2,1,0:T(8,128)(2,1)S(1)}, u32[]{:S(2)}, u32[]{:S(2)}) collective-permute-start(bf16[1,2,8,16,128]{4,3,2,1,0:T(8,128)(2,1)S(1)} %slice.252), channel_id=1, source_target_pairs={{0,2},{2,4},{4,6},{6,8},{8,10},{10,12},{12,14},{14,16},{16,18},{18... | collective-permute-start | bytes 196616 | tf_op jit(solution)/shard_map/ppermute | solution.py:10
  16.2 1.8 collective-permute-done
  18.3 1.6 multiply_convert_fusion
  19.9 1.5 fusion.1
  21.6 4.7 %collective-permute-start.1 = (bf16[1,2,8,16,128]{4,3,2,1,0:T(8,128)(2,1)S(1)}, bf16[1,2,8,16,128]{4,3,2,1,0:T(8,128)(2,1)S(1)}, u32[]{:S(2)}, u32[]{:S(2)}) collective-permute-start(bf16[1,2,8,16,128]{4,3,2,1,0:T(8,128)(2,1)S(1)} %bitcast.670), channel_id=1, source_target_pairs={{0,2},{2,4},{4,6},{6,8},{8,10},{10,12},{12,14},{14,16},{16,18},{18... | collective-permute-start | bytes 196616 | tf_op jit(solution)/shard_map/ppermute | solution.py:10
  31.5 0.3 fusion.33
  32.8 0.3 copy-done.2
  33.8 0.2 fusion.25
  34.3 0.2 fusion.23
  34.6 0.2 fusion.22
  35.0 0.2 fusion.20
  36.0 0.2 fusion.16
  36.5 0.2 fusion.14
  36.7 0.2 fusion.13
  37.2 0.2 fusion.11
  38.1 0.2 fusion.7
  38.6 0.2 fusion.5
  38.8 0.2 fusion.4
  39.1 0.2 fusion.3
  39.3 0.2 fusion.2
  39.6 2.0 pad_maximum_fusion
  41.7 1.5 collective-permute-start.3
  43.2 5.9 %collective-permute-done.3 = bf16[1,2,8,16,128]{4,3,2,1,0:T(8,128)(2,1)S(1)} collective-permute-done((bf16[1,2,8,16,128]{4,3,2,1,0:T(8,128)(2,1)S(1)}, bf16[1,2,8,16,128]{4,3,2,1,0:T(8,128)(2,1)S(1)}, u32[]{:S(2)}, u32[]{:S(2)}) %collective-permute-start.3) | collective-permute-done | bytes 65568 | tf_op jit(solution)/shard_map/ppermute | solution.py:10
  49.3 1.5 convolution_select_fusion
  51.2 1.5 convolution_select_fusion.2
  52.8 126.7 %reduce-scatter.2.cloned.1.call-done = f32[216,256]{1,0:T(8,128)} async-done(((f32[3456,256]{1,0:T(8,128)}), f32[216,256]{1,0:T(8,128)}) %reduce-scatter.2.cloned.1.call-update) | async-done | bytes 221200 | tf_op jit(solution)/shard_map/reduce_scatter | solution.py:91
  179.6 0.8 fusion.93
  180.4 18.8 %all-reduce.4.cloned.1.call-done = f32[216,256]{1,0:T(8,128)} async-done(((f32[216,256]{1,0:T(8,128)}), f32[216,256]{1,0:T(8,128)}) %all-reduce.4.cloned.1.call-update) | async-done | bytes 221200 | tf_op jit(solution)/shard_map/psum | solution.py:92
  199.3 1.6 fusion.357
  (94 shorter events, 10.4 us)
Async XLA Ops:
  7.2 11.1 %copy-start = (bf16[3456,128]{1,0:T(8,128)(2,1)S(1)}, bf16[3456,128]{1,0:T(8,128)(2,1)}, u32[]{:S(2)}) copy-start(bf16[3456,128]{1,0:T(8,128)(2,1)} %param.5) | copy-start | bytes 2654212
  7.2 172.4 %reduce-scatter.2.cloned.1.call-start = ((), (), s32[]{:S(2)}) async-start(), calls=%async_computation.1 | async-start | bytes 3760128 | tf_op jit(solution)/shard_map/reduce_scatter | solution.py:91
  8.3 7.8 %collective-permute-start.2 = (bf16[1,2,8,16,128]{4,2,3,1,0:T(8,128)(2,1)S(1)}, bf16[1,2,8,16,128]{4,2,3,1,0:T(8,128)(2,1)S(1)}, u32[]{:S(2)}, u32[]{:S(2)}) collective-permute-start(bf16[1,2,8,16,128]{4,2,3,1,0:T(8,128)(2,1)S(1)} %slice.259), channel_id=1, source_target_pairs={{2,0},{4,2},{6,4},{8,6},{10,8},{12,10},{14,12},{16,14},{18,16},{20... | collective-permute-start | bytes 196616 | tf_op jit(solution)/shard_map/ppermute | solution.py:10
  10.6 7.5 %collective-permute-start = (bf16[1,2,8,16,128]{4,3,2,1,0:T(8,128)(2,1)S(1)}, bf16[1,2,8,16,128]{4,3,2,1,0:T(8,128)(2,1)S(1)}, u32[]{:S(2)}, u32[]{:S(2)}) collective-permute-start(bf16[1,2,8,16,128]{4,3,2,1,0:T(8,128)(2,1)S(1)} %slice.252), channel_id=1, source_target_pairs={{0,2},{2,4},{4,6},{6,8},{8,10},{10,12},{12,14},{14,16},{16,18},{18... | collective-permute-start | bytes 196616 | tf_op jit(solution)/shard_map/ppermute | solution.py:10
  16.1 2.2 %copy-start.4 = (pred[8,3]{0,1:T(4,128)(4,1)S(1)}, pred[8,3]{0,1:T(4,128)(4,1)}, u32[]{:S(2)}) copy-start(pred[8,3]{0,1:T(4,128)(4,1)} %constant.30) | copy-start | bytes 76
  18.3 1.6 copy-start.3
  21.6 11.2 %collective-permute-start.1 = (bf16[1,2,8,16,128]{4,3,2,1,0:T(8,128)(2,1)S(1)}, bf16[1,2,8,16,128]{4,3,2,1,0:T(8,128)(2,1)S(1)}, u32[]{:S(2)}, u32[]{:S(2)}) collective-permute-start(bf16[1,2,8,16,128]{4,3,2,1,0:T(8,128)(2,1)S(1)} %bitcast.670), channel_id=1, source_target_pairs={{0,2},{2,4},{4,6},{6,8},{8,10},{10,12},{12,14},{14,16},{16,18},{18... | collective-permute-start | bytes 196616 | tf_op jit(solution)/shard_map/ppermute | solution.py:10
  30.5 1.0 copy-start.1
  32.2 0.9 copy-start.2
  41.6 157.7 %all-reduce.4.cloned.1.call-start = ((), (), s32[]{:S(2)}) async-start(), calls=%async_computation.2 | async-start | bytes 442368 | tf_op jit(solution)/shard_map/psum | solution.py:92
  41.7 7.4 %collective-permute-start.3 = (bf16[1,2,8,16,128]{4,3,2,1,0:T(8,128)(2,1)S(1)}, bf16[1,2,8,16,128]{4,3,2,1,0:T(8,128)(2,1)S(1)}, u32[]{:S(2)}, u32[]{:S(2)}) collective-permute-start(bf16[1,2,8,16,128]{4,3,2,1,0:T(8,128)(2,1)S(1)} %bitcast.671), channel_id=1, source_target_pairs={{2,0},{4,2},{6,4},{8,6},{10,8},{12,10},{14,12},{16,14},{18,16},{20... | collective-permute-start | bytes 196616 | tf_op jit(solution)/shard_map/ppermute | solution.py:10
Sparse Core Ops, SparseCore 0:
  41.7 137.8 reduce-scatter.1
  181.9 17.3 all-reduce.3
where the time goes:
time: 208 us
  waiting for transfers between devices  153 us (74%)
  matrix products  18.6 us (9%)
  between operations  14.9 us (7%)
  starting transfers between devices  13 us (6%)
  local copies, waits for them, and re-layouts  4.05 us (2%)
  other arithmetic  3.9 us (2%)
    reduce_scatter x1, waiting for transfers between devices, body(): lax.psum_scatter(both_terms, 'tm', scatter_dimension=0, tiled=True)  127 us
    psum x1, waiting for transfers between devices, body(): mine = lax.psum(partial_rows, 'dp')  18.8 us
    ppermute x4, starting transfers between devices, passed_along(): return lax.ppermute(block, axis, route)  12.9 us
    dot_general x54, matrix products, kernel_grad(): lax.dot_general(piece, flat_grad, (((0,), (0,)), ((), ())), preferred_ele...  12.4 us
    ppermute x4, waiting for transfers between devices, passed_along(): return lax.ppermute(block, axis, route)  7.73 us
    conv_general_dilated x4, matrix products, conv_valid(): lax.conv_general_dilated(field, weights, (1, 1, 1), ((0, 0), (1, 1), (1,...  6.18 us
  transfers between devices with their start and end apart: 6, of which 4 were waited for; matrix products, arithmetic and copies ran while one was open for 6% of the time, Pallas kernels for 0%

commit v1 on v0

v1 whole, which is shorter than its diff:
```python
import jax
import jax.numpy as jnp
from jax import lax
from jax.experimental import pallas as pl
from jax.experimental.pallas import tpu as pltpu
from jax.sharding import PartitionSpec as P

BF16 = jnp.bfloat16
F32 = jnp.float32
TAPS = 3


def silu_grad(value):
    sig = jax.nn.sigmoid(value)
    return sig * (1.0 + value * (1.0 - sig))


def fill(patches, first, field, width, mirrored):
    frames, cells, chans = field.shape
    rows = frames * cells
    flat = field.astype(F32).reshape(rows, chans)
    column = lax.broadcasted_iota(jnp.int32, (rows, chans), 0) % width
    before = jnp.where(column == 0, 0.0, pltpu.roll(flat, 1, 0))
    after = jnp.where(column == width - 1, 0.0, pltpu.roll(flat, rows - 1, 0))
    blocks = (after, flat, before) if mirrored else (before, flat, after)
    for k, block in enumerate(blocks):
        patches[pl.ds(first, frames), width : width + cells, k * chans : (k + 1) * chans] = (
            block.astype(BF16).reshape(frames, cells, chans)
        )
    edge = jnp.zeros((frames, width, TAPS * chans), BF16)
    patches[pl.ds(first, frames), :width, :] = edge
    patches[pl.ds(first, frames), width + cells :, :] = edge


def conv_forward(patches, kernel, frames, cells, width):
    chans = kernel.shape[1]
    left = jnp.concatenate(
        [
            patches[kt : kt + frames, ki * width : ki * width + cells, :].reshape(frames * cells, TAPS * chans)
            for kt in range(TAPS)
            for ki in range(TAPS)
        ],
        axis=1,
    )
    return jnp.dot(left, kernel[...], preferred_element_type=F32)


def conv_backward(patches, kernel, frames, cells, width):
    chans = kernel.shape[1]
    left = jnp.concatenate(
        [
            patches[
                TAPS - 1 - kt : TAPS - 1 - kt + frames,
                (TAPS - 1 - ki) * width : (TAPS - 1 - ki) * width + cells,
                :,
            ].reshape(frames * cells, TAPS * chans)
            for kt in range(TAPS)
            for ki in range(TAPS)
        ],
        axis=1,
    )
    right = jnp.concatenate([kernel[tap * chans : (tap + 1) * chans, :] for tap in range(TAPS**3)], axis=1)
    return lax.dot_general(left, right, (((1,), (1,)), ((), ())), preferred_element_type=F32)


def first_kernel(width, movie, before, upstream, after, one, two, keep, send, mid, grad, mid_tail, grad_head, patches):
    frames, cells, chans = movie.shape
    halo = TAPS - 1
    whole = jnp.concatenate([before[...], movie[...]], axis=0)
    act_in = jax.nn.silu(whole.astype(F32)).astype(BF16)
    fill(patches, 0, act_in, width, False)
    pre = conv_forward(patches, one, frames, cells, width)
    act_mid = jax.nn.silu(pre).astype(BF16).reshape(frames, cells, chans)
    mid[...] = act_mid
    mid_tail[...] = act_mid[frames - halo :]
    up_ext = jnp.concatenate([upstream[...], after[...]], axis=0)
    fill(patches, 0, up_ext, width, True)
    mid_grad = conv_backward(patches, two, frames, cells, width)
    pre_grad = (mid_grad * silu_grad(pre)).astype(BF16).reshape(frames, cells, chans)
    grad[...] = pre_grad
    grad_head[...] = pre_grad[:halo]

    def store(for_one, for_two):
        for_one[:frames] = grad[...]
        for_one[frames:] = act_in
        for_two[:frames] = mid[...]
        for_two[frames:] = up_ext

    is_even = lax.axis_index("dp") % 2 == 0

    @pl.when(is_even)
    def _():
        store(keep, send)

    @pl.when(jnp.logical_not(is_even))
    def _():
        store(send, keep)


def kernel_sums(width, own, other, acc, patches, turned):
    chans = own.shape[2]
    cells = own.shape[1]
    halo = TAPS - 1
    frames = (own.shape[0] - halo) // 2
    ext = frames + halo
    odd = lax.axis_index("dp") % 2
    for clip, source in enumerate((own, other)):
        fill(patches, clip * ext, source[pl.ds(odd * frames, ext)], width, True)
        for n in range(ext):
            block = source[(1 - odd) * frames + n]
            place = (clip * ext + n) * cells
            turned[:, place : place + cells] = block.astype(F32).T.astype(BF16)
    for kt in range(TAPS):
        l_start = (1 - odd) * kt
        r_start = odd * (halo - kt)
        left = jnp.concatenate(
            [
                turned[:, pl.ds(pl.multiple_of((clip * ext + l_start) * cells, cells), frames * cells)]
                for clip in range(2)
            ],
            axis=1,
        )
        for ki in range(TAPS):
            low = (halo - ki) * width
            right = jnp.concatenate(
                [
                    patches[pl.ds(clip * ext + r_start, frames), low : low + cells, :].reshape(
                        frames * cells, TAPS * chans
                    )
                    for clip in range(2)
                ],
                axis=0,
            )
            sums = jnp.dot(left, right, preferred_element_type=F32)
            for kj in range(TAPS):
                row = ((kt * TAPS + ki) * TAPS + kj) * chans
                acc[row : row + chans, :] = sums[:, kj * chans : (kj + 1) * chans]


def plain_sums_kernel(width, own, other, acc, patches, turned):
    kernel_sums(width, own, other, acc, patches, turned)


def relative_sums_kernel(width, distance, own, other, keep, send, acc, patches, turned):
    kernel_sums(width, own, other, acc, patches, turned)
    half, rows, _ = keep.shape
    odd = lax.axis_index("dp") % 2
    me = lax.axis_index("tm")
    for r in range(2 * half):
        far = jnp.where(odd == 1, distance[1][r], distance[0][r])
        block = jnp.bitwise_xor(me, far)
        part = acc[pl.ds(pl.multiple_of(block * rows, 8), rows), :]
        if r < half:
            keep[r] = part
        else:
            send[r - half] = part.astype(BF16)


def last_kernel(width, movie, upstream, mid_before, mid, grad, grad_after, one, two, output, movie_grad, patches):
    frames, cells, chans = movie.shape
    fill(patches, 0, jnp.concatenate([mid_before[...], mid[...]], axis=0), width, False)
    out = conv_forward(patches, two, frames, cells, width).reshape(frames, cells, chans)
    movie_f = movie[...].astype(F32)
    output[...] = (movie_f + out).astype(BF16)
    fill(patches, 0, jnp.concatenate([grad[...], grad_after[...]], axis=0), width, True)
    in_grad = conv_backward(patches, one, frames, cells, width).reshape(frames, cells, chans)
    movie_grad[...] = (upstream[...].astype(F32) + in_grad * silu_grad(movie_f)).astype(BF16)


def call(body, outs, scratch, flops, *args):
    vmem = pl.BlockSpec(memory_space=pltpu.VMEM)
    size = sum(a.size * a.dtype.itemsize for a in args) + sum(o.size * o.dtype.itemsize for o in outs)
    return pl.pallas_call(
        body,
        out_shape=outs,
        in_specs=[vmem] * len(args),
        out_specs=[vmem] * len(outs),
        scratch_shapes=scratch,
        compiler_params=pltpu.CompilerParams(vmem_limit_bytes=24 * 2**20),
        cost_estimate=pl.CostEstimate(flops=flops, bytes_accessed=size, transcendentals=0),
    )(*args)


def passed_along(block, axis, distance):
    devices = range(lax.axis_size(axis))
    route = [(i - distance, i) for i in devices if i - distance in devices]
    return lax.ppermute(block, axis, route)


def swapped(block):
    return lax.ppermute(block, "dp", [(i, i ^ 1) for i in range(lax.axis_size("dp"))])


def halving_sum(keep, send, orders):
    tm, dp = lax.axis_size("tm"), lax.axis_size("dp")
    for stage in range(len(orders[0])):
        route = [
            (t * dp + d, (t ^ (1 << orders[d % 2][stage])) * dp + d) for t in range(tm) for d in range(dp)
        ]
        got = lax.ppermute(send, ("tm", "dp"), route)
        half = keep.shape[0] // 2
        if half:
            send = (keep[half:] + got[half:].astype(F32)).astype(BF16)
            keep = keep[:half] + got[:half].astype(F32)
        else:
            keep = keep + got.astype(F32)
    return keep[0]


def body(movie, kernel_one, kernel_two, upstream):
    clips, frames, height, width, chans = movie.shape
    assert clips == 1
    tm, dp = lax.axis_size("tm"), lax.axis_size("dp")
    assert dp % 2 == 0
    cells = height * width
    halo = TAPS - 1
    ext = frames + halo
    krows = kernel_one.shape[0]
    rows = krows // tm
    shape = jax.ShapeDtypeStruct
    flat = (frames, cells, chans)
    movie_r = movie.reshape(flat)
    upstream_r = upstream.reshape(flat)
    conv_flops = 2 * frames * cells * krows * chans
    patch = pltpu.VMEM((ext, cells + 2 * width, TAPS * chans), BF16)

    before = passed_along(movie_r[frames - halo :], "tm", 1)
    after = passed_along(upstream_r[:halo], "tm", -1)
    bundle = shape((frames + ext, cells, chans), BF16)
    field = shape(flat, BF16)
    edge = shape((halo, cells, chans), BF16)
    keep, send, mid, grad, mid_tail, grad_head = call(
        lambda *refs: first_kernel(width, *refs),
        [bundle, bundle, field, field, edge, edge],
        [patch],
        2 * conv_flops,
        movie_r, before, upstream_r, after, kernel_one, kernel_two,
    )
    other = swapped(send)

    scratch = [
        pltpu.VMEM((2 * ext, cells + 2 * width, TAPS * chans), BF16),
        pltpu.VMEM((chans, 2 * ext * cells), BF16),
    ]
    if dp == 2 and tm > 1 and tm & (tm - 1) == 0 and rows % 8 == 0:
        bits = tm.bit_length() - 1
        orders = (list(range(bits)), [1, 0][:bits] + list(range(2, bits)))
        distance = [
            [sum(1 << order[s] for s in range(bits) if r >> (bits - 1 - s) & 1) for r in range(tm)]
            for order in orders
        ]
        kept, sent = call(
            lambda *refs: relative_sums_kernel(width, distance, *refs),
            [shape((tm // 2, rows, chans), F32), shape((tm // 2, rows, chans), BF16)],
            [pltpu.VMEM((krows, chans), F32)] + scratch,
            2 * conv_flops,
            keep, other,
        )
        mine = halving_sum(kept, sent, orders)
    else:
        (sums,) = call(
            lambda *refs: plain_sums_kernel(width, *refs),
            [shape((krows, chans), F32)],
            scratch,
            2 * conv_flops,
            keep, other,
        )
        mine = lax.psum_scatter(sums, "tm", scatter_dimension=0, tiled=True)
        if dp > 2:
            groups = [[d for d in range(dp) if d % 2 == parity] for parity in range(2)]
            mine = lax.psum(mine, "dp", axis_index_groups=groups)

    mid_before = passed_along(mid_tail, "tm", 1)
    grad_after = passed_along(grad_head, "tm", -1)
    output, movie_grad = call(
        lambda *refs: last_kernel(width, *refs),
        [field, field],
        [patch],
        2 * conv_flops,
        movie_r, upstream_r, mid_before, mid, grad, grad_after, kernel_one, kernel_two,
    )
    theirs = swapped(mine)
    is_even = lax.axis_index("dp") % 2 == 0
    grad_one = jnp.where(is_even, mine, theirs)
    grad_two = jnp.where(is_even, theirs, mine)
    return (output.reshape(movie.shape), movie_grad.reshape(movie.shape), grad_one, grad_two)


def solution(mesh):
    in_specs = (P("dp", "tm", None, None, None), P(), P(), P("dp", "tm", None, None, None))
    out_specs = (
        P("dp", "tm", None, None, None),
        P("dp", "tm", None, None, None),
        P("tm", None),
        P("tm", None),
    )
    return jax.shard_map(body, mesh=mesh, in_specs=in_specs, out_specs=out_specs, check_vma=False)
```

time: 208 us -> 58.6 us (0.28)
  waiting for transfers between devices: 153 us -> 24.6 us
  matrix products: 18.6 us -> 0 us
  between operations: 14.9 us -> 0.77 us
  starting transfers between devices: 13 us -> 20.7 us
  Pallas kernels: 0 us -> 7.24 us
  other arithmetic: 3.9 us -> 0.86 us
    reduce_scatter x1 -> x0, waiting for transfers between devices: 127 us -> none  [body(): lax.psum_scatter(both_terms, 'tm', scatter_dimension=0, tiled=True)]
    psum x1 -> x0, waiting for transfers between devices: 18.8 us -> none  [body(): mine = lax.psum(partial_rows, 'dp')]
    ppermute x0 -> x6, waiting for transfers between devices: none -> 15 us  [the longest x4 13.4 us: halving_sum(): got = lax.ppermute(send, ('tm', 'dp'), route)]
    dot_general x54 -> x0, matrix products: 12.4 us -> none  [kernel_grad(): lax.dot_general(piece, flat_grad, (((0,), (0,)), ((), ())), preferred_ele...]
    ppermute x0 -> x6, starting transfers between devices: none -> 9.37 us  [the longest x4 9.23 us: halving_sum(): got = lax.ppermute(send, ('tm', 'dp'), route)]
    pallas_call x0 -> x3, Pallas kernels: none -> 7.24 us  [call(): pl.pallas_call(body, out_shape=outs, in_specs=[vmem] * len(args), out_spe...]
    conv_general_dilated x4 -> x0, matrix products: 6.18 us -> none  [conv_valid(): lax.conv_general_dilated(field, weights, (1, 1, 1), ((0, 0), (1, 1), (1,...]
  transfers between devices with their start and end apart: 6 -> 10, of which waited for: 4 -> 7; matrix products, arithmetic and copies ran while one was open for 6% -> 1% of each run, Pallas kernels for 0% -> 5%
where the time goes in v1:
time: 58.6 us; the launch traced here: 58.2 us
  waiting for transfers between devices  24.6 us (42%)
  starting transfers between devices  20.7 us (35%)
  Pallas kernels  7.24 us (12%)
  local copies, waits for them, and re-layouts  4.1 us (7%)
  other arithmetic  0.86 us (1%)
  between operations  0.77 us (1%)
    ppermute x4, waiting for transfers between devices, halving_sum(): got = lax.ppermute(send, ('tm', 'dp'), route)  13.4 us
    ppermute x4, starting transfers between devices, passed_along(): return lax.ppermute(block, axis, route)  11.3 us
    ppermute x4, waiting for transfers between devices, passed_along(): return lax.ppermute(block, axis, route)  9.58 us
    ppermute x4, starting transfers between devices, halving_sum(): got = lax.ppermute(send, ('tm', 'dp'), route)  9.23 us
    pallas_call x3, Pallas kernels, call(): pl.pallas_call(body, out_shape=outs, in_specs=[vmem] * len(args), out_spe...  7.24 us
    unnamed x12, local copies, waits for them, and re-layouts  2.36 us
    ppermute x2, waiting for transfers between devices, swapped(): lax.ppermute(block, 'dp', [(i, i ^ 1) for i in range(lax.axis_size('dp'))])  1.62 us
  transfers between devices with their start and end apart: 10, of which 7 were waited for; matrix products, arithmetic and copies ran while one was open for 1% of the time, Pallas kernels for 5%

profile of v1, /device:TPU:0, one launch (start us, length us, event | category | flops | bytes accessed | tf_op | source)
XLA Modules:
  0.0 58.2 jit_solution(9817068801982073463)
XLA Ops:
  0.6 0.0 copy-start
  0.6 0.0 copy-start.1
  0.7 0.9 %slice.48 = bf16[1,2,8,16,128]{4,3,2,1,0:T(8,128)(2,1)S(1)} slice(bf16[1,4,8,16,128]{4,3,2,1,0:T(8,128)(2,1)} %param.4), slice={[0:1], [2:4], [0:8], [0:16], [0:128]} | slice | bytes 131072 | tf_op jit(solution)/shard_map/slice | solution.py:227
  1.5 4.8 %collective-permute-start = (bf16[2,128,128]{2,1,0:T(8,128)(2,1)S(1)}, bf16[2,128,128]{2,1,0:T(8,128)(2,1)S(1)}, u32[]{:S(2)}, u32[]{:S(2)}) collective-permute-start(bf16[2,128,128]{2,1,0:T(8,128)(2,1)S(1)} %bitcast.12), channel_id=1, source_target_pairs={{0,2},{2,4},{4,6},{6,8},{8,10},{10,12},{12,14},{14,16},{16,18},{18... | collective-permute-start | bytes 196616 | tf_op jit(solution)/shard_map/ppermute | solution.py:187
  6.4 0.8 %slice.50 = bf16[1,2,8,16,128]{4,3,2,1,0:T(8,128)(2,1)S(1)} slice(bf16[1,4,8,16,128]{4,3,2,1,0:T(8,128)(2,1)} %param.7), slice={[0:1], [0:2], [0:8], [0:16], [0:128]} | slice | bytes 131072 | tf_op jit(solution)/shard_map/slice | solution.py:228
  7.2 1.3 %collective-permute-start.1 = (bf16[2,128,128]{2,1,0:T(8,128)(2,1)S(1)}, bf16[2,128,128]{2,1,0:T(8,128)(2,1)S(1)}, u32[]{:S(2)}, u32[]{:S(2)}) collective-permute-start(bf16[2,128,128]{2,1,0:T(8,128)(2,1)S(1)} %bitcast.13), channel_id=1, source_target_pairs={{2,0},{4,2},{6,4},{8,6},{10,8},{12,10},{14,12},{16,14},{18,16},{20... | collective-permute-start | bytes 196616 | tf_op jit(solution)/shard_map/ppermute | solution.py:187
  8.5 0.0 collective-permute-done.refs_1_
  8.5 4.8 %collective-permute-done.1.refs_3_ = bf16[2,128,128]{2,1,0:T(8,128)(2,1)S(1)} collective-permute-done((bf16[2,128,128]{2,1,0:T(8,128)(2,1)S(1)}, bf16[2,128,128]{2,1,0:T(8,128)(2,1)S(1)}, u32[]{:S(2)}, u32[]{:S(2)}) %collective-permute-start.1) | collective-permute-done | bytes 65568 | tf_op jit(solution)/shard_map/ppermute | solution.py:187
  13.4 1.2 %copy-done.2 = bf16[3456,128]{1,0:T(8,128)(2,1)S(1)} copy-done((bf16[3456,128]{1,0:T(8,128)(2,1)S(1)}, bf16[3456,128]{1,0:T(8,128)(2,1)}, u32[]{:S(2)}) %copy-start.2) | copy-done | bytes 884760
  14.6 1.2 %copy-done.4 = bf16[3456,128]{1,0:T(8,128)(2,1)S(1)} copy-done((bf16[3456,128]{1,0:T(8,128)(2,1)S(1)}, bf16[3456,128]{1,0:T(8,128)(2,1)}, u32[]{:S(2)}) %copy-start.4) | copy-done | bytes 884760
  15.7 2.3 %shard_map.75 = (bf16[10,128,128]{2,1,0:T(8,128)(2,1)S(1)}, bf16[10,128,128]{2,1,0:T(8,128)(2,1)S(1)}, bf16[4,128,128]{2,1,0:T(8,128)(2,1)S(1)}, bf16[4,128,128]...) custom-call(bf16[4,128,128]{2,1,0:T(8,128)(2,1)S(1)} %bitcast.8, ...), custom_call_target="tpu_custom_call" | custom-call | flops 905969664 | bytes 3211264 | tf_op jit(solution)/shard_map/pallas_call | solution.py:173
  18.0 0.1 collective-permute-start.4
  18.1 1.6 %collective-permute-done.4.refs_1_ = bf16[10,128,128]{2,1,0:T(8,128)(2,1)S(1)} collective-permute-done((bf16[10,128,128]{2,1,0:T(8,128)(2,1)S(1)}, bf16[10,128,128]{2,1,0:T(8,128)(2,1)S(1)}, u32[]{:S(2)}, u32[]{:S(2)}) %collective-permute-start.4) | collective-permute-done | bytes 327712 | tf_op jit(solution)/shard_map/ppermute | solution.py:191
  19.7 2.1 %shard_map.77 = (f32[8,216,128]{2,1,0:T(8,128)S(1)}, bf16[8,216,128]{2,1,0:T(8,128)(2,1)S(1)}) custom-call(bf16[10,128,128]{2,1,0:T(8,128)(2,1)S(1)} %get-tuple-element.20.refs_0_, bf16[10,128,128]{2,1,0:T(8,128)(2,1)S(1)} %collective-permute-done.4.refs_1_), custom_call_target="tpu_custom_call" | custom-call | flops 905969664 | bytes 1982464 | tf_op jit(solution)/shard_map/pallas_call | solution.py:173
  21.8 2.5 %collective-permute-start.5 = (bf16[8,216,128]{2,1,0:T(8,128)(2,1)S(1)}, bf16[8,216,128]{2,1,0:T(8,128)(2,1)S(1)}, u32[]{:S(2)}, u32[]{:S(2)}) collective-permute-start(bf16[8,216,128]{2,1,0:T(8,128)(2,1)S(1)} %get-tuple-element.23), channel_id=1, source_target_pairs={{0,2},{1,5},{2,0},{3,7},{4,6},{5,1},{6,4},{7,3},{8,10},{9,13},{10,... | collective-permute-start | bytes 1327112 | tf_op jit(solution)/shard_map/ppermute | solution.py:200
  24.3 6.3 %collective-permute-done.5 = bf16[8,216,128]{2,1,0:T(8,128)(2,1)S(1)} collective-permute-done((bf16[8,216,128]{2,1,0:T(8,128)(2,1)S(1)}, bf16[8,216,128]{2,1,0:T(8,128)(2,1)S(1)}, u32[]{:S(2)}, u32[]{:S(2)}) %collective-permute-start.5) | collective-permute-done | bytes 442400 | tf_op jit(solution)/shard_map/ppermute | solution.py:200
  30.6 0.1 add_convert_fusion
  30.6 0.0 copy-start.3
  30.7 2.5 %collective-permute-start.6 = (bf16[4,216,128]{2,1,0:T(8,128)(2,1)S(1)}, bf16[4,216,128]{2,1,0:T(8,128)(2,1)S(1)}, u32[]{:S(2)}, u32[]{:S(2)}) collective-permute-start(bf16[4,216,128]{2,1,0:T(8,128)(2,1)S(1)} %get-tuple-element.24), channel_id=1, source_target_pairs={{0,4},{1,3},{2,6},{3,1},{4,0},{5,7},{6,2},{7,5},{8,12},{9,11},{10,... | collective-permute-start | bytes 663560 | tf_op jit(solution)/shard_map/ppermute | solution.py:200
  33.1 3.9 %collective-permute-done.6 = bf16[4,216,128]{2,1,0:T(8,128)(2,1)S(1)} collective-permute-done((bf16[4,216,128]{2,1,0:T(8,128)(2,1)S(1)}, bf16[4,216,128]{2,1,0:T(8,128)(2,1)S(1)}, u32[]{:S(2)}, u32[]{:S(2)}) %collective-permute-start.6) | collective-permute-done | bytes 221216 | tf_op jit(solution)/shard_map/ppermute | solution.py:200
  37.1 1.6 %collective-permute-start.7 = (bf16[2,216,128]{2,1,0:T(8,128)(2,1)S(1)}, bf16[2,216,128]{2,1,0:T(8,128)(2,1)S(1)}, u32[]{:S(2)}, u32[]{:S(2)}) collective-permute-start(bf16[2,216,128]{2,1,0:T(8,128)(2,1)S(1)} %get-tuple-element.26), channel_id=1, source_target_pairs={{0,8},{1,9},{2,10},{3,11},{4,12},{5,13},{6,14},{7,15},{8,0},{9,1},... | collective-permute-start | bytes 331784 | tf_op jit(solution)/shard_map/ppermute | solution.py:200
  38.7 3.2 %collective-permute-done.7 = bf16[2,216,128]{2,1,0:T(8,128)(2,1)S(1)} collective-permute-done((bf16[2,216,128]{2,1,0:T(8,128)(2,1)S(1)}, bf16[2,216,128]{2,1,0:T(8,128)(2,1)S(1)}, u32[]{:S(2)}, u32[]{:S(2)}) %collective-permute-start.7) | collective-permute-done | bytes 110624 | tf_op jit(solution)/shard_map/ppermute | solution.py:200
  41.9 2.7 %collective-permute-start.8 = (bf16[1,216,128]{2,1,0:T(8,128)(2,1)S(1)}, bf16[1,216,128]{2,1,0:T(8,128)(2,1)S(1)}, u32[]{:S(2)}, u32[]{:S(2)}) collective-permute-start(bf16[1,216,128]{2,1,0:T(8,128)(2,1)S(1)} %fusion.1), channel_id=1, source_target_pairs={{0,16},{1,17},{2,18},{3,19},{4,20},{5,21},{6,22},{7,23},{8,24},{9,... | collective-permute-start | bytes 165896 | tf_op jit(solution)/shard_map/ppermute | solution.py:200
  44.6 3.9 %collective-permute-start.2 = (bf16[2,128,128]{2,1,0:T(8,128)(2,1)S(1)}, bf16[2,128,128]{2,1,0:T(8,128)(2,1)S(1)}, u32[]{:S(2)}, u32[]{:S(2)}) collective-permute-start(bf16[2,128,128]{2,1,0:T(8,128)(2,1)S(1)} %get-tuple-element.14), channel_id=1, source_target_pairs={{0,2},{2,4},{4,6},{6,8},{8,10},{10,12},{12,14},{14,16},{16,18},{18... | collective-permute-start | bytes 196616 | tf_op jit(solution)/shard_map/ppermute | solution.py:187
  48.5 1.3 %collective-permute-start.3 = (bf16[2,128,128]{2,1,0:T(8,128)(2,1)S(1)}, bf16[2,128,128]{2,1,0:T(8,128)(2,1)S(1)}, u32[]{:S(2)}, u32[]{:S(2)}) collective-permute-start(bf16[2,128,128]{2,1,0:T(8,128)(2,1)S(1)} %get-tuple-element.17), channel_id=1, source_target_pairs={{2,0},{4,2},{6,4},{8,6},{10,8},{12,10},{14,12},{16,14},{18,16},{20... | collective-permute-start | bytes 196616 | tf_op jit(solution)/shard_map/ppermute | solution.py:187
  49.8 0.0 collective-permute-done.8
  49.8 0.1 collective-permute-start.9
  49.9 1.1 %collective-permute-done.2.refs_2_ = bf16[2,128,128]{2,1,0:T(8,128)(2,1)S(1)} collective-permute-done((bf16[2,128,128]{2,1,0:T(8,128)(2,1)S(1)}, bf16[2,128,128]{2,1,0:T(8,128)(2,1)S(1)}, u32[]{:S(2)}, u32[]{:S(2)}) %collective-permute-start.2) | collective-permute-done | bytes 65568 | tf_op jit(solution)/shard_map/ppermute | solution.py:187
  51.0 3.7 %collective-permute-done.3.refs_5_ = bf16[2,128,128]{2,1,0:T(8,128)(2,1)S(1)} collective-permute-done((bf16[2,128,128]{2,1,0:T(8,128)(2,1)S(1)}, bf16[2,128,128]{2,1,0:T(8,128)(2,1)S(1)}, u32[]{:S(2)}, u32[]{:S(2)}) %collective-permute-start.3) | collective-permute-done | bytes 65568 | tf_op jit(solution)/shard_map/ppermute | solution.py:187
  54.7 2.9 %shard_map.76 = (bf16[4,128,128]{2,1,0:T(8,128)(2,1)}, bf16[4,128,128]{2,1,0:T(8,128)(2,1)}) custom-call(bf16[4,128,128]{2,1,0:T(8,128)(2,1)S(1)} %bitcast.9, bf16[4,128,128]{2,1,0:T(8,128)(2,1)S(1)} %bitcast.11, bf16[2,128,128]{2,1,0:T(8,128)(2,1)S(1)} %collective-permute-done.2.refs_2_, bf16[4,128,128]{2,1,0:T(8,128)(2,1)S(1)} %get-tuple-element.15.refs_3_, ...), custom_call_target="tpu_custom_call" | custom-call | flops 905969664 | bytes 2686976 | tf_op jit(solution)/shard_map/pallas_call | solution.py:173
  57.5 0.0 collective-permute-done.9
  57.5 0.7 %broadcast_select_fusion = (f32[216,128]{1,0:T(8,128)}, f32[216,128]{1,0:T(8,128)}) fusion(f32[216,128]{1,0:T(8,128)S(1)} %collective-permute-done.9, f32[216,128]{1,0:T(8,128)S(1)} %fusion.3, pred[]{:T(512)S(6)} %eq.5), kind=kLoop, calls=%fused_computation.10 | loop fusion | flops 55296 | bytes 442369 | tf_op jit(solution)/shard_map/jit(_where)/select_n | solution.py:285
  (10 shorter events, 0.1 us)
Async XLA Ops:
  0.6 12.8 %copy-start = (bf16[1,4,8,16,128]{4,3,2,1,0:T(8,128)(2,1)S(1)}, bf16[1,4,8,16,128]{4,3,2,1,0:T(8,128)(2,1)}, u32[]{:S(2)}) copy-start(bf16[1,4,8,16,128]{4,3,2,1,0:T(8,128)(2,1)} %param.4) | copy-start | bytes 393220
  0.6 12.8 %copy-start.1 = (bf16[1,4,8,16,128]{4,3,2,1,0:T(8,128)(2,1)S(1)}, bf16[1,4,8,16,128]{4,3,2,1,0:T(8,128)(2,1)}, u32[]{:S(2)}) copy-start(bf16[1,4,8,16,128]{4,3,2,1,0:T(8,128)(2,1)} %param.7) | copy-start | bytes 393220
  1.5 7.0 %collective-permute-start = (bf16[2,128,128]{2,1,0:T(8,128)(2,1)S(1)}, bf16[2,128,128]{2,1,0:T(8,128)(2,1)S(1)}, u32[]{:S(2)}, u32[]{:S(2)}) collective-permute-start(bf16[2,128,128]{2,1,0:T(8,128)(2,1)S(1)} %bitcast.12), channel_id=1, source_target_pairs={{0,2},{2,4},{4,6},{6,8},{8,10},{10,12},{12,14},{14,16},{16,18},{18... | collective-permute-start | bytes 196616 | tf_op jit(solution)/shard_map/ppermute | solution.py:187
  7.2 6.1 %collective-permute-start.1 = (bf16[2,128,128]{2,1,0:T(8,128)(2,1)S(1)}, bf16[2,128,128]{2,1,0:T(8,128)(2,1)S(1)}, u32[]{:S(2)}, u32[]{:S(2)}) collective-permute-start(bf16[2,128,128]{2,1,0:T(8,128)(2,1)S(1)} %bitcast.13), channel_id=1, source_target_pairs={{2,0},{4,2},{6,4},{8,6},{10,8},{12,10},{14,12},{16,14},{18,16},{20... | collective-permute-start | bytes 196616 | tf_op jit(solution)/shard_map/ppermute | solution.py:187
  13.4 1.2 %copy-start.2 = (bf16[3456,128]{1,0:T(8,128)(2,1)S(1)}, bf16[3456,128]{1,0:T(8,128)(2,1)}, u32[]{:S(2)}) copy-start(bf16[3456,128]{1,0:T(8,128)(2,1)} %refs_6_.1) | copy-start | bytes 2654212
  14.6 1.2 %copy-start.4 = (bf16[3456,128]{1,0:T(8,128)(2,1)S(1)}, bf16[3456,128]{1,0:T(8,128)(2,1)}, u32[]{:S(2)}) copy-start(bf16[3456,128]{1,0:T(8,128)(2,1)} %refs_7_.1) | copy-start | bytes 2654212
  18.0 1.7 %collective-permute-start.4 = (bf16[10,128,128]{2,1,0:T(8,128)(2,1)S(1)}, bf16[10,128,128]{2,1,0:T(8,128)(2,1)S(1)}, u32[]{:S(2)}, u32[]{:S(2)}) collective-permute-start(bf16[10,128,128]{2,1,0:T(8,128)(2,1)S(1)} %get-tuple-element.21), channel_id=1, source_target_pairs={{0,1},{1,0},{2,3},{3,2},{4,5},{5,4},{6,7},{7,6},{8,9},{9,8},{10,11... | collective-permute-start | bytes 983048 | tf_op jit(solution)/shard_map/ppermute | solution.py:191
  21.8 8.7 %collective-permute-start.5 = (bf16[8,216,128]{2,1,0:T(8,128)(2,1)S(1)}, bf16[8,216,128]{2,1,0:T(8,128)(2,1)S(1)}, u32[]{:S(2)}, u32[]{:S(2)}) collective-permute-start(bf16[8,216,128]{2,1,0:T(8,128)(2,1)S(1)} %get-tuple-element.23), channel_id=1, source_target_pairs={{0,2},{1,5},{2,0},{3,7},{4,6},{5,1},{6,4},{7,3},{8,10},{9,13},{10,... | collective-permute-start | bytes 1327112 | tf_op jit(solution)/shard_map/ppermute | solution.py:200
  30.6 24.1 %copy-start.5 = (bf16[3456,128]{1,0:T(8,128)(2,1)S(1)}, bf16[3456,128]{1,0:T(8,128)(2,1)}, u32[]{:S(2)}) copy-start(bf16[3456,128]{1,0:T(8,128)(2,1)} %refs_7_.1) | copy-start | bytes 2654212
  30.6 24.0 %copy-start.3 = (bf16[3456,128]{1,0:T(8,128)(2,1)S(1)}, bf16[3456,128]{1,0:T(8,128)(2,1)}, u32[]{:S(2)}) copy-start(bf16[3456,128]{1,0:T(8,128)(2,1)} %refs_6_.1) | copy-start | bytes 2654212
  30.7 6.4 %collective-permute-start.6 = (bf16[4,216,128]{2,1,0:T(8,128)(2,1)S(1)}, bf16[4,216,128]{2,1,0:T(8,128)(2,1)S(1)}, u32[]{:S(2)}, u32[]{:S(2)}) collective-permute-start(bf16[4,216,128]{2,1,0:T(8,128)(2,1)S(1)} %get-tuple-element.24), channel_id=1, source_target_pairs={{0,4},{1,3},{2,6},{3,1},{4,0},{5,7},{6,2},{7,5},{8,12},{9,11},{10,... | collective-permute-start | bytes 663560 | tf_op jit(solution)/shard_map/ppermute | solution.py:200
  37.1 4.8 %collective-permute-start.7 = (bf16[2,216,128]{2,1,0:T(8,128)(2,1)S(1)}, bf16[2,216,128]{2,1,0:T(8,128)(2,1)S(1)}, u32[]{:S(2)}, u32[]{:S(2)}) collective-permute-start(bf16[2,216,128]{2,1,0:T(8,128)(2,1)S(1)} %get-tuple-element.26), channel_id=1, source_target_pairs={{0,8},{1,9},{2,10},{3,11},{4,12},{5,13},{6,14},{7,15},{8,0},{9,1},... | collective-permute-start | bytes 331784 | tf_op jit(solution)/shard_map/ppermute | solution.py:200
  41.9 7.9 %collective-permute-start.8 = (bf16[1,216,128]{2,1,0:T(8,128)(2,1)S(1)}, bf16[1,216,128]{2,1,0:T(8,128)(2,1)S(1)}, u32[]{:S(2)}, u32[]{:S(2)}) collective-permute-start(bf16[1,216,128]{2,1,0:T(8,128)(2,1)S(1)} %fusion.1), channel_id=1, source_target_pairs={{0,16},{1,17},{2,18},{3,19},{4,20},{5,21},{6,22},{7,23},{8,24},{9,... | collective-permute-start | bytes 165896 | tf_op jit(solution)/shard_map/ppermute | solution.py:200
  44.6 6.4 %collective-permute-start.2 = (bf16[2,128,128]{2,1,0:T(8,128)(2,1)S(1)}, bf16[2,128,128]{2,1,0:T(8,128)(2,1)S(1)}, u32[]{:S(2)}, u32[]{:S(2)}) collective-permute-start(bf16[2,128,128]{2,1,0:T(8,128)(2,1)S(1)} %get-tuple-element.14), channel_id=1, source_target_pairs={{0,2},{2,4},{4,6},{6,8},{8,10},{10,12},{12,14},{14,16},{16,18},{18... | collective-permute-start | bytes 196616 | tf_op jit(solution)/shard_map/ppermute | solution.py:187
  48.5 6.2 %collective-permute-start.3 = (bf16[2,128,128]{2,1,0:T(8,128)(2,1)S(1)}, bf16[2,128,128]{2,1,0:T(8,128)(2,1)S(1)}, u32[]{:S(2)}, u32[]{:S(2)}) collective-permute-start(bf16[2,128,128]{2,1,0:T(8,128)(2,1)S(1)} %get-tuple-element.17), channel_id=1, source_target_pairs={{2,0},{4,2},{6,4},{8,6},{10,8},{12,10},{14,12},{16,14},{18,16},{20... | collective-permute-start | bytes 196616 | tf_op jit(solution)/shard_map/ppermute | solution.py:187
  49.8 7.7 %collective-permute-start.9 = (f32[216,128]{1,0:T(8,128)S(1)}, f32[216,128]{1,0:T(8,128)S(1)}, u32[]{:S(2)}, u32[]{:S(2)}) collective-permute-start(f32[216,128]{1,0:T(8,128)S(1)} %fusion.3), channel_id=1, source_target_pairs={{0,1},{1,0},{2,3},{3,2},{4,5},{5,4},{6,7},{7,6},{8,9},{9,8},{10,11... | collective-permute-start | bytes 331784 | tf_op jit(solution)/shard_map/ppermute | solution.py:191

commit v2 on v1

--- a/solution.py
+++ b/solution.py
@@ -63,28 +63,119 @@
     return lax.dot_general(left, right, (((1,), (1,)), ((), ())), preferred_element_type=F32)
 
 
-def first_kernel(width, movie, before, upstream, after, one, two, keep, send, mid, grad, mid_tail, grad_head, patches):
+def taps_forward(patches, kernel, kt, first, count, cells, width):
+    chans = kernel.shape[1]
+    left = jnp.concatenate(
+        [
+            patches[first : first + count, ki * width : ki * width + cells, :].reshape(count * cells, TAPS * chans)
+            for ki in range(TAPS)
+        ],
+        axis=1,
+    )
+    rows = TAPS * TAPS * chans
+    return jnp.dot(left, kernel[kt * rows : (kt + 1) * rows, :], preferred_element_type=F32)
+
+
+def taps_backward(patches, kernel, kt, first, count, cells, width):
+    chans = kernel.shape[1]
+    left = jnp.concatenate(
+        [
+            patches[
+                first : first + count, (TAPS - 1 - ki) * width : (TAPS - 1 - ki) * width + cells, :
+            ].reshape(count * cells, TAPS * chans)
+            for ki in range(TAPS)
+        ],
+        axis=1,
+    )
+    taps = range(kt * TAPS * TAPS, (kt + 1) * TAPS * TAPS)
+    right = jnp.concatenate([kernel[tap * chans : (tap + 1) * chans, :] for tap in taps], axis=1)
+    return lax.dot_general(left, right, (((1,), (1,)), ((), ())), preferred_element_type=F32)
+
+
+def edges_kernel(movie, upstream, near, far, sems):
+    frames = movie.shape[0]
+    halo = near.shape[0]
+    even = lax.axis_index("tm") % 2 == 0
+
+    def run(forward, backward):
+        copies = [
+            pltpu.make_async_copy(movie.at[pl.ds(frames - halo, halo)], forward, sems.at[0]),
+            pltpu.make_async_copy(upstream.at[pl.ds(0, halo)], backward, sems.at[1]),
+        ]
+        for copy in copies:
+            copy.start()
+        for copy in copies:
+            copy.wait()
+
+    @pl.when(even)
+    def _():
+        run(near, far)
+
+    @pl.when(jnp.logical_not(even))
+    def _():
+        run(far, near)
+
+
+def sorted_edges(near, far):
+    even = lax.axis_index("tm") % 2 == 0
+    return jnp.where(even, far[...], near[...]), jnp.where(even, near[...], far[...])
+
+
+def inner_kernel(
+    width, movie, upstream, one, two, act_in, pre_part, grad_part, act_patches, up_patches
+):
     frames, cells, chans = movie.shape
+    act_in[...] = jax.nn.silu(movie[...].astype(F32)).astype(BF16)
+    fill(act_patches, 0, act_in[...], width, False)
+    fill(up_patches, 0, upstream[...], width, True)
+    pre_part[...] = taps_forward(act_patches, one, TAPS - 1, 0, frames, cells, width)
+    for lag in range(1, TAPS):
+        part = taps_forward(act_patches, one, TAPS - 1 - lag, 0, frames - lag, cells, width)
+        pre_part[lag * cells :, :] += part
+    grad_part[...] = taps_backward(up_patches, two, TAPS - 1, 0, frames, cells, width)
+    for lag in range(1, TAPS):
+        part = taps_backward(up_patches, two, TAPS - 1 - lag, lag, frames - lag, cells, width)
+        grad_part[: (frames - lag) * cells, :] += part
+
+
+def outer_kernel(
+    width, near, far, act_in, upstream, pre_part, grad_part, one, two, keep, send, mid, grad, near_out, far_out, patches
+):
+    frames, cells, chans = act_in.shape
     halo = TAPS - 1
-    whole = jnp.concatenate([before[...], movie[...]], axis=0)
-    act_in = jax.nn.silu(whole.astype(F32)).astype(BF16)
-    fill(patches, 0, act_in, width, False)
-    pre = conv_forward(patches, one, frames, cells, width)
+    before, after = sorted_edges(near, far)
+    act_before = jax.nn.silu(before.astype(F32)).astype(BF16)
+    fill(patches, 0, act_before, width, False)
+    pres = [pre_part[t * cells : (t + 1) * cells, :] for t in range(frames)]
+    for kt in range(halo):
+        part = taps_forward(patches, one, kt, kt, halo - kt, cells, width)
+        for t in range(halo - kt):
+            pres[t] = pres[t] + part[t * cells : (t + 1) * cells]
+    pre = jnp.concatenate(pres, axis=0)
     act_mid = jax.nn.silu(pre).astype(BF16).reshape(frames, cells, chans)
     mid[...] = act_mid
-    mid_tail[...] = act_mid[frames - halo :]
-    up_ext = jnp.concatenate([upstream[...], after[...]], axis=0)
-    fill(patches, 0, up_ext, width, True)
-    mid_grad = conv_backward(patches, two, frames, cells, width)
+    fill(patches, 0, after, width, True)
+    grads = [grad_part[t * cells : (t + 1) * cells, :] for t in range(frames)]
+    for kt in range(halo):
+        part = taps_backward(patches, two, kt, 0, halo - kt, cells, width)
+        for n in range(halo - kt):
+            t = frames - (halo - kt) + n
+            grads[t] = grads[t] + part[n * cells : (n + 1) * cells]
+    mid_grad = jnp.concatenate(grads, axis=0)
     pre_grad = (mid_grad * silu_grad(pre)).astype(BF16).reshape(frames, cells, chans)
     grad[...] = pre_grad
-    grad_head[...] = pre_grad[:halo]
+    even = lax.axis_index("tm") % 2 == 0
+    mid_tail, grad_head = act_mid[frames - halo :], pre_grad[:halo]
+    near_out[...] = jnp.where(even, mid_tail, grad_head)
+    far_out[...] = jnp.where(even, grad_head, mid_tail)
 
     def store(for_one, for_two):
         for_one[:frames] = grad[...]
-        for_one[frames:] = act_in
+        for_one[frames : frames + halo] = act_before
+        for_one[frames + halo :] = act_in[...]
         for_two[:frames] = mid[...]
-        for_two[frames:] = up_ext
+        for_two[frames : 2 * frames] = upstream[...]
+        for_two[2 * frames :] = after
 
     is_even = lax.axis_index("dp") % 2 == 0
 
@@ -156,55 +247,57 @@
             send[r - half] = part.astype(BF16)
 
 
-def last_kernel(width, movie, upstream, mid_before, mid, grad, grad_after, one, two, output, movie_grad, patches):
+def last_kernel(width, movie, upstream, near, far, mid, grad, one, two, output, movie_grad, patches):
     frames, cells, chans = movie.shape
-    fill(patches, 0, jnp.concatenate([mid_before[...], mid[...]], axis=0), width, False)
+    mid_before, grad_after = sorted_edges(near, far)
+    fill(patches, 0, jnp.concatenate([mid_before, mid[...]], axis=0), width, False)
     out = conv_forward(patches, two, frames, cells, width).reshape(frames, cells, chans)
     movie_f = movie[...].astype(F32)
     output[...] = (movie_f + out).astype(BF16)
-    fill(patches, 0, jnp.concatenate([grad[...], grad_after[...]], axis=0), width, True)
+    fill(patches, 0, jnp.concatenate([grad[...], grad_after], axis=0), width, True)
     in_grad = conv_backward(patches, one, frames, cells, width).reshape(frames, cells, chans)
     movie_grad[...] = (upstream[...].astype(F32) + in_grad * silu_grad(movie_f)).astype(BF16)
 
 
-def call(body, outs, scratch, flops, *args):
+def call(body, outs, scratch, flops, *args, unplaced=(), limit=24):
     vmem = pl.BlockSpec(memory_space=pltpu.VMEM)
+    anywhere = pl.BlockSpec(memory_space=pltpu.MemorySpace.HBM)
     size = sum(a.size * a.dtype.itemsize for a in args) + sum(o.size * o.dtype.itemsize for o in outs)
     return pl.pallas_call(
         body,
         out_shape=outs,
-        in_specs=[vmem] * len(args),
+        in_specs=[anywhere if i in unplaced else vmem for i in range(len(args))],
         out_specs=[vmem] * len(outs),
         scratch_shapes=scratch,
-        compiler_params=pltpu.CompilerParams(vmem_limit_bytes=24 * 2**20),
+        compiler_params=pltpu.CompilerParams(vmem_limit_bytes=int(limit * 2**20)),
         cost_estimate=pl.CostEstimate(flops=flops, bytes_accessed=size, transcendentals=0),
     )(*args)
 
 
-def passed_along(block, axis, distance):
-    devices = range(lax.axis_size(axis))
-    route = [(i - distance, i) for i in devices if i - distance in devices]
-    return lax.ppermute(block, axis, route)
+def paired(block, first):
+    pairs = [(i, i + 1) for i in range(first, lax.axis_size("tm") - 1, 2)]
+    return lax.ppermute(block, "tm", pairs + [(j, i) for i, j in pairs])
 
 
 def swapped(block):
     return lax.ppermute(block, "dp", [(i, i ^ 1) for i in range(lax.axis_size("dp"))])
 
 
-def halving_sum(keep, send, orders):
+def distances(orders):
+    out = []
+    for groups in orders:
+        dist = [0]
+        for group in reversed(groups):
+            steps = [sum(1 << bit for n, bit in enumerate(group) if q >> n & 1) for q in range(1 << len(group))]
+            dist = [step | low for step in steps for low in dist]
+        out.append(dist)
+    return out
+
+
+def exchanged(send, steps):
     tm, dp = lax.axis_size("tm"), lax.axis_size("dp")
-    for stage in range(len(orders[0])):
-        route = [
-            (t * dp + d, (t ^ (1 << orders[d % 2][stage])) * dp + d) for t in range(tm) for d in range(dp)
-        ]
-        got = lax.ppermute(send, ("tm", "dp"), route)
-        half = keep.shape[0] // 2
-        if half:
-            send = (keep[half:] + got[half:].astype(F32)).astype(BF16)
-            keep = keep[:half] + got[:half].astype(F32)
-        else:
-            keep = keep + got.astype(F32)
-    return keep[0]
+    route = [(t * dp + d, (t ^ steps[d % 2]) * dp + d) for t in range(tm) for d in range(dp)]
+    return lax.ppermute(send, ("tm", "dp"), route)
 
 
 def body(movie, kernel_one, kernel_two, upstream):
@@ -224,19 +317,49 @@
     conv_flops = 2 * frames * cells * krows * chans
     patch = pltpu.VMEM((ext, cells + 2 * width, TAPS * chans), BF16)
 
-    before = passed_along(movie_r[frames - halo :], "tm", 1)
-    after = passed_along(upstream_r[:halo], "tm", -1)
     bundle = shape((frames + ext, cells, chans), BF16)
     field = shape(flat, BF16)
     edge = shape((halo, cells, chans), BF16)
-    keep, send, mid, grad, mid_tail, grad_head = call(
-        lambda *refs: first_kernel(width, *refs),
+    part = shape((frames * cells, chans), F32)
+    own_patch = shape((frames, cells + 2 * width, TAPS * chans), BF16)
+
+    near, far = call(
+        edges_kernel,
+        [edge, edge],
+        [pltpu.SemaphoreType.DMA((2,))],
+        8000000000,
+        movie_r, upstream_r,
+        unplaced=(0, 1),
+        limit=60,
+    )
+    near = paired(near, 0)
+    far = paired(far, 1)
+    act_in, pre_part, grad_part = call(
+        lambda *refs: inner_kernel(width, *refs),
+        [field, part, part],
+        [pltpu.VMEM(own_patch.shape, BF16)] * 2,
+        3 * conv_flops // 2,
+        movie_r, upstream_r, kernel_one, kernel_two,
+    )
+    keep, send, mid, grad, near_out, far_out = call(
+        lambda *refs: outer_kernel(width, *refs),
         [bundle, bundle, field, field, edge, edge],
-        [patch],
-        2 * conv_flops,
-        movie_r, before, upstream_r, after, kernel_one, kernel_two,
+        [pltpu.VMEM((halo, cells + 2 * width, TAPS * chans), BF16)],
+        conv_flops // 2,
+        near, far, act_in, upstream_r, pre_part, grad_part, kernel_one, kernel_two,
     )
     other = swapped(send)
+    near_mid = paired(near_out, 0)
+    far_mid = paired(far_out, 1)
+
+    def finish(near_mid, far_mid):
+        return call(
+            lambda *refs: last_kernel(width, *refs),
+            [field, field],
+            [patch],
+            2 * conv_flops,
+            movie_r, upstream_r, near_mid, far_mid, mid, grad, kernel_one, kernel_two,
+        )
 
     scratch = [
         pltpu.VMEM((2 * ext, cells + 2 * width, TAPS * chans), BF16),
@@ -244,19 +367,33 @@
     ]
     if dp == 2 and tm > 1 and tm & (tm - 1) == 0 and rows % 8 == 0:
         bits = tm.bit_length() - 1
-        orders = (list(range(bits)), [1, 0][:bits] + list(range(2, bits)))
-        distance = [
-            [sum(1 << order[s] for s in range(bits) if r >> (bits - 1 - s) & 1) for r in range(tm)]
-            for order in orders
-        ]
+        rest = [list(range(low, min(low + 2, bits))) for low in range(2, bits, 2)]
+        orders = ([[0], [1]][:bits] + rest, [[1], [0]][2 - min(bits, 2) :] + rest)
         kept, sent = call(
-            lambda *refs: relative_sums_kernel(width, distance, *refs),
+            lambda *refs: relative_sums_kernel(width, distances(orders), *refs),
             [shape((tm // 2, rows, chans), F32), shape((tm // 2, rows, chans), BF16)],
             [pltpu.VMEM((krows, chans), F32)] + scratch,
             2 * conv_flops,
             keep, other,
         )
-        mine = halving_sum(kept, sent, orders)
+        sent, near_mid, far_mid = lax.optimization_barrier((sent, near_mid, far_mid))
+        sends = [sent]
+        for stage in range(len(orders[0])):
+            steps = [distances([groups[stage : stage + 1]])[0] for groups in orders]
+            gots = [
+                exchanged(sends[q - 1], (steps[0][q], steps[1][q])) for q in reversed(range(1, len(steps[0])))
+            ]
+            if stage + 1 == len(orders[0]):
+                output, movie_grad = finish(near_mid, far_mid)
+                *gots, output, movie_grad = lax.optimization_barrier((*gots, output, movie_grad))
+            for got in gots:
+                kept = kept + got.astype(F32)
+            if stage + 1 < len(orders[0]):
+                parts = 1 << len(orders[0][stage + 1])
+                size = kept.shape[0] // parts
+                sends = [kept[q * size : (q + 1) * size].astype(BF16) for q in range(1, parts)]
+                kept = kept[:size]
+        mine = kept[0]
     else:
         (sums,) = call(
             lambda *refs: plain_sums_kernel(width, *refs),
@@ -265,20 +402,11 @@
             2 * conv_flops,
             keep, other,
         )
+        output, movie_grad = finish(near_mid, far_mid)
         mine = lax.psum_scatter(sums, "tm", scatter_dimension=0, tiled=True)
         if dp > 2:
             groups = [[d for d in range(dp) if d % 2 == parity] for parity in range(2)]
             mine = lax.psum(mine, "dp", axis_index_groups=groups)
-
-    mid_before = passed_along(mid_tail, "tm", 1)
-    grad_after = passed_along(grad_head, "tm", -1)
-    output, movie_grad = call(
-        lambda *refs: last_kernel(width, *refs),
-        [field, field],
-        [patch],
-        2 * conv_flops,
-        movie_r, upstream_r, mid_before, mid, grad, grad_after, kernel_one, kernel_two,
-    )
     theirs = swapped(mine)
     is_even = lax.axis_index("dp") % 2 == 0
     grad_one = jnp.where(is_even, mine, theirs)

time: 58.6 us -> 48 us (0.82)
  waiting for transfers between devices: 24.6 us -> 13.1 us
  local copies, waits for them, and re-layouts: 4.1 us -> 0.06 us
  starting transfers between devices: 20.7 us -> 24 us
  Pallas kernels: 7.24 us -> 9 us
    ppermute x8 -> x9, waiting for transfers between devices: 23 us -> 11.8 us  [the longest x5 11.7 us: exchanged(): return lax.ppermute(send, ('tm', 'dp'), route)]
    ppermute x8 -> x9, starting transfers between devices: 20.6 us -> 23.9 us  [the longest x5 14.6 us: exchanged(): return lax.ppermute(send, ('tm', 'dp'), route)]
    unnamed x12 -> x8, local copies, waits for them, and re-layouts: 2.36 us -> 0.02 us
    pallas_call x3 -> x5, Pallas kernels: 7.24 us -> 9 us  [call(): pl.pallas_call(body, out_shape=outs, in_specs=[anywhere if i in unplaced...]
    slice x2, local copies, waits for them, and re-layouts: 1.74 us -> 0.05 us  [body(): kept[q * size:(q + 1) * size].astype(BF16)]
  transfers between devices with their start and end apart: 10 -> 11, of which waited for: 7 -> 5; matrix products, arithmetic and copies ran while one was open for 1% -> 0% of each run, Pallas kernels for 5% -> 14%
where the time goes in v2:
time: 48 us; the launch traced here: 47.9 us
  starting transfers between devices  24 us (50%)
  waiting for transfers between devices  13.1 us (27%)
  Pallas kernels  9 us (19%)
  other arithmetic  0.86 us (2%)
  between operations  0.83 us (2%)
    ppermute x5, starting transfers between devices, exchanged(): return lax.ppermute(send, ('tm', 'dp'), route)  14.6 us
    ppermute x5, waiting for transfers between devices, exchanged(): return lax.ppermute(send, ('tm', 'dp'), route)  11.7 us
    ppermute x4, starting transfers between devices, paired(): return lax.ppermute(block, 'tm', pairs + [(j, i) for i, j in pairs])  9.24 us
    pallas_call x5, Pallas kernels, call(): pl.pallas_call(body, out_shape=outs, in_specs=[anywhere if i in unplaced...  9 us
    ppermute x2, waiting for transfers between devices, swapped(): lax.ppermute(block, 'dp', [(i, i ^ 1) for i in range(lax.axis_size('dp'))])  1.3 us
  transfers between devices with their start and end apart: 11, of which 5 were waited for; matrix products, arithmetic and copies ran while one was open for 0% of the time, Pallas kernels for 14%

profile of v2, /device:TPU:0, one launch (start us, length us, event | category | flops | bytes accessed | tf_op | source)
XLA Modules:
  0.0 47.9 jit_solution(5492366178538275829)
XLA Ops:
  0.6 0.0 copy-start
  0.6 0.0 copy-start.1
  0.7 1.7 %shard_map.75 = (bf16[2,128,128]{2,1,0:T(8,128)(2,1)}, bf16[2,128,128]{2,1,0:T(8,128)(2,1)}) custom-call(bf16[4,128,128]{2,1,0:T(8,128)(2,1)} %bitcast.10, bf16[4,128,128]{2,1,0:T(8,128)(2,1)} %bitcast.6), custom_call_target="tpu_custom_call" | custom-call | flops 8000000000 | bytes 393216 | tf_op jit(solution)/shard_map/pallas_call | solution.py:266
  2.4 3.0 %collective-permute-start = (bf16[2,128,128]{2,1,0:T(8,128)(2,1)}, bf16[2,128,128]{2,1,0:T(8,128)(2,1)S(1)}, u32[]{:S(2)}, u32[]{:S(2)}) collective-permute-start(bf16[2,128,128]{2,1,0:T(8,128)(2,1)} %get-tuple-element.27), channel_id=1, source_target_pairs={{0,2},{4,6},{8,10},{12,14},{16,18},{20,22},{24,26},{28,30},{2,0},{... | collective-permute-start | bytes 196616 | tf_op jit(solution)/shard_map/ppermute | solution.py:279
  5.4 0.7 %collective-permute-start.1 = (bf16[2,128,128]{2,1,0:T(8,128)(2,1)}, bf16[2,128,128]{2,1,0:T(8,128)(2,1)S(1)}, u32[]{:S(2)}, u32[]{:S(2)}) collective-permute-start(bf16[2,128,128]{2,1,0:T(8,128)(2,1)} %get-tuple-element.28), channel_id=1, source_target_pairs={{2,4},{6,8},{10,12},{14,16},{18,20},{22,24},{26,28},{4,2},{8,6},{1... | collective-permute-start | bytes 196616 | tf_op jit(solution)/shard_map/ppermute | solution.py:279
  6.1 1.6 %shard_map.76 = (bf16[4,128,128]{2,1,0:T(8,128)(2,1)S(1)}, f32[512,128]{1,0:T(8,128)S(1)}, f32[512,128]{1,0:T(8,128)S(1)}) custom-call(bf16[4,128,128]{2,1,0:T(8,128)(2,1)S(1)} %bitcast.11, bf16[4,128,128]{2,1,0:T(8,128)(2,1)S(1)} %bitcast.7, bf16[3456,128]{1,0:T(8,128)(2,1)S(1)} %copy-done, bf16[3456,128]{1,0:T(8,128)(2,1)S(1)} %copy-done.1), custom_call_target="tpu_custom_call" | custom-call | flops 679477248 | bytes 2686976 | tf_op jit(solution)/shard_map/pallas_call | solution.py:266
  7.7 0.1 collective-permute-done.refs_0_
  7.8 0.0 collective-permute-done.1.refs_1_
  7.8 0.7 %shard_map.77 = (bf16[10,128,128]{2,1,0:T(8,128)(2,1)S(1)}, bf16[10,128,128]{2,1,0:T(8,128)(2,1)S(1)}, bf16[4,128,128]{2,1,0:T(8,128)(2,1)S(1)}, bf16[4,128,128]...) custom-call(bf16[2,128,128]{2,1,0:T(8,128)(2,1)S(1)} %collective-permute-done.refs_0_, ...), custom_call_target="tpu_custom_call" | custom-call | flops 226492416 | bytes 3735552 | tf_op jit(solution)/shard_map/pallas_call | solution.py:266
  8.5 0.1 collective-permute-start.2
  8.6 4.9 %collective-permute-start.3 = (bf16[2,128,128]{2,1,0:T(8,128)(2,1)S(1)}, bf16[2,128,128]{2,1,0:T(8,128)(2,1)S(1)}, u32[]{:S(2)}, u32[]{:S(2)}) collective-permute-start(bf16[2,128,128]{2,1,0:T(8,128)(2,1)S(1)} %get-tuple-element.36), channel_id=1, source_target_pairs={{0,2},{4,6},{8,10},{12,14},{16,18},{20,22},{24,26},{28,30},{2,0},{... | collective-permute-start | bytes 196616 | tf_op jit(solution)/shard_map/ppermute | solution.py:279
  13.6 0.7 %collective-permute-start.4 = (bf16[2,128,128]{2,1,0:T(8,128)(2,1)S(1)}, bf16[2,128,128]{2,1,0:T(8,128)(2,1)S(1)}, u32[]{:S(2)}, u32[]{:S(2)}) collective-permute-start(bf16[2,128,128]{2,1,0:T(8,128)(2,1)S(1)} %get-tuple-element.37), channel_id=1, source_target_pairs={{2,4},{6,8},{10,12},{14,16},{18,20},{22,24},{26,28},{4,2},{8,6},{1... | collective-permute-start | bytes 196616 | tf_op jit(solution)/shard_map/ppermute | solution.py:279
  14.2 0.0 collective-permute-done.2.refs_1_
  14.2 2.1 %shard_map.78 = (f32[8,216,128]{2,1,0:T(8,128)S(1)}, bf16[8,216,128]{2,1,0:T(8,128)(2,1)S(1)}) custom-call(bf16[10,128,128]{2,1,0:T(8,128)(2,1)S(1)} %get-tuple-element.32.refs_0_, bf16[10,128,128]{2,1,0:T(8,128)(2,1)S(1)} %collective-permute-done.2.refs_1_), custom_call_target="tpu_custom_call" | custom-call | flops 905969664 | bytes 1982464 | tf_op jit(solution)/shard_map/pallas_call | solution.py:266
  16.3 0.0 collective-permute-done.3.refs_2_
  16.3 0.0 collective-permute-done.4.refs_3_
  16.3 5.9 %collective-permute-start.5 = (bf16[8,216,128]{2,1,0:T(8,128)(2,1)S(1)}, bf16[8,216,128]{2,1,0:T(8,128)(2,1)S(1)}, u32[]{:S(2)}, u32[]{:S(2)}) collective-permute-start(bf16[8,216,128]{2,1,0:T(8,128)(2,1)S(1)} %get-tuple-element.38), channel_id=1, source_target_pairs={{0,2},{1,5},{2,0},{3,7},{4,6},{5,1},{6,4},{7,3},{8,10},{9,13},{10,... | collective-permute-start | bytes 1327112 | tf_op jit(solution)/shard_map/ppermute | solution.py:300
  22.2 6.3 %collective-permute-done.5 = bf16[8,216,128]{2,1,0:T(8,128)(2,1)S(1)} collective-permute-done((bf16[8,216,128]{2,1,0:T(8,128)(2,1)S(1)}, bf16[8,216,128]{2,1,0:T(8,128)(2,1)S(1)}, u32[]{:S(2)}, u32[]{:S(2)}) %collective-permute-start.5) | collective-permute-done | bytes 442400 | tf_op jit(solution)/shard_map/ppermute | solution.py:300
  28.5 0.1 convert_add_fusion
  28.6 3.4 %collective-permute-start.6 = (bf16[4,216,128]{2,1,0:T(8,128)(2,1)S(1)}, bf16[4,216,128]{2,1,0:T(8,128)(2,1)S(1)}, u32[]{:S(2)}, u32[]{:S(2)}) collective-permute-start(bf16[4,216,128]{2,1,0:T(8,128)(2,1)S(1)} %slice.43), channel_id=1, source_target_pairs={{0,4},{1,3},{2,6},{3,1},{4,0},{5,7},{6,2},{7,5},{8,12},{9,11},{10,... | collective-permute-start | bytes 663560 | tf_op jit(solution)/shard_map/ppermute | solution.py:300
  32.0 3.9 %collective-permute-done.6 = bf16[4,216,128]{2,1,0:T(8,128)(2,1)S(1)} collective-permute-done((bf16[4,216,128]{2,1,0:T(8,128)(2,1)S(1)}, bf16[4,216,128]{2,1,0:T(8,128)(2,1)S(1)}, u32[]{:S(2)}, u32[]{:S(2)}) %collective-permute-start.6) | collective-permute-done | bytes 221216 | tf_op jit(solution)/shard_map/ppermute | solution.py:300
  35.9 0.1 fusion.3
  36.0 4.7 %collective-permute-start.7 = (bf16[1,216,128]{2,1,0:T(8,128)(2,1)S(1)}, bf16[1,216,128]{2,1,0:T(8,128)(2,1)S(1)}, u32[]{:S(2)}, u32[]{:S(2)}) collective-permute-start(bf16[1,216,128]{2,1,0:T(8,128)(2,1)S(1)} %get-tuple-element.56), channel_id=1, source_target_pairs={{0,24},{1,25},{2,26},{3,27},{4,28},{5,29},{6,30},{7,31},{8,16},{9,... | collective-permute-start | bytes 165896 | tf_op jit(solution)/shard_map/ppermute | solution.py:300
  40.7 0.0 collective-permute-start.8
  40.7 0.6 %collective-permute-start.9 = (bf16[1,216,128]{2,1,0:T(8,128)(2,1)S(1)}, bf16[1,216,128]{2,1,0:T(8,128)(2,1)S(1)}, u32[]{:S(2)}, u32[]{:S(2)}) collective-permute-start(bf16[1,216,128]{2,1,0:T(8,128)(2,1)S(1)} %get-tuple-element.54), channel_id=1, source_target_pairs={{0,8},{1,9},{2,10},{3,11},{4,12},{5,13},{6,14},{7,15},{8,0},{9,1},... | collective-permute-start | bytes 165896 | tf_op jit(solution)/shard_map/ppermute | solution.py:300
  41.3 2.9 %shard_map.79 = (bf16[4,128,128]{2,1,0:T(8,128)(2,1)}, bf16[4,128,128]{2,1,0:T(8,128)(2,1)}) custom-call(bf16[4,128,128]{2,1,0:T(8,128)(2,1)S(1)} %bitcast.12, bf16[4,128,128]{2,1,0:T(8,128)(2,1)S(1)} %bitcast.9, bf16[2,128,128]{2,1,0:T(8,128)(2,1)S(1)} %collective-permute-done.3.refs_2_, bf16[2,128,128]{2,1,0:T(8,128)(2,1)S(1)} %collective-permute-done.4.refs_3_, ...), custom_call_target="tpu_custom_call" | custom-call | flops 905969664 | bytes 2686976 | tf_op jit(solution)/shard_map/pallas_call | solution.py:266
  44.2 0.0 collective-permute-done.7
  44.2 1.5 %collective-permute-done.8 = bf16[1,216,128]{2,1,0:T(8,128)(2,1)S(1)} collective-permute-done((bf16[1,216,128]{2,1,0:T(8,128)(2,1)S(1)}, bf16[1,216,128]{2,1,0:T(8,128)(2,1)S(1)}, u32[]{:S(2)}, u32[]{:S(2)}) %collective-permute-start.8) | collective-permute-done | bytes 55328 | tf_op jit(solution)/shard_map/ppermute | solution.py:300
  45.8 0.0 collective-permute-done.9
  45.8 0.1 collective-permute-start.10
  45.9 1.3 %collective-permute-done.10 = f32[216,128]{1,0:T(8,128)S(1)} collective-permute-done((f32[216,128]{1,0:T(8,128)S(1)}, f32[216,128]{1,0:T(8,128)S(1)}, u32[]{:S(2)}, u32[]{:S(2)}) %collective-permute-start.10) | collective-permute-done | bytes 110624 | tf_op jit(solution)/shard_map/ppermute | solution.py:283
  47.2 0.7 %broadcast_select_fusion = (f32[216,128]{1,0:T(8,128)}, f32[216,128]{1,0:T(8,128)}) fusion(f32[216,128]{1,0:T(8,128)S(1)} %collective-permute-done.10, f32[216,128]{1,0:T(8,128)S(1)} %fusion.2, pred[]{:T(512)S(6)} %eq.5), kind=kLoop, calls=%fused_computation.7 | loop fusion | flops 55296 | bytes 442369 | tf_op jit(solution)/shard_map/jit(_where)/select_n | solution.py:413
  (9 shorter events, 0.1 us)
Async XLA Ops:
  0.6 5.4 %copy-start = (bf16[3456,128]{1,0:T(8,128)(2,1)S(1)}, bf16[3456,128]{1,0:T(8,128)(2,1)}, u32[]{:S(2)}) copy-start(bf16[3456,128]{1,0:T(8,128)(2,1)} %refs_6_.3) | copy-start | bytes 2654212
  0.6 5.4 %copy-start.1 = (bf16[3456,128]{1,0:T(8,128)(2,1)S(1)}, bf16[3456,128]{1,0:T(8,128)(2,1)}, u32[]{:S(2)}) copy-start(bf16[3456,128]{1,0:T(8,128)(2,1)} %refs_7_.3) | copy-start | bytes 2654212
  0.7 5.4 %copy-start.2 = (bf16[1,4,8,16,128]{4,3,2,1,0:T(8,128)(2,1)S(1)}, bf16[1,4,8,16,128]{4,3,2,1,0:T(8,128)(2,1)}, u32[]{:S(2)}) copy-start(bf16[1,4,8,16,128]{4,3,2,1,0:T(8,128)(2,1)} %param.7) | copy-start | bytes 393220
  0.7 5.4 %copy-start.3 = (bf16[1,4,8,16,128]{4,3,2,1,0:T(8,128)(2,1)S(1)}, bf16[1,4,8,16,128]{4,3,2,1,0:T(8,128)(2,1)}, u32[]{:S(2)}) copy-start(bf16[1,4,8,16,128]{4,3,2,1,0:T(8,128)(2,1)} %param.4) | copy-start | bytes 393220
  2.4 5.5 %collective-permute-start = (bf16[2,128,128]{2,1,0:T(8,128)(2,1)}, bf16[2,128,128]{2,1,0:T(8,128)(2,1)S(1)}, u32[]{:S(2)}, u32[]{:S(2)}) collective-permute-start(bf16[2,128,128]{2,1,0:T(8,128)(2,1)} %get-tuple-element.27), channel_id=1, source_target_pairs={{0,2},{4,6},{8,10},{12,14},{16,18},{20,22},{24,26},{28,30},{2,0},{... | collective-permute-start | bytes 196616 | tf_op jit(solution)/shard_map/ppermute | solution.py:279
  5.4 2.5 %collective-permute-start.1 = (bf16[2,128,128]{2,1,0:T(8,128)(2,1)}, bf16[2,128,128]{2,1,0:T(8,128)(2,1)S(1)}, u32[]{:S(2)}, u32[]{:S(2)}) collective-permute-start(bf16[2,128,128]{2,1,0:T(8,128)(2,1)} %get-tuple-element.28), channel_id=1, source_target_pairs={{2,4},{6,8},{10,12},{14,16},{18,20},{22,24},{26,28},{4,2},{8,6},{1... | collective-permute-start | bytes 196616 | tf_op jit(solution)/shard_map/ppermute | solution.py:279
  8.5 5.7 %collective-permute-start.2 = (bf16[10,128,128]{2,1,0:T(8,128)(2,1)S(1)}, bf16[10,128,128]{2,1,0:T(8,128)(2,1)S(1)}, u32[]{:S(2)}, u32[]{:S(2)}) collective-permute-start(bf16[10,128,128]{2,1,0:T(8,128)(2,1)S(1)} %get-tuple-element.33), channel_id=1, source_target_pairs={{0,1},{1,0},{2,3},{3,2},{4,5},{5,4},{6,7},{7,6},{8,9},{9,8},{10,11... | collective-permute-start | bytes 983048 | tf_op jit(solution)/shard_map/ppermute | solution.py:283
  8.6 7.7 %collective-permute-start.3 = (bf16[2,128,128]{2,1,0:T(8,128)(2,1)S(1)}, bf16[2,128,128]{2,1,0:T(8,128)(2,1)S(1)}, u32[]{:S(2)}, u32[]{:S(2)}) collective-permute-start(bf16[2,128,128]{2,1,0:T(8,128)(2,1)S(1)} %get-tuple-element.36), channel_id=1, source_target_pairs={{0,2},{4,6},{8,10},{12,14},{16,18},{20,22},{24,26},{28,30},{2,0},{... | collective-permute-start | bytes 196616 | tf_op jit(solution)/shard_map/ppermute | solution.py:279
  13.6 2.8 %collective-permute-start.4 = (bf16[2,128,128]{2,1,0:T(8,128)(2,1)S(1)}, bf16[2,128,128]{2,1,0:T(8,128)(2,1)S(1)}, u32[]{:S(2)}, u32[]{:S(2)}) collective-permute-start(bf16[2,128,128]{2,1,0:T(8,128)(2,1)S(1)} %get-tuple-element.37), channel_id=1, source_target_pairs={{2,4},{6,8},{10,12},{14,16},{18,20},{22,24},{26,28},{4,2},{8,6},{1... | collective-permute-start | bytes 196616 | tf_op jit(solution)/shard_map/ppermute | solution.py:279
  16.3 12.2 %collective-permute-start.5 = (bf16[8,216,128]{2,1,0:T(8,128)(2,1)S(1)}, bf16[8,216,128]{2,1,0:T(8,128)(2,1)S(1)}, u32[]{:S(2)}, u32[]{:S(2)}) collective-permute-start(bf16[8,216,128]{2,1,0:T(8,128)(2,1)S(1)} %get-tuple-element.38), channel_id=1, source_target_pairs={{0,2},{1,5},{2,0},{3,7},{4,6},{5,1},{6,4},{7,3},{8,10},{9,13},{10,... | collective-permute-start | bytes 1327112 | tf_op jit(solution)/shard_map/ppermute | solution.py:300
  28.6 7.3 %collective-permute-start.6 = (bf16[4,216,128]{2,1,0:T(8,128)(2,1)S(1)}, bf16[4,216,128]{2,1,0:T(8,128)(2,1)S(1)}, u32[]{:S(2)}, u32[]{:S(2)}) collective-permute-start(bf16[4,216,128]{2,1,0:T(8,128)(2,1)S(1)} %slice.43), channel_id=1, source_target_pairs={{0,4},{1,3},{2,6},{3,1},{4,0},{5,7},{6,2},{7,5},{8,12},{9,11},{10,... | collective-permute-start | bytes 663560 | tf_op jit(solution)/shard_map/ppermute | solution.py:300
  36.0 8.2 %collective-permute-start.7 = (bf16[1,216,128]{2,1,0:T(8,128)(2,1)S(1)}, bf16[1,216,128]{2,1,0:T(8,128)(2,1)S(1)}, u32[]{:S(2)}, u32[]{:S(2)}) collective-permute-start(bf16[1,216,128]{2,1,0:T(8,128)(2,1)S(1)} %get-tuple-element.56), channel_id=1, source_target_pairs={{0,24},{1,25},{2,26},{3,27},{4,28},{5,29},{6,30},{7,31},{8,16},{9,... | collective-permute-start | bytes 165896 | tf_op jit(solution)/shard_map/ppermute | solution.py:300
  40.7 5.1 %collective-permute-start.8 = (bf16[1,216,128]{2,1,0:T(8,128)(2,1)S(1)}, bf16[1,216,128]{2,1,0:T(8,128)(2,1)S(1)}, u32[]{:S(2)}, u32[]{:S(2)}) collective-permute-start(bf16[1,216,128]{2,1,0:T(8,128)(2,1)S(1)} %get-tuple-element.55), channel_id=1, source_target_pairs={{0,16},{1,17},{2,18},{3,19},{4,20},{5,21},{6,22},{7,23},{8,24},{9,... | collective-permute-start | bytes 165896 | tf_op jit(solution)/shard_map/ppermute | solution.py:300
  40.7 5.1 %collective-permute-start.9 = (bf16[1,216,128]{2,1,0:T(8,128)(2,1)S(1)}, bf16[1,216,128]{2,1,0:T(8,128)(2,1)S(1)}, u32[]{:S(2)}, u32[]{:S(2)}) collective-permute-start(bf16[1,216,128]{2,1,0:T(8,128)(2,1)S(1)} %get-tuple-element.54), channel_id=1, source_target_pairs={{0,8},{1,9},{2,10},{3,11},{4,12},{5,13},{6,14},{7,15},{8,0},{9,1},... | collective-permute-start | bytes 165896 | tf_op jit(solution)/shard_map/ppermute | solution.py:300
  45.8 1.4 %collective-permute-start.10 = (f32[216,128]{1,0:T(8,128)S(1)}, f32[216,128]{1,0:T(8,128)S(1)}, u32[]{:S(2)}, u32[]{:S(2)}) collective-permute-start(f32[216,128]{1,0:T(8,128)S(1)} %fusion.2), channel_id=1, source_target_pairs={{0,1},{1,0},{2,3},{3,2},{4,5},{5,4},{6,7},{7,6},{8,9},{9,8},{10,11... | collective-permute-start | bytes 331784 | tf_op jit(solution)/shard_map/ppermute | solution.py:283

commit v3 on v2

--- a/solution.py
+++ b/solution.py
@@ -330,7 +330,7 @@
         8000000000,
         movie_r, upstream_r,
         unplaced=(0, 1),
-        limit=60,
+        limit=53.8,
     )
     near = paired(near, 0)
     far = paired(far, 1)
@@ -376,13 +376,15 @@
             2 * conv_flops,
             keep, other,
         )
-        sent, near_mid, far_mid = lax.optimization_barrier((sent, near_mid, far_mid))
+        sent, near_mid = lax.optimization_barrier((sent, near_mid))
         sends = [sent]
         for stage in range(len(orders[0])):
             steps = [distances([groups[stage : stage + 1]])[0] for groups in orders]
             gots = [
                 exchanged(sends[q - 1], (steps[0][q], steps[1][q])) for q in reversed(range(1, len(steps[0])))
             ]
+            if stage == 0:
+                *gots, far_mid = lax.optimization_barrier((*gots, far_mid))
             if stage + 1 == len(orders[0]):
                 output, movie_grad = finish(near_mid, far_mid)
                 *gots, output, movie_grad = lax.optimization_barrier((*gots, output, movie_grad))

time: 48 us -> 44.4 us (0.925)
  starting transfers between devices: 24 us -> 20.1 us
  waiting for transfers between devices: 13.1 us -> 13.9 us
  Pallas kernels: 9 us -> 8.41 us
    ppermute x5, starting transfers between devices: 14.6 us -> 10.9 us  [exchanged(): return lax.ppermute(send, ('tm', 'dp'), route)]
    pallas_call x5, Pallas kernels: 9 us -> 8.41 us  [call(): pl.pallas_call(body, out_shape=outs, in_specs=[anywhere if i in unplaced...]
    ppermute x4, waiting for transfers between devices: 0.11 us -> 0.62 us  [paired(): return lax.ppermute(block, 'tm', pairs + [(j, i) for i, j in pairs])]
  transfers between devices with their start and end apart: 11 -> 11, of which waited for: 5 -> 5; matrix products, arithmetic and copies ran while one was open for 0% -> 0% of each run, Pallas kernels for 14% -> 15%
where the time goes in v3:
time: 44.4 us; the launch traced here: 44.2 us
  starting transfers between devices  20.1 us (45%)
  waiting for transfers between devices  13.9 us (31%)
  Pallas kernels  8.41 us (19%)
  other arithmetic  0.86 us (2%)
  between operations  0.83 us (2%)
    ppermute x5, waiting for transfers between devices, exchanged(): return lax.ppermute(send, ('tm', 'dp'), route)  12 us
    ppermute x5, starting transfers between devices, exchanged(): return lax.ppermute(send, ('tm', 'dp'), route)  10.9 us
    ppermute x4, starting transfers between devices, paired(): return lax.ppermute(block, 'tm', pairs + [(j, i) for i, j in pairs])  9.08 us
    pallas_call x5, Pallas kernels, call(): pl.pallas_call(body, out_shape=outs, in_specs=[anywhere if i in unplaced...  8.41 us
    ppermute x2, waiting for transfers between devices, swapped(): lax.ppermute(block, 'dp', [(i, i ^ 1) for i in range(lax.axis_size('dp'))])  1.3 us
  transfers between devices with their start and end apart: 11, of which 5 were waited for; matrix products, arithmetic and copies ran while one was open for 0% of the time, Pallas kernels for 15%

profile of v3, /device:TPU:0, one launch (start us, length us, event | category | flops | bytes accessed | tf_op | source)
XLA Modules:
  0.0 44.2 jit_solution(12284673367897567116)
XLA Ops:
  0.6 0.0 copy-start
  0.6 0.0 copy-start.1
  0.7 1.0 %shard_map.75 = (bf16[2,128,128]{2,1,0:T(8,128)(2,1)S(1)}, bf16[2,128,128]{2,1,0:T(8,128)(2,1)S(1)}) custom-call(bf16[4,128,128]{2,1,0:T(8,128)(2,1)} %bitcast.10, bf16[4,128,128]{2,1,0:T(8,128)(2,1)} %bitcast.6), custom_call_target="tpu_custom_call" | custom-call | flops 8000000000 | bytes 393216 | tf_op jit(solution)/shard_map/pallas_call | solution.py:266
  1.7 3.0 %collective-permute-start = (bf16[2,128,128]{2,1,0:T(8,128)(2,1)S(1)}, bf16[2,128,128]{2,1,0:T(8,128)(2,1)S(1)}, u32[]{:S(2)}, u32[]{:S(2)}) collective-permute-start(bf16[2,128,128]{2,1,0:T(8,128)(2,1)S(1)} %get-tuple-element.28), channel_id=1, source_target_pairs={{0,2},{4,6},{8,10},{12,14},{16,18},{20,22},{24,26},{28,30},{2,0},{... | collective-permute-start | bytes 196616 | tf_op jit(solution)/shard_map/ppermute | solution.py:279
  4.7 0.7 %collective-permute-start.1 = (bf16[2,128,128]{2,1,0:T(8,128)(2,1)S(1)}, bf16[2,128,128]{2,1,0:T(8,128)(2,1)S(1)}, u32[]{:S(2)}, u32[]{:S(2)}) collective-permute-start(bf16[2,128,128]{2,1,0:T(8,128)(2,1)S(1)} %get-tuple-element.29), channel_id=1, source_target_pairs={{2,4},{6,8},{10,12},{14,16},{18,20},{22,24},{26,28},{4,2},{8,6},{1... | collective-permute-start | bytes 196616 | tf_op jit(solution)/shard_map/ppermute | solution.py:279
  5.4 1.7 %shard_map.76 = (bf16[4,128,128]{2,1,0:T(8,128)(2,1)S(1)}, f32[512,128]{1,0:T(8,128)S(1)}, f32[512,128]{1,0:T(8,128)S(1)}) custom-call(bf16[4,128,128]{2,1,0:T(8,128)(2,1)S(1)} %bitcast.11, bf16[4,128,128]{2,1,0:T(8,128)(2,1)S(1)} %bitcast.7, bf16[3456,128]{1,0:T(8,128)(2,1)S(1)} %copy-done, bf16[3456,128]{1,0:T(8,128)(2,1)S(1)} %copy-done.1), custom_call_target="tpu_custom_call" | custom-call | flops 679477248 | bytes 2686976 | tf_op jit(solution)/shard_map/pallas_call | solution.py:266
  7.1 0.0 collective-permute-done.refs_0_
  7.1 0.0 collective-permute-done.1.refs_1_
  7.1 0.7 %shard_map.77 = (bf16[10,128,128]{2,1,0:T(8,128)(2,1)S(1)}, bf16[10,128,128]{2,1,0:T(8,128)(2,1)S(1)}, bf16[4,128,128]{2,1,0:T(8,128)(2,1)S(1)}, bf16[4,128,128]...) custom-call(bf16[2,128,128]{2,1,0:T(8,128)(2,1)S(1)} %collective-permute-done.refs_0_, ...), custom_call_target="tpu_custom_call" | custom-call | flops 226492416 | bytes 3735552 | tf_op jit(solution)/shard_map/pallas_call | solution.py:266
  7.9 0.1 collective-permute-start.2
  8.0 4.8 %collective-permute-start.3 = (bf16[2,128,128]{2,1,0:T(8,128)(2,1)S(1)}, bf16[2,128,128]{2,1,0:T(8,128)(2,1)S(1)}, u32[]{:S(2)}, u32[]{:S(2)}) collective-permute-start(bf16[2,128,128]{2,1,0:T(8,128)(2,1)S(1)} %get-tuple-element.37), channel_id=1, source_target_pairs={{0,2},{4,6},{8,10},{12,14},{16,18},{20,22},{24,26},{28,30},{2,0},{... | collective-permute-start | bytes 196616 | tf_op jit(solution)/shard_map/ppermute | solution.py:279
  12.7 0.0 collective-permute-done.2.refs_1_
  12.7 2.1 %shard_map.78 = (f32[8,216,128]{2,1,0:T(8,128)S(1)}, bf16[8,216,128]{2,1,0:T(8,128)(2,1)S(1)}) custom-call(bf16[10,128,128]{2,1,0:T(8,128)(2,1)S(1)} %get-tuple-element.33.refs_0_, bf16[10,128,128]{2,1,0:T(8,128)(2,1)S(1)} %collective-permute-done.2.refs_1_), custom_call_target="tpu_custom_call" | custom-call | flops 905969664 | bytes 1982464 | tf_op jit(solution)/shard_map/pallas_call | solution.py:266
  14.8 0.6 %collective-permute-done.3.refs_2_ = bf16[2,128,128]{2,1,0:T(8,128)(2,1)S(1)} collective-permute-done((bf16[2,128,128]{2,1,0:T(8,128)(2,1)S(1)}, bf16[2,128,128]{2,1,0:T(8,128)(2,1)S(1)}, u32[]{:S(2)}, u32[]{:S(2)}) %collective-permute-start.3) | collective-permute-done | bytes 65568 | tf_op jit(solution)/shard_map/ppermute | solution.py:279
  15.4 1.8 %collective-permute-start.4 = (bf16[8,216,128]{2,1,0:T(8,128)(2,1)S(1)}, bf16[8,216,128]{2,1,0:T(8,128)(2,1)S(1)}, u32[]{:S(2)}, u32[]{:S(2)}) collective-permute-start(bf16[8,216,128]{2,1,0:T(8,128)(2,1)S(1)} %get-tuple-element.38), channel_id=1, source_target_pairs={{0,2},{1,5},{2,0},{3,7},{4,6},{5,1},{6,4},{7,3},{8,10},{9,13},{10,... | collective-permute-start | bytes 1327112 | tf_op jit(solution)/shard_map/ppermute | solution.py:300
  17.2 0.7 %collective-permute-start.5 = (bf16[2,128,128]{2,1,0:T(8,128)(2,1)S(1)}, bf16[2,128,128]{2,1,0:T(8,128)(2,1)S(1)}, u32[]{:S(2)}, u32[]{:S(2)}) collective-permute-start(bf16[2,128,128]{2,1,0:T(8,128)(2,1)S(1)} %get-tuple-element.39), channel_id=1, source_target_pairs={{2,4},{6,8},{10,12},{14,16},{18,20},{22,24},{26,28},{4,2},{8,6},{1... | collective-permute-start | bytes 196616 | tf_op jit(solution)/shard_map/ppermute | solution.py:279
  17.8 0.0 collective-permute-done.5.refs_3_
  17.8 6.6 %collective-permute-done.4 = bf16[8,216,128]{2,1,0:T(8,128)(2,1)S(1)} collective-permute-done((bf16[8,216,128]{2,1,0:T(8,128)(2,1)S(1)}, bf16[8,216,128]{2,1,0:T(8,128)(2,1)S(1)}, u32[]{:S(2)}, u32[]{:S(2)}) %collective-permute-start.4) | collective-permute-done | bytes 442400 | tf_op jit(solution)/shard_map/ppermute | solution.py:300
  24.4 0.1 convert_add_fusion
  24.5 2.9 %collective-permute-start.6 = (bf16[4,216,128]{2,1,0:T(8,128)(2,1)S(1)}, bf16[4,216,128]{2,1,0:T(8,128)(2,1)S(1)}, u32[]{:S(2)}, u32[]{:S(2)}) collective-permute-start(bf16[4,216,128]{2,1,0:T(8,128)(2,1)S(1)} %slice.43), channel_id=1, source_target_pairs={{0,4},{1,3},{2,6},{3,1},{4,0},{5,7},{6,2},{7,5},{8,12},{9,11},{10,... | collective-permute-start | bytes 663560 | tf_op jit(solution)/shard_map/ppermute | solution.py:300
  27.5 3.9 %collective-permute-done.6 = bf16[4,216,128]{2,1,0:T(8,128)(2,1)S(1)} collective-permute-done((bf16[4,216,128]{2,1,0:T(8,128)(2,1)S(1)}, bf16[4,216,128]{2,1,0:T(8,128)(2,1)S(1)}, u32[]{:S(2)}, u32[]{:S(2)}) %collective-permute-start.6) | collective-permute-done | bytes 221216 | tf_op jit(solution)/shard_map/ppermute | solution.py:300
  31.4 0.1 fusion.3
  31.5 5.6 %collective-permute-start.7 = (bf16[1,216,128]{2,1,0:T(8,128)(2,1)S(1)}, bf16[1,216,128]{2,1,0:T(8,128)(2,1)S(1)}, u32[]{:S(2)}, u32[]{:S(2)}) collective-permute-start(bf16[1,216,128]{2,1,0:T(8,128)(2,1)S(1)} %get-tuple-element.58), channel_id=1, source_target_pairs={{0,24},{1,25},{2,26},{3,27},{4,28},{5,29},{6,30},{7,31},{8,16},{9,... | collective-permute-start | bytes 165896 | tf_op jit(solution)/shard_map/ppermute | solution.py:300
  37.0 0.0 collective-permute-start.8
  37.0 0.6 %collective-permute-start.9 = (bf16[1,216,128]{2,1,0:T(8,128)(2,1)S(1)}, bf16[1,216,128]{2,1,0:T(8,128)(2,1)S(1)}, u32[]{:S(2)}, u32[]{:S(2)}) collective-permute-start(bf16[1,216,128]{2,1,0:T(8,128)(2,1)S(1)} %get-tuple-element.56), channel_id=1, source_target_pairs={{0,8},{1,9},{2,10},{3,11},{4,12},{5,13},{6,14},{7,15},{8,0},{9,1},... | collective-permute-start | bytes 165896 | tf_op jit(solution)/shard_map/ppermute | solution.py:300
  37.7 2.9 %shard_map.79 = (bf16[4,128,128]{2,1,0:T(8,128)(2,1)}, bf16[4,128,128]{2,1,0:T(8,128)(2,1)}) custom-call(bf16[4,128,128]{2,1,0:T(8,128)(2,1)S(1)} %bitcast.12, bf16[4,128,128]{2,1,0:T(8,128)(2,1)S(1)} %bitcast.9, bf16[2,128,128]{2,1,0:T(8,128)(2,1)S(1)} %collective-permute-done.3.refs_2_, bf16[2,128,128]{2,1,0:T(8,128)(2,1)S(1)} %collective-permute-done.5.refs_3_, ...), custom_call_target="tpu_custom_call" | custom-call | flops 905969664 | bytes 2686976 | tf_op jit(solution)/shard_map/pallas_call | solution.py:266
  40.6 0.0 collective-permute-done.7
  40.6 1.5 %collective-permute-done.8 = bf16[1,216,128]{2,1,0:T(8,128)(2,1)S(1)} collective-permute-done((bf16[1,216,128]{2,1,0:T(8,128)(2,1)S(1)}, bf16[1,216,128]{2,1,0:T(8,128)(2,1)S(1)}, u32[]{:S(2)}, u32[]{:S(2)}) %collective-permute-start.8) | collective-permute-done | bytes 55328 | tf_op jit(solution)/shard_map/ppermute | solution.py:300
  42.1 0.0 collective-permute-done.9
  42.1 0.1 collective-permute-start.10
  42.2 1.3 %collective-permute-done.10 = f32[216,128]{1,0:T(8,128)S(1)} collective-permute-done((f32[216,128]{1,0:T(8,128)S(1)}, f32[216,128]{1,0:T(8,128)S(1)}, u32[]{:S(2)}, u32[]{:S(2)}) %collective-permute-start.10) | collective-permute-done | bytes 110624 | tf_op jit(solution)/shard_map/ppermute | solution.py:283
  43.5 0.7 %broadcast_select_fusion = (f32[216,128]{1,0:T(8,128)}, f32[216,128]{1,0:T(8,128)}) fusion(f32[216,128]{1,0:T(8,128)S(1)} %collective-permute-done.10, f32[216,128]{1,0:T(8,128)S(1)} %fusion.2, pred[]{:T(512)S(6)} %eq.5), kind=kLoop, calls=%fused_computation.7 | loop fusion | flops 55296 | bytes 442369 | tf_op jit(solution)/shard_map/jit(_where)/select_n | solution.py:415
  (9 shorter events, 0.1 us)
Async XLA Ops:
  0.6 4.8 %copy-start = (bf16[3456,128]{1,0:T(8,128)(2,1)S(1)}, bf16[3456,128]{1,0:T(8,128)(2,1)}, u32[]{:S(2)}) copy-start(bf16[3456,128]{1,0:T(8,128)(2,1)} %refs_6_.3) | copy-start | bytes 2654212
  0.6 4.8 %copy-start.1 = (bf16[3456,128]{1,0:T(8,128)(2,1)S(1)}, bf16[3456,128]{1,0:T(8,128)(2,1)}, u32[]{:S(2)}) copy-start(bf16[3456,128]{1,0:T(8,128)(2,1)} %refs_7_.3) | copy-start | bytes 2654212
  0.7 4.8 %copy-start.2 = (bf16[1,4,8,16,128]{4,3,2,1,0:T(8,128)(2,1)S(1)}, bf16[1,4,8,16,128]{4,3,2,1,0:T(8,128)(2,1)}, u32[]{:S(2)}) copy-start(bf16[1,4,8,16,128]{4,3,2,1,0:T(8,128)(2,1)} %param.7) | copy-start | bytes 393220
  0.7 4.8 %copy-start.3 = (bf16[1,4,8,16,128]{4,3,2,1,0:T(8,128)(2,1)S(1)}, bf16[1,4,8,16,128]{4,3,2,1,0:T(8,128)(2,1)}, u32[]{:S(2)}) copy-start(bf16[1,4,8,16,128]{4,3,2,1,0:T(8,128)(2,1)} %param.4) | copy-start | bytes 393220
  1.7 5.4 %collective-permute-start = (bf16[2,128,128]{2,1,0:T(8,128)(2,1)S(1)}, bf16[2,128,128]{2,1,0:T(8,128)(2,1)S(1)}, u32[]{:S(2)}, u32[]{:S(2)}) collective-permute-start(bf16[2,128,128]{2,1,0:T(8,128)(2,1)S(1)} %get-tuple-element.28), channel_id=1, source_target_pairs={{0,2},{4,6},{8,10},{12,14},{16,18},{20,22},{24,26},{28,30},{2,0},{... | collective-permute-start | bytes 196616 | tf_op jit(solution)/shard_map/ppermute | solution.py:279
  4.7 2.4 %collective-permute-start.1 = (bf16[2,128,128]{2,1,0:T(8,128)(2,1)S(1)}, bf16[2,128,128]{2,1,0:T(8,128)(2,1)S(1)}, u32[]{:S(2)}, u32[]{:S(2)}) collective-permute-start(bf16[2,128,128]{2,1,0:T(8,128)(2,1)S(1)} %get-tuple-element.29), channel_id=1, source_target_pairs={{2,4},{6,8},{10,12},{14,16},{18,20},{22,24},{26,28},{4,2},{8,6},{1... | collective-permute-start | bytes 196616 | tf_op jit(solution)/shard_map/ppermute | solution.py:279
  7.9 4.8 %collective-permute-start.2 = (bf16[10,128,128]{2,1,0:T(8,128)(2,1)S(1)}, bf16[10,128,128]{2,1,0:T(8,128)(2,1)S(1)}, u32[]{:S(2)}, u32[]{:S(2)}) collective-permute-start(bf16[10,128,128]{2,1,0:T(8,128)(2,1)S(1)} %get-tuple-element.34), channel_id=1, source_target_pairs={{0,1},{1,0},{2,3},{3,2},{4,5},{5,4},{6,7},{7,6},{8,9},{9,8},{10,11... | collective-permute-start | bytes 983048 | tf_op jit(solution)/shard_map/ppermute | solution.py:283
  8.0 7.5 %collective-permute-start.3 = (bf16[2,128,128]{2,1,0:T(8,128)(2,1)S(1)}, bf16[2,128,128]{2,1,0:T(8,128)(2,1)S(1)}, u32[]{:S(2)}, u32[]{:S(2)}) collective-permute-start(bf16[2,128,128]{2,1,0:T(8,128)(2,1)S(1)} %get-tuple-element.37), channel_id=1, source_target_pairs={{0,2},{4,6},{8,10},{12,14},{16,18},{20,22},{24,26},{28,30},{2,0},{... | collective-permute-start | bytes 196616 | tf_op jit(solution)/shard_map/ppermute | solution.py:279
  15.4 9.0 %collective-permute-start.4 = (bf16[8,216,128]{2,1,0:T(8,128)(2,1)S(1)}, bf16[8,216,128]{2,1,0:T(8,128)(2,1)S(1)}, u32[]{:S(2)}, u32[]{:S(2)}) collective-permute-start(bf16[8,216,128]{2,1,0:T(8,128)(2,1)S(1)} %get-tuple-element.38), channel_id=1, source_target_pairs={{0,2},{1,5},{2,0},{3,7},{4,6},{5,1},{6,4},{7,3},{8,10},{9,13},{10,... | collective-permute-start | bytes 1327112 | tf_op jit(solution)/shard_map/ppermute | solution.py:300
  17.2 0.7 %collective-permute-start.5 = (bf16[2,128,128]{2,1,0:T(8,128)(2,1)S(1)}, bf16[2,128,128]{2,1,0:T(8,128)(2,1)S(1)}, u32[]{:S(2)}, u32[]{:S(2)}) collective-permute-start(bf16[2,128,128]{2,1,0:T(8,128)(2,1)S(1)} %get-tuple-element.39), channel_id=1, source_target_pairs={{2,4},{6,8},{10,12},{14,16},{18,20},{22,24},{26,28},{4,2},{8,6},{1... | collective-permute-start | bytes 196616 | tf_op jit(solution)/shard_map/ppermute | solution.py:279
  24.5 6.8 %collective-permute-start.6 = (bf16[4,216,128]{2,1,0:T(8,128)(2,1)S(1)}, bf16[4,216,128]{2,1,0:T(8,128)(2,1)S(1)}, u32[]{:S(2)}, u32[]{:S(2)}) collective-permute-start(bf16[4,216,128]{2,1,0:T(8,128)(2,1)S(1)} %slice.43), channel_id=1, source_target_pairs={{0,4},{1,3},{2,6},{3,1},{4,0},{5,7},{6,2},{7,5},{8,12},{9,11},{10,... | collective-permute-start | bytes 663560 | tf_op jit(solution)/shard_map/ppermute | solution.py:300
  31.5 9.1 %collective-permute-start.7 = (bf16[1,216,128]{2,1,0:T(8,128)(2,1)S(1)}, bf16[1,216,128]{2,1,0:T(8,128)(2,1)S(1)}, u32[]{:S(2)}, u32[]{:S(2)}) collective-permute-start(bf16[1,216,128]{2,1,0:T(8,128)(2,1)S(1)} %get-tuple-element.58), channel_id=1, source_target_pairs={{0,24},{1,25},{2,26},{3,27},{4,28},{5,29},{6,30},{7,31},{8,16},{9,... | collective-permute-start | bytes 165896 | tf_op jit(solution)/shard_map/ppermute | solution.py:300
  37.0 5.1 %collective-permute-start.8 = (bf16[1,216,128]{2,1,0:T(8,128)(2,1)S(1)}, bf16[1,216,128]{2,1,0:T(8,128)(2,1)S(1)}, u32[]{:S(2)}, u32[]{:S(2)}) collective-permute-start(bf16[1,216,128]{2,1,0:T(8,128)(2,1)S(1)} %get-tuple-element.57), channel_id=1, source_target_pairs={{0,16},{1,17},{2,18},{3,19},{4,20},{5,21},{6,22},{7,23},{8,24},{9,... | collective-permute-start | bytes 165896 | tf_op jit(solution)/shard_map/ppermute | solution.py:300
  37.0 5.1 %collective-permute-start.9 = (bf16[1,216,128]{2,1,0:T(8,128)(2,1)S(1)}, bf16[1,216,128]{2,1,0:T(8,128)(2,1)S(1)}, u32[]{:S(2)}, u32[]{:S(2)}) collective-permute-start(bf16[1,216,128]{2,1,0:T(8,128)(2,1)S(1)} %get-tuple-element.56), channel_id=1, source_target_pairs={{0,8},{1,9},{2,10},{3,11},{4,12},{5,13},{6,14},{7,15},{8,0},{9,1},... | collective-permute-start | bytes 165896 | tf_op jit(solution)/shard_map/ppermute | solution.py:300
  42.1 1.4 %collective-permute-start.10 = (f32[216,128]{1,0:T(8,128)S(1)}, f32[216,128]{1,0:T(8,128)S(1)}, u32[]{:S(2)}, u32[]{:S(2)}) collective-permute-start(f32[216,128]{1,0:T(8,128)S(1)} %fusion.2), channel_id=1, source_target_pairs={{0,1},{1,0},{2,3},{3,2},{4,5},{5,4},{6,7},{7,6},{8,9},{9,8},{10,11... | collective-permute-start | bytes 331784 | tf_op jit(solution)/shard_map/ppermute | solution.py:283

commit v4 on v3

--- a/solution.py
+++ b/solution.py
@@ -139,7 +139,7 @@
 
 
 def outer_kernel(
-    width, near, far, act_in, upstream, pre_part, grad_part, one, two, keep, send, mid, grad, near_out, far_out, patches
+    width, far, near, act_in, upstream, pre_part, grad_part, one, two, keep, send, mid, grad, near_out, far_out, patches
 ):
     frames, cells, chans = act_in.shape
     halo = TAPS - 1
@@ -232,19 +232,17 @@
     kernel_sums(width, own, other, acc, patches, turned)
 
 
-def relative_sums_kernel(width, distance, own, other, keep, send, acc, patches, turned):
+def relative_sums_kernel(width, distance, own, other, stay, pass_on, send_stay, send_on, acc, patches, turned):
     kernel_sums(width, own, other, acc, patches, turned)
-    half, rows, _ = keep.shape
+    size, rows, _ = stay.shape
     odd = lax.axis_index("dp") % 2
     me = lax.axis_index("tm")
-    for r in range(2 * half):
-        far = jnp.where(odd == 1, distance[1][r], distance[0][r])
-        block = jnp.bitwise_xor(me, far)
-        part = acc[pl.ds(pl.multiple_of(block * rows, 8), rows), :]
-        if r < half:
-            keep[r] = part
-        else:
-            send[r - half] = part.astype(BF16)
+    for n, quarter in enumerate((stay, pass_on, send_stay, send_on)):
+        for r in range(size):
+            far = jnp.where(odd == 1, distance[1][n * size + r], distance[0][n * size + r])
+            block = jnp.bitwise_xor(me, far)
+            part = acc[pl.ds(pl.multiple_of(block * rows, 8), rows), :]
+            quarter[r] = part.astype(quarter.dtype)
 
 
 def last_kernel(width, movie, upstream, near, far, mid, grad, one, two, output, movie_grad, patches):
@@ -281,17 +279,6 @@
 
 def swapped(block):
     return lax.ppermute(block, "dp", [(i, i ^ 1) for i in range(lax.axis_size("dp"))])
-
-
-def distances(orders):
-    out = []
-    for groups in orders:
-        dist = [0]
-        for group in reversed(groups):
-            steps = [sum(1 << bit for n, bit in enumerate(group) if q >> n & 1) for q in range(1 << len(group))]
-            dist = [step | low for step in steps for low in dist]
-        out.append(dist)
-    return out
 
 
 def exchanged(send, steps):
@@ -332,8 +319,8 @@
         unplaced=(0, 1),
         limit=53.8,
     )
+    far = paired(far, 1)
     near = paired(near, 0)
-    far = paired(far, 1)
     act_in, pre_part, grad_part = call(
         lambda *refs: inner_kernel(width, *refs),
         [field, part, part],
@@ -346,7 +333,7 @@
         [bundle, bundle, field, field, edge, edge],
         [pltpu.VMEM((halo, cells + 2 * width, TAPS * chans), BF16)],
         conv_flops // 2,
-        near, far, act_in, upstream_r, pre_part, grad_part, kernel_one, kernel_two,
+        far, near, act_in, upstream_r, pre_part, grad_part, kernel_one, kernel_two,
     )
     other = swapped(send)
     near_mid = paired(near_out, 0)
@@ -365,37 +352,32 @@
         pltpu.VMEM((2 * ext, cells + 2 * width, TAPS * chans), BF16),
         pltpu.VMEM((chans, 2 * ext * cells), BF16),
     ]
-    if dp == 2 and tm > 1 and tm & (tm - 1) == 0 and rows % 8 == 0:
-        bits = tm.bit_length() - 1
-        rest = [list(range(low, min(low + 2, bits))) for low in range(2, bits, 2)]
-        orders = ([[0], [1]][:bits] + rest, [[1], [0]][2 - min(bits, 2) :] + rest)
-        kept, sent = call(
-            lambda *refs: relative_sums_kernel(width, distances(orders), *refs),
-            [shape((tm // 2, rows, chans), F32), shape((tm // 2, rows, chans), BF16)],
+    if dp == 2 and tm >= 4 and tm & (tm - 1) == 0 and rows % 8 == 0:
+        size = tm // 4
+        orders = ((1, 2), (2, 1))
+        distance = [
+            [a * first + b * second + 4 * q for a in range(2) for b in range(2) for q in range(size)]
+            for first, second in orders
+        ]
+        wide, narrow = shape((size, rows, chans), F32), shape((size, rows, chans), BF16)
+        stay, pass_on, send_stay, send_on = call(
+            lambda *refs: relative_sums_kernel(width, distance, *refs),
+            [wide, wide, narrow, narrow],
             [pltpu.VMEM((krows, chans), F32)] + scratch,
             2 * conv_flops,
             keep, other,
         )
-        sent, near_mid = lax.optimization_barrier((sent, near_mid))
-        sends = [sent]
-        for stage in range(len(orders[0])):
-            steps = [distances([groups[stage : stage + 1]])[0] for groups in orders]
-            gots = [
-                exchanged(sends[q - 1], (steps[0][q], steps[1][q])) for q in reversed(range(1, len(steps[0])))
-            ]
-            if stage == 0:
-                *gots, far_mid = lax.optimization_barrier((*gots, far_mid))
-            if stage + 1 == len(orders[0]):
-                output, movie_grad = finish(near_mid, far_mid)
-                *gots, output, movie_grad = lax.optimization_barrier((*gots, output, movie_grad))
-            for got in gots:
-                kept = kept + got.astype(F32)
-            if stage + 1 < len(orders[0]):
-                parts = 1 << len(orders[0][stage + 1])
-                size = kept.shape[0] // parts
-                sends = [kept[q * size : (q + 1) * size].astype(BF16) for q in range(1, parts)]
-                kept = kept[:size]
+        send_on, near_mid = lax.optimization_barrier((send_on, near_mid))
+        got_on = exchanged(send_on, (orders[0][0], orders[1][0]))
+        got_stay = exchanged(send_stay, (orders[0][0], orders[1][0]))
+        got = exchanged((pass_on + got_on.astype(F32)).astype(BF16), (orders[0][1], orders[1][1]))
+        kept = stay + got_stay.astype(F32) + got.astype(F32)
+        gots = [exchanged(kept[q].astype(BF16), (4 * q, 4 * q)) for q in reversed(range(1, size))]
+        output, movie_grad = finish(near_mid, far_mid)
+        *gots, output, movie_grad = lax.optimization_barrier((*gots, output, movie_grad))
         mine = kept[0]
+        for got in gots:
+            mine = mine + got.astype(F32)
     else:
         (sums,) = call(
             lambda *refs: plain_sums_kernel(width, *refs),

time: 44.4 us -> 40.9 us (0.921)
  starting transfers between devices: 20.1 us -> 17.7 us
  waiting for transfers between devices: 13.9 us -> 12.9 us
    ppermute x5 -> x6, waiting for transfers between devices: 12 us -> 9.59 us  [exchanged(): return lax.ppermute(send, ('tm', 'dp'), route)]
    ppermute x5 -> x6, starting transfers between devices: 10.9 us -> 8.61 us  [exchanged(): return lax.ppermute(send, ('tm', 'dp'), route)]
    ppermute x4, waiting for transfers between devices: 0.62 us -> 2.02 us  [paired(): return lax.ppermute(block, 'tm', pairs + [(j, i) for i, j in pairs])]
  transfers between devices with their start and end apart: 11 -> 12, of which waited for: 5 -> 7; matrix products, arithmetic and copies ran while one was open for 0% -> 0% of each run, Pallas kernels for 15% -> 16%
where the time goes in v4:
time: 40.9 us; the launch traced here: 40.7 us
  starting transfers between devices  17.7 us (43%)
  waiting for transfers between devices  12.9 us (32%)
  Pallas kernels  8.41 us (21%)
  other arithmetic  0.87 us (2%)
  between operations  0.78 us (2%)
    ppermute x6, waiting for transfers between devices, exchanged(): return lax.ppermute(send, ('tm', 'dp'), route)  9.59 us
    ppermute x4, starting transfers between devices, paired(): return lax.ppermute(block, 'tm', pairs + [(j, i) for i, j in pairs])  8.96 us
    ppermute x6, starting transfers between devices, exchanged(): return lax.ppermute(send, ('tm', 'dp'), route)  8.61 us
    pallas_call x5, Pallas kernels, call(): pl.pallas_call(body, out_shape=outs, in_specs=[anywhere if i in unplaced...  8.41 us
    ppermute x4, waiting for transfers between devices, paired(): return lax.ppermute(block, 'tm', pairs + [(j, i) for i, j in pairs])  2.02 us
    ppermute x2, waiting for transfers between devices, swapped(): lax.ppermute(block, 'dp', [(i, i ^ 1) for i in range(lax.axis_size('dp'))])  1.3 us
  transfers between devices with their start and end apart: 12, of which 7 were waited for; matrix products, arithmetic and copies ran while one was open for 0% of the time, Pallas kernels for 16%

profile of v4, /device:TPU:0, one launch (start us, length us, event | category | flops | bytes accessed | tf_op | source)
XLA Modules:
  0.0 40.7 jit_solution(11519144648395830596)
XLA Ops:
  0.7 1.0 %shard_map.75 = (bf16[2,128,128]{2,1,0:T(8,128)(2,1)S(1)}, bf16[2,128,128]{2,1,0:T(8,128)(2,1)S(1)}) custom-call(bf16[4,128,128]{2,1,0:T(8,128)(2,1)} %bitcast.22, bf16[4,128,128]{2,1,0:T(8,128)(2,1)} %bitcast.18), custom_call_target="tpu_custom_call" | custom-call | flops 8000000000 | bytes 393216 | tf_op jit(solution)/shard_map/pallas_call | solution.py:264
  1.7 0.7 %collective-permute-start = (bf16[2,128,128]{2,1,0:T(8,128)(2,1)S(1)}, bf16[2,128,128]{2,1,0:T(8,128)(2,1)S(1)}, u32[]{:S(2)}, u32[]{:S(2)}) collective-permute-start(bf16[2,128,128]{2,1,0:T(8,128)(2,1)S(1)} %get-tuple-element.28), channel_id=1, source_target_pairs={{2,4},{6,8},{10,12},{14,16},{18,20},{22,24},{26,28},{4,2},{8,6},{1... | collective-permute-start | bytes 196616 | tf_op jit(solution)/shard_map/ppermute | solution.py:277
  2.4 5.7 %collective-permute-start.1 = (bf16[2,128,128]{2,1,0:T(8,128)(2,1)S(1)}, bf16[2,128,128]{2,1,0:T(8,128)(2,1)S(1)}, u32[]{:S(2)}, u32[]{:S(2)}) collective-permute-start(bf16[2,128,128]{2,1,0:T(8,128)(2,1)S(1)} %get-tuple-element.29), channel_id=1, source_target_pairs={{0,2},{4,6},{8,10},{12,14},{16,18},{20,22},{24,26},{28,30},{2,0},{... | collective-permute-start | bytes 196616 | tf_op jit(solution)/shard_map/ppermute | solution.py:277
  8.1 0.0 copy-done
  8.1 1.7 %shard_map.76 = (bf16[4,128,128]{2,1,0:T(8,128)(2,1)S(1)}, f32[512,128]{1,0:T(8,128)S(1)}, f32[512,128]{1,0:T(8,128)S(1)}) custom-call(bf16[4,128,128]{2,1,0:T(8,128)(2,1)S(1)} %bitcast.23, bf16[4,128,128]{2,1,0:T(8,128)(2,1)S(1)} %bitcast.19, bf16[3456,128]{1,0:T(8,128)(2,1)S(1)} %copy-done, bf16[3456,128]{1,0:T(8,128)(2,1)S(1)} %copy-done.1), custom_call_target="tpu_custom_call" | custom-call | flops 679477248 | bytes 2686976 | tf_op jit(solution)/shard_map/pallas_call | solution.py:264
  9.8 0.0 collective-permute-done.refs_0_
  9.8 1.4 %collective-permute-done.1.refs_1_ = bf16[2,128,128]{2,1,0:T(8,128)(2,1)S(1)} collective-permute-done((bf16[2,128,128]{2,1,0:T(8,128)(2,1)S(1)}, bf16[2,128,128]{2,1,0:T(8,128)(2,1)S(1)}, u32[]{:S(2)}, u32[]{:S(2)}) %collective-permute-start.1) | collective-permute-done | bytes 65568 | tf_op jit(solution)/shard_map/ppermute | solution.py:277
  11.3 0.7 %shard_map.77 = (bf16[10,128,128]{2,1,0:T(8,128)(2,1)S(1)}, bf16[10,128,128]{2,1,0:T(8,128)(2,1)S(1)}, bf16[4,128,128]{2,1,0:T(8,128)(2,1)S(1)}, bf16[4,128,128]...) custom-call(bf16[2,128,128]{2,1,0:T(8,128)(2,1)S(1)} %collective-permute-done.refs_0_, ...), custom_call_target="tpu_custom_call" | custom-call | flops 226492416 | bytes 3735552 | tf_op jit(solution)/shard_map/pallas_call | solution.py:264
  12.0 0.1 collective-permute-start.2
  12.1 1.9 %collective-permute-start.4 = (bf16[2,128,128]{2,1,0:T(8,128)(2,1)S(1)}, bf16[2,128,128]{2,1,0:T(8,128)(2,1)S(1)}, u32[]{:S(2)}, u32[]{:S(2)}) collective-permute-start(bf16[2,128,128]{2,1,0:T(8,128)(2,1)S(1)} %get-tuple-element.39), channel_id=1, source_target_pairs={{0,2},{4,6},{8,10},{12,14},{16,18},{20,22},{24,26},{28,30},{2,0},{... | collective-permute-start | bytes 196616 | tf_op jit(solution)/shard_map/ppermute | solution.py:277
  14.0 0.0 collective-permute-done.2.refs_1_
  14.0 2.1 %shard_map.78 = (f32[4,216,128]{2,1,0:T(8,128)S(1)}, f32[4,216,128]{2,1,0:T(8,128)S(1)}, bf16[4,216,128]{2,1,0:T(8,128)(2,1)S(1)}, bf16[4,216,128]{2,1,0:T(8,128)(2,1)S(1)}) custom-call(bf16[10,128,128]{2,1,0:T(8,128)(2,1)S(1)} %get-tuple-element.33.refs_0_, bf16[10,128,128]{2,1,0:T(8,128)(2,1)S(1)} %collective-permute-done.2.refs_1_), custom_call_target="tpu_custom_call" | custom-call | flops 905969664 | bytes 1982464 | tf_op jit(solution)/shard_map/pallas_call | solution.py:264
  16.1 0.6 %collective-permute-done.4.refs_2_ = bf16[2,128,128]{2,1,0:T(8,128)(2,1)S(1)} collective-permute-done((bf16[2,128,128]{2,1,0:T(8,128)(2,1)S(1)}, bf16[2,128,128]{2,1,0:T(8,128)(2,1)S(1)}, u32[]{:S(2)}, u32[]{:S(2)}) %collective-permute-start.4) | collective-permute-done | bytes 65568 | tf_op jit(solution)/shard_map/ppermute | solution.py:277
  16.7 1.8 %collective-permute-start.5 = (bf16[4,216,128]{2,1,0:T(8,128)(2,1)S(1)}, bf16[4,216,128]{2,1,0:T(8,128)(2,1)S(1)}, u32[]{:S(2)}, u32[]{:S(2)}) collective-permute-start(bf16[4,216,128]{2,1,0:T(8,128)(2,1)S(1)} %get-tuple-element.40), channel_id=1, source_target_pairs={{0,2},{1,5},{2,0},{3,7},{4,6},{5,1},{6,4},{7,3},{8,10},{9,13},{10,... | collective-permute-start | bytes 663560 | tf_op jit(solution)/shard_map/ppermute | solution.py:287
  18.4 0.3 collective-permute-start.3
  18.7 3.9 %collective-permute-done.5 = bf16[4,216,128]{2,1,0:T(8,128)(2,1)S(1)} collective-permute-done((bf16[4,216,128]{2,1,0:T(8,128)(2,1)S(1)}, bf16[4,216,128]{2,1,0:T(8,128)(2,1)S(1)}, u32[]{:S(2)}, u32[]{:S(2)}) %collective-permute-start.5) | collective-permute-done | bytes 221216 | tf_op jit(solution)/shard_map/ppermute | solution.py:287
  22.6 1.2 %collective-permute-start.6 = (bf16[4,216,128]{2,1,0:T(8,128)(2,1)S(1)}, bf16[4,216,128]{2,1,0:T(8,128)(2,1)S(1)}, u32[]{:S(2)}, u32[]{:S(2)}) collective-permute-start(bf16[4,216,128]{2,1,0:T(8,128)(2,1)S(1)} %add_convert_fusion), channel_id=1, source_target_pairs={{0,4},{1,3},{2,6},{3,1},{4,0},{5,7},{6,2},{7,5},{8,12},{9,11},{10,... | collective-permute-start | bytes 663560 | tf_op jit(solution)/shard_map/ppermute | solution.py:287
  23.8 0.7 %collective-permute-start.10 = (bf16[2,128,128]{2,1,0:T(8,128)(2,1)S(1)}, bf16[2,128,128]{2,1,0:T(8,128)(2,1)S(1)}, u32[]{:S(2)}, u32[]{:S(2)}) collective-permute-start(bf16[2,128,128]{2,1,0:T(8,128)(2,1)S(1)} %get-tuple-element.42), channel_id=1, source_target_pairs={{2,4},{6,8},{10,12},{14,16},{18,20},{22,24},{26,28},{4,2},{8,6},{1... | collective-permute-start | bytes 196616 | tf_op jit(solution)/shard_map/ppermute | solution.py:277
  24.5 1.2 %collective-permute-done.3 = bf16[4,216,128]{2,1,0:T(8,128)(2,1)S(1)} collective-permute-done((bf16[4,216,128]{2,1,0:T(8,128)(2,1)S(1)}, bf16[4,216,128]{2,1,0:T(8,128)(2,1)S(1)}, u32[]{:S(2)}, u32[]{:S(2)}) %collective-permute-start.3) | collective-permute-done | bytes 221216 | tf_op jit(solution)/shard_map/ppermute | solution.py:287
  25.7 3.0 %collective-permute-done.6 = bf16[4,216,128]{2,1,0:T(8,128)(2,1)S(1)} collective-permute-done((bf16[4,216,128]{2,1,0:T(8,128)(2,1)S(1)}, bf16[4,216,128]{2,1,0:T(8,128)(2,1)S(1)}, u32[]{:S(2)}, u32[]{:S(2)}) %collective-permute-start.6) | collective-permute-done | bytes 221216 | tf_op jit(solution)/shard_map/ppermute | solution.py:287
  28.6 0.1 fusion.3
  28.8 4.8 %collective-permute-start.7 = (bf16[216,128]{1,0:T(8,128)(2,1)S(1)}, bf16[216,128]{1,0:T(8,128)(2,1)S(1)}, u32[]{:S(2)}, u32[]{:S(2)}) collective-permute-start(bf16[216,128]{1,0:T(8,128)(2,1)S(1)} %get-tuple-element.58), channel_id=1, source_target_pairs={{0,24},{1,25},{2,26},{3,27},{4,28},{5,29},{6,30},{7,31},{8,16},{9,... | collective-permute-start | bytes 165896 | tf_op jit(solution)/shard_map/ppermute | solution.py:287
  33.5 0.0 collective-permute-start.8
  33.5 0.6 %collective-permute-start.9 = (bf16[216,128]{1,0:T(8,128)(2,1)S(1)}, bf16[216,128]{1,0:T(8,128)(2,1)S(1)}, u32[]{:S(2)}, u32[]{:S(2)}) collective-permute-start(bf16[216,128]{1,0:T(8,128)(2,1)S(1)} %get-tuple-element.56), channel_id=1, source_target_pairs={{0,8},{1,9},{2,10},{3,11},{4,12},{5,13},{6,14},{7,15},{8,0},{9,1},... | collective-permute-start | bytes 165896 | tf_op jit(solution)/shard_map/ppermute | solution.py:287
  34.2 0.0 collective-permute-done.10.refs_3_
  34.2 2.9 %shard_map.79 = (bf16[4,128,128]{2,1,0:T(8,128)(2,1)}, bf16[4,128,128]{2,1,0:T(8,128)(2,1)}) custom-call(bf16[4,128,128]{2,1,0:T(8,128)(2,1)S(1)} %bitcast.24, bf16[4,128,128]{2,1,0:T(8,128)(2,1)S(1)} %bitcast.21, bf16[2,128,128]{2,1,0:T(8,128)(2,1)S(1)} %collective-permute-done.4.refs_2_, bf16[2,128,128]{2,1,0:T(8,128)(2,1)S(1)} %collective-permute-done.10.refs_3_, ...), custom_call_target="tpu_custom_call" | custom-call | flops 905969664 | bytes 2686976 | tf_op jit(solution)/shard_map/pallas_call | solution.py:264
  37.1 0.0 collective-permute-done.7
  37.1 1.5 %collective-permute-done.8 = bf16[216,128]{1,0:T(8,128)(2,1)S(1)} collective-permute-done((bf16[216,128]{1,0:T(8,128)(2,1)S(1)}, bf16[216,128]{1,0:T(8,128)(2,1)S(1)}, u32[]{:S(2)}, u32[]{:S(2)}) %collective-permute-start.8) | collective-permute-done | bytes 55328 | tf_op jit(solution)/shard_map/ppermute | solution.py:287
  38.6 0.0 collective-permute-done.9
  38.6 0.1 collective-permute-start.11
  38.7 1.3 %collective-permute-done.11 = f32[216,128]{1,0:T(8,128)S(1)} collective-permute-done((f32[216,128]{1,0:T(8,128)S(1)}, f32[216,128]{1,0:T(8,128)S(1)}, u32[]{:S(2)}, u32[]{:S(2)}) %collective-permute-start.11) | collective-permute-done | bytes 110624 | tf_op jit(solution)/shard_map/ppermute | solution.py:281
  40.0 0.7 %broadcast_select_fusion = (f32[216,128]{1,0:T(8,128)}, f32[216,128]{1,0:T(8,128)}) fusion(f32[216,128]{1,0:T(8,128)S(1)} %collective-permute-done.11, f32[216,128]{1,0:T(8,128)S(1)} %fusion.2, pred[]{:T(512)S(6)} %eq.5), kind=kLoop, calls=%fused_computation.9 | loop fusion | flops 55296 | bytes 442369 | tf_op jit(solution)/shard_map/jit(_where)/select_n | solution.py:397
  (10 shorter events, 0.1 us)
Async XLA Ops:
  0.6 7.5 %copy-start = (bf16[3456,128]{1,0:T(8,128)(2,1)S(1)}, bf16[3456,128]{1,0:T(8,128)(2,1)}, u32[]{:S(2)}) copy-start(bf16[3456,128]{1,0:T(8,128)(2,1)} %refs_6_.3) | copy-start | bytes 2654212
  0.6 7.5 %copy-start.1 = (bf16[3456,128]{1,0:T(8,128)(2,1)S(1)}, bf16[3456,128]{1,0:T(8,128)(2,1)}, u32[]{:S(2)}) copy-start(bf16[3456,128]{1,0:T(8,128)(2,1)} %refs_7_.3) | copy-start | bytes 2654212
  0.7 7.5 %copy-start.2 = (bf16[1,4,8,16,128]{4,3,2,1,0:T(8,128)(2,1)S(1)}, bf16[1,4,8,16,128]{4,3,2,1,0:T(8,128)(2,1)}, u32[]{:S(2)}) copy-start(bf16[1,4,8,16,128]{4,3,2,1,0:T(8,128)(2,1)} %param.7) | copy-start | bytes 393220
  0.7 7.5 %copy-start.3 = (bf16[1,4,8,16,128]{4,3,2,1,0:T(8,128)(2,1)S(1)}, bf16[1,4,8,16,128]{4,3,2,1,0:T(8,128)(2,1)}, u32[]{:S(2)}) copy-start(bf16[1,4,8,16,128]{4,3,2,1,0:T(8,128)(2,1)} %param.4) | copy-start | bytes 393220
  1.7 8.1 %collective-permute-start = (bf16[2,128,128]{2,1,0:T(8,128)(2,1)S(1)}, bf16[2,128,128]{2,1,0:T(8,128)(2,1)S(1)}, u32[]{:S(2)}, u32[]{:S(2)}) collective-permute-start(bf16[2,128,128]{2,1,0:T(8,128)(2,1)S(1)} %get-tuple-element.28), channel_id=1, source_target_pairs={{2,4},{6,8},{10,12},{14,16},{18,20},{22,24},{26,28},{4,2},{8,6},{1... | collective-permute-start | bytes 196616 | tf_op jit(solution)/shard_map/ppermute | solution.py:277
  2.4 8.9 %collective-permute-start.1 = (bf16[2,128,128]{2,1,0:T(8,128)(2,1)S(1)}, bf16[2,128,128]{2,1,0:T(8,128)(2,1)S(1)}, u32[]{:S(2)}, u32[]{:S(2)}) collective-permute-start(bf16[2,128,128]{2,1,0:T(8,128)(2,1)S(1)} %get-tuple-element.29), channel_id=1, source_target_pairs={{0,2},{4,6},{8,10},{12,14},{16,18},{20,22},{24,26},{28,30},{2,0},{... | collective-permute-start | bytes 196616 | tf_op jit(solution)/shard_map/ppermute | solution.py:277
  12.0 2.0 %collective-permute-start.2 = (bf16[10,128,128]{2,1,0:T(8,128)(2,1)S(1)}, bf16[10,128,128]{2,1,0:T(8,128)(2,1)S(1)}, u32[]{:S(2)}, u32[]{:S(2)}) collective-permute-start(bf16[10,128,128]{2,1,0:T(8,128)(2,1)S(1)} %get-tuple-element.34), channel_id=1, source_target_pairs={{0,1},{1,0},{2,3},{3,2},{4,5},{5,4},{6,7},{7,6},{8,9},{9,8},{10,11... | collective-permute-start | bytes 983048 | tf_op jit(solution)/shard_map/ppermute | solution.py:281
  12.1 4.6 %collective-permute-start.4 = (bf16[2,128,128]{2,1,0:T(8,128)(2,1)S(1)}, bf16[2,128,128]{2,1,0:T(8,128)(2,1)S(1)}, u32[]{:S(2)}, u32[]{:S(2)}) collective-permute-start(bf16[2,128,128]{2,1,0:T(8,128)(2,1)S(1)} %get-tuple-element.39), channel_id=1, source_target_pairs={{0,2},{4,6},{8,10},{12,14},{16,18},{20,22},{24,26},{28,30},{2,0},{... | collective-permute-start | bytes 196616 | tf_op jit(solution)/shard_map/ppermute | solution.py:277
  16.7 5.9 %collective-permute-start.5 = (bf16[4,216,128]{2,1,0:T(8,128)(2,1)S(1)}, bf16[4,216,128]{2,1,0:T(8,128)(2,1)S(1)}, u32[]{:S(2)}, u32[]{:S(2)}) collective-permute-start(bf16[4,216,128]{2,1,0:T(8,128)(2,1)S(1)} %get-tuple-element.40), channel_id=1, source_target_pairs={{0,2},{1,5},{2,0},{3,7},{4,6},{5,1},{6,4},{7,3},{8,10},{9,13},{10,... | collective-permute-start | bytes 663560 | tf_op jit(solution)/shard_map/ppermute | solution.py:287
  18.4 7.2 %collective-permute-start.3 = (bf16[4,216,128]{2,1,0:T(8,128)(2,1)S(1)}, bf16[4,216,128]{2,1,0:T(8,128)(2,1)S(1)}, u32[]{:S(2)}, u32[]{:S(2)}) collective-permute-start(bf16[4,216,128]{2,1,0:T(8,128)(2,1)S(1)} %get-tuple-element.36), channel_id=1, source_target_pairs={{0,2},{1,5},{2,0},{3,7},{4,6},{5,1},{6,4},{7,3},{8,10},{9,13},{10,... | collective-permute-start | bytes 663560 | tf_op jit(solution)/shard_map/ppermute | solution.py:287
  22.6 6.0 %collective-permute-start.6 = (bf16[4,216,128]{2,1,0:T(8,128)(2,1)S(1)}, bf16[4,216,128]{2,1,0:T(8,128)(2,1)S(1)}, u32[]{:S(2)}, u32[]{:S(2)}) collective-permute-start(bf16[4,216,128]{2,1,0:T(8,128)(2,1)S(1)} %add_convert_fusion), channel_id=1, source_target_pairs={{0,4},{1,3},{2,6},{3,1},{4,0},{5,7},{6,2},{7,5},{8,12},{9,11},{10,... | collective-permute-start | bytes 663560 | tf_op jit(solution)/shard_map/ppermute | solution.py:287
  23.8 10.4 %collective-permute-start.10 = (bf16[2,128,128]{2,1,0:T(8,128)(2,1)S(1)}, bf16[2,128,128]{2,1,0:T(8,128)(2,1)S(1)}, u32[]{:S(2)}, u32[]{:S(2)}) collective-permute-start(bf16[2,128,128]{2,1,0:T(8,128)(2,1)S(1)} %get-tuple-element.42), channel_id=1, source_target_pairs={{2,4},{6,8},{10,12},{14,16},{18,20},{22,24},{26,28},{4,2},{8,6},{1... | collective-permute-start | bytes 196616 | tf_op jit(solution)/shard_map/ppermute | solution.py:277
  28.8 8.3 %collective-permute-start.7 = (bf16[216,128]{1,0:T(8,128)(2,1)S(1)}, bf16[216,128]{1,0:T(8,128)(2,1)S(1)}, u32[]{:S(2)}, u32[]{:S(2)}) collective-permute-start(bf16[216,128]{1,0:T(8,128)(2,1)S(1)} %get-tuple-element.58), channel_id=1, source_target_pairs={{0,24},{1,25},{2,26},{3,27},{4,28},{5,29},{6,30},{7,31},{8,16},{9,... | collective-permute-start | bytes 165896 | tf_op jit(solution)/shard_map/ppermute | solution.py:287
  33.5 5.1 %collective-permute-start.8 = (bf16[216,128]{1,0:T(8,128)(2,1)S(1)}, bf16[216,128]{1,0:T(8,128)(2,1)S(1)}, u32[]{:S(2)}, u32[]{:S(2)}) collective-permute-start(bf16[216,128]{1,0:T(8,128)(2,1)S(1)} %get-tuple-element.57), channel_id=1, source_target_pairs={{0,16},{1,17},{2,18},{3,19},{4,20},{5,21},{6,22},{7,23},{8,24},{9,... | collective-permute-start | bytes 165896 | tf_op jit(solution)/shard_map/ppermute | solution.py:287
  33.5 5.1 %collective-permute-start.9 = (bf16[216,128]{1,0:T(8,128)(2,1)S(1)}, bf16[216,128]{1,0:T(8,128)(2,1)S(1)}, u32[]{:S(2)}, u32[]{:S(2)}) collective-permute-start(bf16[216,128]{1,0:T(8,128)(2,1)S(1)} %get-tuple-element.56), channel_id=1, source_target_pairs={{0,8},{1,9},{2,10},{3,11},{4,12},{5,13},{6,14},{7,15},{8,0},{9,1},... | collective-permute-start | bytes 165896 | tf_op jit(solution)/shard_map/ppermute | solution.py:287
  38.6 1.4 %collective-permute-start.11 = (f32[216,128]{1,0:T(8,128)S(1)}, f32[216,128]{1,0:T(8,128)S(1)}, u32[]{:S(2)}, u32[]{:S(2)}) collective-permute-start(f32[216,128]{1,0:T(8,128)S(1)} %fusion.2), channel_id=1, source_target_pairs={{0,1},{1,0},{2,3},{3,2},{4,5},{5,4},{6,7},{7,6},{8,9},{9,8},{10,11... | collective-permute-start | bytes 331784 | tf_op jit(solution)/shard_map/ppermute | solution.py:281

commit v5 on v4

--- a/solution.py
+++ b/solution.py
@@ -32,37 +32,6 @@
     patches[pl.ds(first, frames), width + cells :, :] = edge
 
 
-def conv_forward(patches, kernel, frames, cells, width):
-    chans = kernel.shape[1]
-    left = jnp.concatenate(
-        [
-            patches[kt : kt + frames, ki * width : ki * width + cells, :].reshape(frames * cells, TAPS * chans)
-            for kt in range(TAPS)
-            for ki in range(TAPS)
-        ],
-        axis=1,
-    )
-    return jnp.dot(left, kernel[...], preferred_element_type=F32)
-
-
-def conv_backward(patches, kernel, frames, cells, width):
-    chans = kernel.shape[1]
-    left = jnp.concatenate(
-        [
-            patches[
-                TAPS - 1 - kt : TAPS - 1 - kt + frames,
-                (TAPS - 1 - ki) * width : (TAPS - 1 - ki) * width + cells,
-                :,
-            ].reshape(frames * cells, TAPS * chans)
-            for kt in range(TAPS)
-            for ki in range(TAPS)
-        ],
-        axis=1,
-    )
-    right = jnp.concatenate([kernel[tap * chans : (tap + 1) * chans, :] for tap in range(TAPS**3)], axis=1)
-    return lax.dot_general(left, right, (((1,), (1,)), ((), ())), preferred_element_type=F32)
-
-
 def taps_forward(patches, kernel, kt, first, count, cells, width):
     chans = kernel.shape[1]
     left = jnp.concatenate(
@@ -121,21 +90,50 @@
     return jnp.where(even, far[...], near[...]), jnp.where(even, near[...], far[...])
 
 
-def inner_kernel(
-    width, movie, upstream, one, two, act_in, pre_part, grad_part, act_patches, up_patches
-):
-    frames, cells, chans = movie.shape
+def own_forward(patches, kernel, out, frames, cells, width):
+    out[...] = taps_forward(patches, kernel, TAPS - 1, 0, frames, cells, width)
+    for lag in range(1, TAPS):
+        out[lag * cells :, :] += taps_forward(patches, kernel, TAPS - 1 - lag, 0, frames - lag, cells, width)
+
+
+def own_backward(patches, kernel, out, frames, cells, width):
+    out[...] = taps_backward(patches, kernel, TAPS - 1, 0, frames, cells, width)
+    for lag in range(1, TAPS):
+        part = taps_backward(patches, kernel, TAPS - 1 - lag, lag, frames - lag, cells, width)
+        out[: (frames - lag) * cells, :] += part
+
+
+def with_before(width, part, patches, kernel, before):
+    _, cells, chans = before.shape
+    fill(patches, 0, before, width, False)
+    sums = [part[row : row + cells, :] for row in range(0, part.shape[0], cells)]
+    for kt in range(TAPS - 1):
+        count = TAPS - 1 - kt
+        more = taps_forward(patches, kernel, kt, kt, count, cells, width)
+        for n in range(count):
+            sums[n] = sums[n] + more[n * cells : (n + 1) * cells]
+    return jnp.concatenate(sums, axis=0)
+
+
+def with_after(width, part, patches, kernel, after):
+    _, cells, chans = after.shape
+    fill(patches, 0, after, width, True)
+    sums = [part[row : row + cells, :] for row in range(0, part.shape[0], cells)]
+    for kt in range(TAPS - 1):
+        count = TAPS - 1 - kt
+        more = taps_backward(patches, kernel, kt, 0, count, cells, width)
+        for n in range(count):
+            sums[n - count] = sums[n - count] + more[n * cells : (n + 1) * cells]
+    return jnp.concatenate(sums, axis=0)
+
+
+def inner_kernel(width, movie, upstream, one, two, act_in, pre_part, grad_part, act_patches, up_patches):
+    frames, cells, _ = movie.shape
     act_in[...] = jax.nn.silu(movie[...].astype(F32)).astype(BF16)
     fill(act_patches, 0, act_in[...], width, False)
+    own_forward(act_patches, one, pre_part, frames, cells, width)
     fill(up_patches, 0, upstream[...], width, True)
-    pre_part[...] = taps_forward(act_patches, one, TAPS - 1, 0, frames, cells, width)
-    for lag in range(1, TAPS):
-        part = taps_forward(act_patches, one, TAPS - 1 - lag, 0, frames - lag, cells, width)
-        pre_part[lag * cells :, :] += part
-    grad_part[...] = taps_backward(up_patches, two, TAPS - 1, 0, frames, cells, width)
-    for lag in range(1, TAPS):
-        part = taps_backward(up_patches, two, TAPS - 1 - lag, lag, frames - lag, cells, width)
-        grad_part[: (frames - lag) * cells, :] += part
+    own_backward(up_patches, two, grad_part, frames, cells, width)
 
 
 def outer_kernel(
@@ -145,23 +143,10 @@
     halo = TAPS - 1
     before, after = sorted_edges(near, far)
     act_before = jax.nn.silu(before.astype(F32)).astype(BF16)
-    fill(patches, 0, act_before, width, False)
-    pres = [pre_part[t * cells : (t + 1) * cells, :] for t in range(frames)]
-    for kt in range(halo):
-        part = taps_forward(patches, one, kt, kt, halo - kt, cells, width)
-        for t in range(halo - kt):
-            pres[t] = pres[t] + part[t * cells : (t + 1) * cells]
-    pre = jnp.concatenate(pres, axis=0)
+    pre = with_before(width, pre_part, patches, one, act_before)
     act_mid = jax.nn.silu(pre).astype(BF16).reshape(frames, cells, chans)
     mid[...] = act_mid
-    fill(patches, 0, after, width, True)
-    grads = [grad_part[t * cells : (t + 1) * cells, :] for t in range(frames)]
-    for kt in range(halo):
-        part = taps_backward(patches, two, kt, 0, halo - kt, cells, width)
-        for n in range(halo - kt):
-            t = frames - (halo - kt) + n
-            grads[t] = grads[t] + part[n * cells : (n + 1) * cells]
-    mid_grad = jnp.concatenate(grads, axis=0)
+    mid_grad = with_after(width, grad_part, patches, two, after)
     pre_grad = (mid_grad * silu_grad(pre)).astype(BF16).reshape(frames, cells, chans)
     grad[...] = pre_grad
     even = lax.axis_index("tm") % 2 == 0
@@ -200,7 +185,7 @@
         for n in range(ext):
             block = source[(1 - odd) * frames + n]
             place = (clip * ext + n) * cells
-            turned[:, place : place + cells] = block.astype(F32).T.astype(BF16)
+            turned[:, place : place + cells] = block.T
     for kt in range(TAPS):
         l_start = (1 - odd) * kt
         r_start = odd * (halo - kt)
@@ -245,15 +230,21 @@
             quarter[r] = part.astype(quarter.dtype)
 
 
-def last_kernel(width, movie, upstream, near, far, mid, grad, one, two, output, movie_grad, patches):
-    frames, cells, chans = movie.shape
+def middle_kernel(width, mid, grad, one, two, out_part, in_part, mid_patches, grad_patches):
+    frames, cells, _ = mid.shape
+    fill(mid_patches, 0, mid[...], width, False)
+    own_forward(mid_patches, two, out_part, frames, cells, width)
+    fill(grad_patches, 0, grad[...], width, True)
+    own_backward(grad_patches, one, in_part, frames, cells, width)
+
+
+def last_kernel(width, movie, upstream, near, far, out_part, in_part, one, two, output, movie_grad, patches):
+    shape = movie.shape
     mid_before, grad_after = sorted_edges(near, far)
-    fill(patches, 0, jnp.concatenate([mid_before, mid[...]], axis=0), width, False)
-    out = conv_forward(patches, two, frames, cells, width).reshape(frames, cells, chans)
     movie_f = movie[...].astype(F32)
+    out = with_before(width, out_part, patches, two, mid_before).reshape(shape)
     output[...] = (movie_f + out).astype(BF16)
-    fill(patches, 0, jnp.concatenate([grad[...], grad_after], axis=0), width, True)
-    in_grad = conv_backward(patches, one, frames, cells, width).reshape(frames, cells, chans)
+    in_grad = with_after(width, in_part, patches, one, grad_after).reshape(shape)
     movie_grad[...] = (upstream[...].astype(F32) + in_grad * silu_grad(movie_f)).astype(BF16)
 
 
@@ -302,7 +293,6 @@
     movie_r = movie.reshape(flat)
     upstream_r = upstream.reshape(flat)
     conv_flops = 2 * frames * cells * krows * chans
-    patch = pltpu.VMEM((ext, cells + 2 * width, TAPS * chans), BF16)
 
     bundle = shape((frames + ext, cells, chans), BF16)
     field = shape(flat, BF16)
@@ -339,13 +329,24 @@
     near_mid = paired(near_out, 0)
     far_mid = paired(far_out, 1)
 
-    def finish(near_mid, far_mid):
+    edge_patch = pltpu.VMEM((halo, cells + 2 * width, TAPS * chans), BF16)
+
+    def middle(mid, grad):
+        return call(
+            lambda *refs: middle_kernel(width, *refs),
+            [part, part],
+            [pltpu.VMEM(own_patch.shape, BF16)] * 2,
+            3 * conv_flops // 2,
+            mid, grad, kernel_one, kernel_two,
+        )
+
+    def finish(near_mid, far_mid, out_part, in_part):
         return call(
             lambda *refs: last_kernel(width, *refs),
             [field, field],
-            [patch],
-            2 * conv_flops,
-            movie_r, upstream_r, near_mid, far_mid, mid, grad, kernel_one, kernel_two,
+            [edge_patch],
+            conv_flops // 2,
+            movie_r, upstream_r, near_mid, far_mid, out_part, in_part, kernel_one, kernel_two,
         )
 
     scratch = [
@@ -367,13 +368,15 @@
             2 * conv_flops,
             keep, other,
         )
-        send_on, near_mid = lax.optimization_barrier((send_on, near_mid))
+        send_on, near_mid, mid, grad = lax.optimization_barrier((send_on, near_mid, mid, grad))
+        parts = middle(mid, grad)
         got_on = exchanged(send_on, (orders[0][0], orders[1][0]))
         got_stay = exchanged(send_stay, (orders[0][0], orders[1][0]))
+        got_on, *parts = lax.optimization_barrier((got_on, *parts))
         got = exchanged((pass_on + got_on.astype(F32)).astype(BF16), (orders[0][1], orders[1][1]))
         kept = stay + got_stay.astype(F32) + got.astype(F32)
-        gots = [exchanged(kept[q].astype(BF16), (4 * q, 4 * q)) for q in reversed(range(1, size))]
-        output, movie_grad = finish(near_mid, far_mid)
+        gots = [exchanged(kept[q].astype(BF16), (4 * q, 4 * q)) for q in (2, 3, 1)]
+        output, movie_grad = finish(near_mid, far_mid, *parts)
         *gots, output, movie_grad = lax.optimization_barrier((*gots, output, movie_grad))
         mine = kept[0]
         for got in gots:
@@ -386,7 +389,7 @@
             2 * conv_flops,
             keep, other,
         )
-        output, movie_grad = finish(near_mid, far_mid)
+        output, movie_grad = finish(near_mid, far_mid, *middle(mid, grad))
         mine = lax.psum_scatter(sums, "tm", scatter_dimension=0, tiled=True)
         if dp > 2:
             groups = [[d for d in range(dp) if d % 2 == parity] for parity in range(2)]

time: 40.9 us -> 40.7 us (level)
    pallas_call x5 -> x6, Pallas kernels: 8.41 us -> 8.39 us  [call(): pl.pallas_call(body, out_shape=outs, in_specs=[anywhere if i in unplaced...]
  transfers between devices with their start and end apart: 12 -> 12, of which waited for: 7 -> 8; matrix products, arithmetic and copies ran while one was open for 0% -> 0% of each run, Pallas kernels for 16% -> 16%
where the time goes in v5:
time: 40.7 us; the launch traced here: 40.5 us
  starting transfers between devices  17.6 us (43%)
  waiting for transfers between devices  12.8 us (31%)
  Pallas kernels  8.39 us (21%)
  other arithmetic  0.87 us (2%)
  between operations  0.78 us (2%)
    ppermute x6, waiting for transfers between devices, exchanged(): return lax.ppermute(send, ('tm', 'dp'), route)  9.4 us
    ppermute x4, starting transfers between devices, paired(): return lax.ppermute(block, 'tm', pairs + [(j, i) for i, j in pairs])  8.96 us
    ppermute x6, starting transfers between devices, exchanged(): return lax.ppermute(send, ('tm', 'dp'), route)  8.54 us
    pallas_call x6, Pallas kernels, call(): pl.pallas_call(body, out_shape=outs, in_specs=[anywhere if i in unplaced...  8.39 us
    ppermute x4, waiting for transfers between devices, paired(): return lax.ppermute(block, 'tm', pairs + [(j, i) for i, j in pairs])  2.08 us
    ppermute x2, waiting for transfers between devices, swapped(): lax.ppermute(block, 'dp', [(i, i ^ 1) for i in range(lax.axis_size('dp'))])  1.3 us
  transfers between devices with their start and end apart: 12, of which 8 were waited for; matrix products, arithmetic and copies ran while one was open for 0% of the time, Pallas kernels for 16%

profile of v5, /device:TPU:0, one launch (start us, length us, event | category | flops | bytes accessed | tf_op | source)
XLA Modules:
  0.0 40.5 jit_solution(13050653409330269955)
XLA Ops:
  0.7 1.0 %shard_map.75 = (bf16[2,128,128]{2,1,0:T(8,128)(2,1)S(1)}, bf16[2,128,128]{2,1,0:T(8,128)(2,1)S(1)}) custom-call(bf16[4,128,128]{2,1,0:T(8,128)(2,1)} %bitcast.22, bf16[4,128,128]{2,1,0:T(8,128)(2,1)} %bitcast.18), custom_call_target="tpu_custom_call" | custom-call | flops 8000000000 | bytes 393216 | tf_op jit(solution)/shard_map/pallas_call | solution.py:255
  1.7 0.7 %collective-permute-start = (bf16[2,128,128]{2,1,0:T(8,128)(2,1)S(1)}, bf16[2,128,128]{2,1,0:T(8,128)(2,1)S(1)}, u32[]{:S(2)}, u32[]{:S(2)}) collective-permute-start(bf16[2,128,128]{2,1,0:T(8,128)(2,1)S(1)} %get-tuple-element.35), channel_id=1, source_target_pairs={{2,4},{6,8},{10,12},{14,16},{18,20},{22,24},{26,28},{4,2},{8,6},{1... | collective-permute-start | bytes 196616 | tf_op jit(solution)/shard_map/ppermute | solution.py:268
  2.4 5.7 %collective-permute-start.1 = (bf16[2,128,128]{2,1,0:T(8,128)(2,1)S(1)}, bf16[2,128,128]{2,1,0:T(8,128)(2,1)S(1)}, u32[]{:S(2)}, u32[]{:S(2)}) collective-permute-start(bf16[2,128,128]{2,1,0:T(8,128)(2,1)S(1)} %get-tuple-element.36), channel_id=1, source_target_pairs={{0,2},{4,6},{8,10},{12,14},{16,18},{20,22},{24,26},{28,30},{2,0},{... | collective-permute-start | bytes 196616 | tf_op jit(solution)/shard_map/ppermute | solution.py:268
  8.1 1.7 %shard_map.76 = (bf16[4,128,128]{2,1,0:T(8,128)(2,1)S(1)}, f32[512,128]{1,0:T(8,128)S(1)}, f32[512,128]{1,0:T(8,128)S(1)}) custom-call(bf16[4,128,128]{2,1,0:T(8,128)(2,1)S(1)} %bitcast.23, bf16[4,128,128]{2,1,0:T(8,128)(2,1)S(1)} %bitcast.19, bf16[3456,128]{1,0:T(8,128)(2,1)S(1)} %copy-done, bf16[3456,128]{1,0:T(8,128)(2,1)S(1)} %copy-done.1), custom_call_target="tpu_custom_call" | custom-call | flops 679477248 | bytes 2686976 | tf_op jit(solution)/shard_map/pallas_call | solution.py:255
  9.8 0.0 collective-permute-done.refs_0_
  9.8 1.4 %collective-permute-done.1.refs_1_ = bf16[2,128,128]{2,1,0:T(8,128)(2,1)S(1)} collective-permute-done((bf16[2,128,128]{2,1,0:T(8,128)(2,1)S(1)}, bf16[2,128,128]{2,1,0:T(8,128)(2,1)S(1)}, u32[]{:S(2)}, u32[]{:S(2)}) %collective-permute-start.1) | collective-permute-done | bytes 65568 | tf_op jit(solution)/shard_map/ppermute | solution.py:268
  11.3 0.7 %shard_map.77 = (bf16[10,128,128]{2,1,0:T(8,128)(2,1)S(1)}, bf16[10,128,128]{2,1,0:T(8,128)(2,1)S(1)}, bf16[4,128,128]{2,1,0:T(8,128)(2,1)S(1)}, bf16[4,128,128]...) custom-call(bf16[2,128,128]{2,1,0:T(8,128)(2,1)S(1)} %collective-permute-done.refs_0_, ...), custom_call_target="tpu_custom_call" | custom-call | flops 226492416 | bytes 3735552 | tf_op jit(solution)/shard_map/pallas_call | solution.py:255
  12.0 0.1 collective-permute-start.2
  12.1 1.9 %collective-permute-start.4 = (bf16[2,128,128]{2,1,0:T(8,128)(2,1)S(1)}, bf16[2,128,128]{2,1,0:T(8,128)(2,1)S(1)}, u32[]{:S(2)}, u32[]{:S(2)}) collective-permute-start(bf16[2,128,128]{2,1,0:T(8,128)(2,1)S(1)} %get-tuple-element.46), channel_id=1, source_target_pairs={{0,2},{4,6},{8,10},{12,14},{16,18},{20,22},{24,26},{28,30},{2,0},{... | collective-permute-start | bytes 196616 | tf_op jit(solution)/shard_map/ppermute | solution.py:268
  14.0 0.0 collective-permute-done.2.refs_1_
  14.0 2.0 %shard_map.78 = (f32[4,216,128]{2,1,0:T(8,128)S(1)}, f32[4,216,128]{2,1,0:T(8,128)S(1)}, bf16[4,216,128]{2,1,0:T(8,128)(2,1)S(1)}, bf16[4,216,128]{2,1,0:T(8,128)(2,1)S(1)}) custom-call(bf16[10,128,128]{2,1,0:T(8,128)(2,1)S(1)} %get-tuple-element.40.refs_0_, bf16[10,128,128]{2,1,0:T(8,128)(2,1)S(1)} %collective-permute-done.2.refs_1_), custom_call_target="tpu_custom_call" | custom-call | flops 905969664 | bytes 1982464 | tf_op jit(solution)/shard_map/pallas_call | solution.py:255
  16.0 0.7 %collective-permute-done.4.refs_2_ = bf16[2,128,128]{2,1,0:T(8,128)(2,1)S(1)} collective-permute-done((bf16[2,128,128]{2,1,0:T(8,128)(2,1)S(1)}, bf16[2,128,128]{2,1,0:T(8,128)(2,1)S(1)}, u32[]{:S(2)}, u32[]{:S(2)}) %collective-permute-start.4) | collective-permute-done | bytes 65568 | tf_op jit(solution)/shard_map/ppermute | solution.py:268
  16.7 1.8 %collective-permute-start.5 = (bf16[4,216,128]{2,1,0:T(8,128)(2,1)S(1)}, bf16[4,216,128]{2,1,0:T(8,128)(2,1)S(1)}, u32[]{:S(2)}, u32[]{:S(2)}) collective-permute-start(bf16[4,216,128]{2,1,0:T(8,128)(2,1)S(1)} %get-tuple-element.49), channel_id=1, source_target_pairs={{0,2},{1,5},{2,0},{3,7},{4,6},{5,1},{6,4},{7,3},{8,10},{9,13},{10,... | collective-permute-start | bytes 663560 | tf_op jit(solution)/shard_map/ppermute | solution.py:278
  18.4 0.3 collective-permute-start.3
  18.7 1.6 %shard_map.79 = (f32[512,128]{1,0:T(8,128)S(1)}, f32[512,128]{1,0:T(8,128)S(1)}) custom-call(bf16[4,128,128]{2,1,0:T(8,128)(2,1)S(1)} %get-tuple-element.50.refs_0_, bf16[4,128,128]{2,1,0:T(8,128)(2,1)S(1)} %get-tuple-element.51.refs_1_, bf16[3456,128]{1,0:T(8,128)(2,1)S(1)} %copy-done, bf16[3456,128]{1,0:T(8,128)(2,1)S(1)} %copy-done.1), custom_call_target="tpu_custom_call" | custom-call | flops 679477248 | bytes 2555904 | tf_op jit(solution)/shard_map/pallas_call | solution.py:255
  20.3 2.3 %collective-permute-done.5 = bf16[4,216,128]{2,1,0:T(8,128)(2,1)S(1)} collective-permute-done((bf16[4,216,128]{2,1,0:T(8,128)(2,1)S(1)}, bf16[4,216,128]{2,1,0:T(8,128)(2,1)S(1)}, u32[]{:S(2)}, u32[]{:S(2)}) %collective-permute-start.5) | collective-permute-done | bytes 221216 | tf_op jit(solution)/shard_map/ppermute | solution.py:278
  22.6 1.2 %collective-permute-start.6 = (bf16[4,216,128]{2,1,0:T(8,128)(2,1)S(1)}, bf16[4,216,128]{2,1,0:T(8,128)(2,1)S(1)}, u32[]{:S(2)}, u32[]{:S(2)}) collective-permute-start(bf16[4,216,128]{2,1,0:T(8,128)(2,1)S(1)} %add_convert_fusion), channel_id=1, source_target_pairs={{0,4},{1,3},{2,6},{3,1},{4,0},{5,7},{6,2},{7,5},{8,12},{9,11},{10,... | collective-permute-start | bytes 663560 | tf_op jit(solution)/shard_map/ppermute | solution.py:278
  23.8 0.7 %collective-permute-start.10 = (bf16[2,128,128]{2,1,0:T(8,128)(2,1)S(1)}, bf16[2,128,128]{2,1,0:T(8,128)(2,1)S(1)}, u32[]{:S(2)}, u32[]{:S(2)}) collective-permute-start(bf16[2,128,128]{2,1,0:T(8,128)(2,1)S(1)} %get-tuple-element.56), channel_id=1, source_target_pairs={{2,4},{6,8},{10,12},{14,16},{18,20},{22,24},{26,28},{4,2},{8,6},{1... | collective-permute-start | bytes 196616 | tf_op jit(solution)/shard_map/ppermute | solution.py:268
  24.5 1.2 %collective-permute-done.3 = bf16[4,216,128]{2,1,0:T(8,128)(2,1)S(1)} collective-permute-done((bf16[4,216,128]{2,1,0:T(8,128)(2,1)S(1)}, bf16[4,216,128]{2,1,0:T(8,128)(2,1)S(1)}, u32[]{:S(2)}, u32[]{:S(2)}) %collective-permute-start.3) | collective-permute-done | bytes 221216 | tf_op jit(solution)/shard_map/ppermute | solution.py:278
  25.7 3.0 %collective-permute-done.6 = bf16[4,216,128]{2,1,0:T(8,128)(2,1)S(1)} collective-permute-done((bf16[4,216,128]{2,1,0:T(8,128)(2,1)S(1)}, bf16[4,216,128]{2,1,0:T(8,128)(2,1)S(1)}, u32[]{:S(2)}, u32[]{:S(2)}) %collective-permute-start.6) | collective-permute-done | bytes 221216 | tf_op jit(solution)/shard_map/ppermute | solution.py:278
  28.6 0.1 fusion.3
  28.8 3.1 %collective-permute-start.7 = (bf16[216,128]{1,0:T(8,128)(2,1)S(1)}, bf16[216,128]{1,0:T(8,128)(2,1)S(1)}, u32[]{:S(2)}, u32[]{:S(2)}) collective-permute-start(bf16[216,128]{1,0:T(8,128)(2,1)S(1)} %get-tuple-element.72), channel_id=1, source_target_pairs={{0,16},{1,17},{2,18},{3,19},{4,20},{5,21},{6,22},{7,23},{8,24},{9,... | collective-permute-start | bytes 165896 | tf_op jit(solution)/shard_map/ppermute | solution.py:278
  31.8 1.8 %collective-permute-start.8 = (bf16[216,128]{1,0:T(8,128)(2,1)S(1)}, bf16[216,128]{1,0:T(8,128)(2,1)S(1)}, u32[]{:S(2)}, u32[]{:S(2)}) collective-permute-start(bf16[216,128]{1,0:T(8,128)(2,1)S(1)} %get-tuple-element.71), channel_id=1, source_target_pairs={{0,24},{1,25},{2,26},{3,27},{4,28},{5,29},{6,30},{7,31},{8,16},{9,... | collective-permute-start | bytes 165896 | tf_op jit(solution)/shard_map/ppermute | solution.py:278
  33.6 0.5 %collective-permute-start.9 = (bf16[216,128]{1,0:T(8,128)(2,1)S(1)}, bf16[216,128]{1,0:T(8,128)(2,1)S(1)}, u32[]{:S(2)}, u32[]{:S(2)}) collective-permute-start(bf16[216,128]{1,0:T(8,128)(2,1)S(1)} %get-tuple-element.70), channel_id=1, source_target_pairs={{0,8},{1,9},{2,10},{3,11},{4,12},{5,13},{6,14},{7,15},{8,0},{9,1},... | collective-permute-start | bytes 165896 | tf_op jit(solution)/shard_map/ppermute | solution.py:278
  34.1 0.0 collective-permute-done.10.refs_3_
  34.1 1.3 %shard_map.80 = (bf16[4,128,128]{2,1,0:T(8,128)(2,1)}, bf16[4,128,128]{2,1,0:T(8,128)(2,1)}) custom-call(bf16[4,128,128]{2,1,0:T(8,128)(2,1)S(1)} %bitcast.24, bf16[4,128,128]{2,1,0:T(8,128)(2,1)S(1)} %bitcast.21, bf16[2,128,128]{2,1,0:T(8,128)(2,1)S(1)} %collective-permute-done.4.refs_2_, bf16[2,128,128]{2,1,0:T(8,128)(2,1)S(1)} %collective-permute-done.10.refs_3_, ...), custom_call_target="tpu_custom_call" | custom-call | flops 226492416 | bytes 2949120 | tf_op jit(solution)/shard_map/pallas_call | solution.py:255
  35.4 0.0 collective-permute-done.7
  35.4 2.5 %collective-permute-done.8 = bf16[216,128]{1,0:T(8,128)(2,1)S(1)} collective-permute-done((bf16[216,128]{1,0:T(8,128)(2,1)S(1)}, bf16[216,128]{1,0:T(8,128)(2,1)S(1)}, u32[]{:S(2)}, u32[]{:S(2)}) %collective-permute-start.8) | collective-permute-done | bytes 55328 | tf_op jit(solution)/shard_map/ppermute | solution.py:278
  37.9 0.4 %collective-permute-done.9 = bf16[216,128]{1,0:T(8,128)(2,1)S(1)} collective-permute-done((bf16[216,128]{1,0:T(8,128)(2,1)S(1)}, bf16[216,128]{1,0:T(8,128)(2,1)S(1)}, u32[]{:S(2)}, u32[]{:S(2)}) %collective-permute-start.9) | collective-permute-done | bytes 55328 | tf_op jit(solution)/shard_map/ppermute | solution.py:278
  38.4 0.1 collective-permute-start.11
  38.5 1.3 %collective-permute-done.11 = f32[216,128]{1,0:T(8,128)S(1)} collective-permute-done((f32[216,128]{1,0:T(8,128)S(1)}, f32[216,128]{1,0:T(8,128)S(1)}, u32[]{:S(2)}, u32[]{:S(2)}) %collective-permute-start.11) | collective-permute-done | bytes 110624 | tf_op jit(solution)/shard_map/ppermute | solution.py:272
  39.8 0.7 %broadcast_select_fusion = (f32[216,128]{1,0:T(8,128)}, f32[216,128]{1,0:T(8,128)}) fusion(f32[216,128]{1,0:T(8,128)S(1)} %collective-permute-done.11, f32[216,128]{1,0:T(8,128)S(1)} %fusion.2, pred[]{:T(512)S(6)} %eq.5), kind=kLoop, calls=%fused_computation.9 | loop fusion | flops 55296 | bytes 442369 | tf_op jit(solution)/shard_map/jit(_where)/select_n | solution.py:400
  (11 shorter events, 0.1 us)
Async XLA Ops:
  0.6 7.5 %copy-start = (bf16[3456,128]{1,0:T(8,128)(2,1)S(1)}, bf16[3456,128]{1,0:T(8,128)(2,1)}, u32[]{:S(2)}) copy-start(bf16[3456,128]{1,0:T(8,128)(2,1)} %refs_6_.3) | copy-start | bytes 2654212
  0.6 7.5 %copy-start.1 = (bf16[3456,128]{1,0:T(8,128)(2,1)S(1)}, bf16[3456,128]{1,0:T(8,128)(2,1)}, u32[]{:S(2)}) copy-start(bf16[3456,128]{1,0:T(8,128)(2,1)} %refs_7_.3) | copy-start | bytes 2654212
  0.7 7.5 %copy-start.2 = (bf16[1,4,8,16,128]{4,3,2,1,0:T(8,128)(2,1)S(1)}, bf16[1,4,8,16,128]{4,3,2,1,0:T(8,128)(2,1)}, u32[]{:S(2)}) copy-start(bf16[1,4,8,16,128]{4,3,2,1,0:T(8,128)(2,1)} %param.7) | copy-start | bytes 393220
  0.7 7.5 %copy-start.3 = (bf16[1,4,8,16,128]{4,3,2,1,0:T(8,128)(2,1)S(1)}, bf16[1,4,8,16,128]{4,3,2,1,0:T(8,128)(2,1)}, u32[]{:S(2)}) copy-start(bf16[1,4,8,16,128]{4,3,2,1,0:T(8,128)(2,1)} %param.4) | copy-start | bytes 393220
  1.7 8.1 %collective-permute-start = (bf16[2,128,128]{2,1,0:T(8,128)(2,1)S(1)}, bf16[2,128,128]{2,1,0:T(8,128)(2,1)S(1)}, u32[]{:S(2)}, u32[]{:S(2)}) collective-permute-start(bf16[2,128,128]{2,1,0:T(8,128)(2,1)S(1)} %get-tuple-element.35), channel_id=1, source_target_pairs={{2,4},{6,8},{10,12},{14,16},{18,20},{22,24},{26,28},{4,2},{8,6},{1... | collective-permute-start | bytes 196616 | tf_op jit(solution)/shard_map/ppermute | solution.py:268
  2.4 8.9 %collective-permute-start.1 = (bf16[2,128,128]{2,1,0:T(8,128)(2,1)S(1)}, bf16[2,128,128]{2,1,0:T(8,128)(2,1)S(1)}, u32[]{:S(2)}, u32[]{:S(2)}) collective-permute-start(bf16[2,128,128]{2,1,0:T(8,128)(2,1)S(1)} %get-tuple-element.36), channel_id=1, source_target_pairs={{0,2},{4,6},{8,10},{12,14},{16,18},{20,22},{24,26},{28,30},{2,0},{... | collective-permute-start | bytes 196616 | tf_op jit(solution)/shard_map/ppermute | solution.py:268
  12.0 2.0 %collective-permute-start.2 = (bf16[10,128,128]{2,1,0:T(8,128)(2,1)S(1)}, bf16[10,128,128]{2,1,0:T(8,128)(2,1)S(1)}, u32[]{:S(2)}, u32[]{:S(2)}) collective-permute-start(bf16[10,128,128]{2,1,0:T(8,128)(2,1)S(1)} %get-tuple-element.41), channel_id=1, source_target_pairs={{0,1},{1,0},{2,3},{3,2},{4,5},{5,4},{6,7},{7,6},{8,9},{9,8},{10,11... | collective-permute-start | bytes 983048 | tf_op jit(solution)/shard_map/ppermute | solution.py:272
  12.1 4.6 %collective-permute-start.4 = (bf16[2,128,128]{2,1,0:T(8,128)(2,1)S(1)}, bf16[2,128,128]{2,1,0:T(8,128)(2,1)S(1)}, u32[]{:S(2)}, u32[]{:S(2)}) collective-permute-start(bf16[2,128,128]{2,1,0:T(8,128)(2,1)S(1)} %get-tuple-element.46), channel_id=1, source_target_pairs={{0,2},{4,6},{8,10},{12,14},{16,18},{20,22},{24,26},{28,30},{2,0},{... | collective-permute-start | bytes 196616 | tf_op jit(solution)/shard_map/ppermute | solution.py:268
  16.7 5.9 %collective-permute-start.5 = (bf16[4,216,128]{2,1,0:T(8,128)(2,1)S(1)}, bf16[4,216,128]{2,1,0:T(8,128)(2,1)S(1)}, u32[]{:S(2)}, u32[]{:S(2)}) collective-permute-start(bf16[4,216,128]{2,1,0:T(8,128)(2,1)S(1)} %get-tuple-element.49), channel_id=1, source_target_pairs={{0,2},{1,5},{2,0},{3,7},{4,6},{5,1},{6,4},{7,3},{8,10},{9,13},{10,... | collective-permute-start | bytes 663560 | tf_op jit(solution)/shard_map/ppermute | solution.py:278
  18.4 7.2 %collective-permute-start.3 = (bf16[4,216,128]{2,1,0:T(8,128)(2,1)S(1)}, bf16[4,216,128]{2,1,0:T(8,128)(2,1)S(1)}, u32[]{:S(2)}, u32[]{:S(2)}) collective-permute-start(bf16[4,216,128]{2,1,0:T(8,128)(2,1)S(1)} %get-tuple-element.43), channel_id=1, source_target_pairs={{0,2},{1,5},{2,0},{3,7},{4,6},{5,1},{6,4},{7,3},{8,10},{9,13},{10,... | collective-permute-start | bytes 663560 | tf_op jit(solution)/shard_map/ppermute | solution.py:278
  22.6 6.0 %collective-permute-start.6 = (bf16[4,216,128]{2,1,0:T(8,128)(2,1)S(1)}, bf16[4,216,128]{2,1,0:T(8,128)(2,1)S(1)}, u32[]{:S(2)}, u32[]{:S(2)}) collective-permute-start(bf16[4,216,128]{2,1,0:T(8,128)(2,1)S(1)} %add_convert_fusion), channel_id=1, source_target_pairs={{0,4},{1,3},{2,6},{3,1},{4,0},{5,7},{6,2},{7,5},{8,12},{9,11},{10,... | collective-permute-start | bytes 663560 | tf_op jit(solution)/shard_map/ppermute | solution.py:278
  23.8 10.3 %collective-permute-start.10 = (bf16[2,128,128]{2,1,0:T(8,128)(2,1)S(1)}, bf16[2,128,128]{2,1,0:T(8,128)(2,1)S(1)}, u32[]{:S(2)}, u32[]{:S(2)}) collective-permute-start(bf16[2,128,128]{2,1,0:T(8,128)(2,1)S(1)} %get-tuple-element.56), channel_id=1, source_target_pairs={{2,4},{6,8},{10,12},{14,16},{18,20},{22,24},{26,28},{4,2},{8,6},{1... | collective-permute-start | bytes 196616 | tf_op jit(solution)/shard_map/ppermute | solution.py:268
  28.8 6.7 %collective-permute-start.7 = (bf16[216,128]{1,0:T(8,128)(2,1)S(1)}, bf16[216,128]{1,0:T(8,128)(2,1)S(1)}, u32[]{:S(2)}, u32[]{:S(2)}) collective-permute-start(bf16[216,128]{1,0:T(8,128)(2,1)S(1)} %get-tuple-element.72), channel_id=1, source_target_pairs={{0,16},{1,17},{2,18},{3,19},{4,20},{5,21},{6,22},{7,23},{8,24},{9,... | collective-permute-start | bytes 165896 | tf_op jit(solution)/shard_map/ppermute | solution.py:278
  31.8 6.1 %collective-permute-start.8 = (bf16[216,128]{1,0:T(8,128)(2,1)S(1)}, bf16[216,128]{1,0:T(8,128)(2,1)S(1)}, u32[]{:S(2)}, u32[]{:S(2)}) collective-permute-start(bf16[216,128]{1,0:T(8,128)(2,1)S(1)} %get-tuple-element.71), channel_id=1, source_target_pairs={{0,24},{1,25},{2,26},{3,27},{4,28},{5,29},{6,30},{7,31},{8,16},{9,... | collective-permute-start | bytes 165896 | tf_op jit(solution)/shard_map/ppermute | solution.py:278
  33.6 4.7 %collective-permute-start.9 = (bf16[216,128]{1,0:T(8,128)(2,1)S(1)}, bf16[216,128]{1,0:T(8,128)(2,1)S(1)}, u32[]{:S(2)}, u32[]{:S(2)}) collective-permute-start(bf16[216,128]{1,0:T(8,128)(2,1)S(1)} %get-tuple-element.70), channel_id=1, source_target_pairs={{0,8},{1,9},{2,10},{3,11},{4,12},{5,13},{6,14},{7,15},{8,0},{9,1},... | collective-permute-start | bytes 165896 | tf_op jit(solution)/shard_map/ppermute | solution.py:278
  38.4 1.4 %collective-permute-start.11 = (f32[216,128]{1,0:T(8,128)S(1)}, f32[216,128]{1,0:T(8,128)S(1)}, u32[]{:S(2)}, u32[]{:S(2)}) collective-permute-start(f32[216,128]{1,0:T(8,128)S(1)} %fusion.2), channel_id=1, source_target_pairs={{0,1},{1,0},{2,3},{3,2},{4,5},{5,4},{6,7},{7,6},{8,9},{9,8},{10,11... | collective-permute-start | bytes 331784 | tf_op jit(solution)/shard_map/ppermute | solution.py:272

commit v6 on v5

--- a/solution.py
+++ b/solution.py
@@ -368,7 +368,7 @@
             2 * conv_flops,
             keep, other,
         )
-        send_on, near_mid, mid, grad = lax.optimization_barrier((send_on, near_mid, mid, grad))
+        send_on, mid, grad = lax.optimization_barrier((send_on, mid, grad))
         parts = middle(mid, grad)
         got_on = exchanged(send_on, (orders[0][0], orders[1][0]))
         got_stay = exchanged(send_stay, (orders[0][0], orders[1][0]))

time: 40.7 us -> 39.4 us (0.968)
  waiting for transfers between devices: 12.8 us -> 10.3 us
  starting transfers between devices: 17.6 us -> 18.9 us
    ppermute x6, waiting for transfers between devices: 9.4 us -> 5.94 us  [exchanged(): return lax.ppermute(send, ('tm', 'dp'), route)]
    ppermute x4, starting transfers between devices: 8.96 us -> 10.7 us  [paired(): return lax.ppermute(block, 'tm', pairs + [(j, i) for i, j in pairs])]
    ppermute x2, waiting for transfers between devices: 1.3 us -> 2.91 us  [swapped(): lax.ppermute(block, 'dp', [(i, i ^ 1) for i in range(lax.axis_size('dp'))])]
    ppermute x4, waiting for transfers between devices: 2.08 us -> 1.43 us  [paired(): return lax.ppermute(block, 'tm', pairs + [(j, i) for i, j in pairs])]
    ppermute x6, starting transfers between devices: 8.54 us -> 8.01 us  [exchanged(): return lax.ppermute(send, ('tm', 'dp'), route)]
  transfers between devices with their start and end apart: 12 -> 12, of which waited for: 8 -> 6; matrix products, arithmetic and copies ran while one was open for 0% -> 0% of each run, Pallas kernels for 16% -> 12%
where the time goes in v6:
time: 39.4 us; the launch traced here: 39.2 us
  starting transfers between devices  18.9 us (48%)
  waiting for transfers between devices  10.3 us (26%)
  Pallas kernels  8.4 us (21%)
  other arithmetic  0.85 us (2%)
  between operations  0.78 us (2%)
    ppermute x4, starting transfers between devices, paired(): return lax.ppermute(block, 'tm', pairs + [(j, i) for i, j in pairs])  10.7 us
    pallas_call x6, Pallas kernels, call(): pl.pallas_call(body, out_shape=outs, in_specs=[anywhere if i in unplaced...  8.4 us
    ppermute x6, starting transfers between devices, exchanged(): return lax.ppermute(send, ('tm', 'dp'), route)  8.01 us
    ppermute x6, waiting for transfers between devices, exchanged(): return lax.ppermute(send, ('tm', 'dp'), route)  5.94 us
    ppermute x2, waiting for transfers between devices, swapped(): lax.ppermute(block, 'dp', [(i, i ^ 1) for i in range(lax.axis_size('dp'))])  2.91 us
    ppermute x4, waiting for transfers between devices, paired(): return lax.ppermute(block, 'tm', pairs + [(j, i) for i, j in pairs])  1.43 us
  transfers between devices with their start and end apart: 12, of which 6 were waited for; matrix products, arithmetic and copies ran while one was open for 0% of the time, Pallas kernels for 12%

profile of v6, /device:TPU:0, one launch (start us, length us, event | category | flops | bytes accessed | tf_op | source)
XLA Modules:
  0.0 39.2 jit_solution(8722306817542015868)
XLA Ops:
  0.7 1.0 %shard_map.75 = (bf16[2,128,128]{2,1,0:T(8,128)(2,1)S(1)}, bf16[2,128,128]{2,1,0:T(8,128)(2,1)S(1)}) custom-call(bf16[4,128,128]{2,1,0:T(8,128)(2,1)} %bitcast.22, bf16[4,128,128]{2,1,0:T(8,128)(2,1)} %bitcast.18), custom_call_target="tpu_custom_call" | custom-call | flops 8000000000 | bytes 393216 | tf_op jit(solution)/shard_map/pallas_call | solution.py:255
  1.7 0.7 %collective-permute-start = (bf16[2,128,128]{2,1,0:T(8,128)(2,1)S(1)}, bf16[2,128,128]{2,1,0:T(8,128)(2,1)S(1)}, u32[]{:S(2)}, u32[]{:S(2)}) collective-permute-start(bf16[2,128,128]{2,1,0:T(8,128)(2,1)S(1)} %get-tuple-element.34), channel_id=1, source_target_pairs={{2,4},{6,8},{10,12},{14,16},{18,20},{22,24},{26,28},{4,2},{8,6},{1... | collective-permute-start | bytes 196616 | tf_op jit(solution)/shard_map/ppermute | solution.py:268
  2.4 5.7 %collective-permute-start.1 = (bf16[2,128,128]{2,1,0:T(8,128)(2,1)S(1)}, bf16[2,128,128]{2,1,0:T(8,128)(2,1)S(1)}, u32[]{:S(2)}, u32[]{:S(2)}) collective-permute-start(bf16[2,128,128]{2,1,0:T(8,128)(2,1)S(1)} %get-tuple-element.35), channel_id=1, source_target_pairs={{0,2},{4,6},{8,10},{12,14},{16,18},{20,22},{24,26},{28,30},{2,0},{... | collective-permute-start | bytes 196616 | tf_op jit(solution)/shard_map/ppermute | solution.py:268
  8.1 1.7 %shard_map.76 = (bf16[4,128,128]{2,1,0:T(8,128)(2,1)S(1)}, f32[512,128]{1,0:T(8,128)S(1)}, f32[512,128]{1,0:T(8,128)S(1)}) custom-call(bf16[4,128,128]{2,1,0:T(8,128)(2,1)S(1)} %bitcast.23, bf16[4,128,128]{2,1,0:T(8,128)(2,1)S(1)} %bitcast.19, bf16[3456,128]{1,0:T(8,128)(2,1)S(1)} %copy-done, bf16[3456,128]{1,0:T(8,128)(2,1)S(1)} %copy-done.1), custom_call_target="tpu_custom_call" | custom-call | flops 679477248 | bytes 2686976 | tf_op jit(solution)/shard_map/pallas_call | solution.py:255
  9.8 0.0 collective-permute-done.refs_0_
  9.8 1.4 %collective-permute-done.1.refs_1_ = bf16[2,128,128]{2,1,0:T(8,128)(2,1)S(1)} collective-permute-done((bf16[2,128,128]{2,1,0:T(8,128)(2,1)S(1)}, bf16[2,128,128]{2,1,0:T(8,128)(2,1)S(1)}, u32[]{:S(2)}, u32[]{:S(2)}) %collective-permute-start.1) | collective-permute-done | bytes 65568 | tf_op jit(solution)/shard_map/ppermute | solution.py:268
  11.3 0.7 %shard_map.77 = (bf16[10,128,128]{2,1,0:T(8,128)(2,1)S(1)}, bf16[10,128,128]{2,1,0:T(8,128)(2,1)S(1)}, bf16[4,128,128]{2,1,0:T(8,128)(2,1)S(1)}, bf16[4,128,128]...) custom-call(bf16[2,128,128]{2,1,0:T(8,128)(2,1)S(1)} %collective-permute-done.refs_0_, ...), custom_call_target="tpu_custom_call" | custom-call | flops 226492416 | bytes 3735552 | tf_op jit(solution)/shard_map/pallas_call | solution.py:255
  12.0 0.1 collective-permute-start.2
  12.1 1.6 %collective-permute-done.2.refs_1_ = bf16[10,128,128]{2,1,0:T(8,128)(2,1)S(1)} collective-permute-done((bf16[10,128,128]{2,1,0:T(8,128)(2,1)S(1)}, bf16[10,128,128]{2,1,0:T(8,128)(2,1)S(1)}, u32[]{:S(2)}, u32[]{:S(2)}) %collective-permute-start.2) | collective-permute-done | bytes 327712 | tf_op jit(solution)/shard_map/ppermute | solution.py:272
  13.7 2.0 %shard_map.78 = (f32[4,216,128]{2,1,0:T(8,128)S(1)}, f32[4,216,128]{2,1,0:T(8,128)S(1)}, bf16[4,216,128]{2,1,0:T(8,128)(2,1)S(1)}, bf16[4,216,128]{2,1,0:T(8,128)(2,1)S(1)}) custom-call(bf16[10,128,128]{2,1,0:T(8,128)(2,1)S(1)} %get-tuple-element.39.refs_0_, bf16[10,128,128]{2,1,0:T(8,128)(2,1)S(1)} %collective-permute-done.2.refs_1_), custom_call_target="tpu_custom_call" | custom-call | flops 905969664 | bytes 1982464 | tf_op jit(solution)/shard_map/pallas_call | solution.py:255
  15.7 1.9 %collective-permute-start.4 = (bf16[4,216,128]{2,1,0:T(8,128)(2,1)S(1)}, bf16[4,216,128]{2,1,0:T(8,128)(2,1)S(1)}, u32[]{:S(2)}, u32[]{:S(2)}) collective-permute-start(bf16[4,216,128]{2,1,0:T(8,128)(2,1)S(1)} %get-tuple-element.47), channel_id=1, source_target_pairs={{0,2},{1,5},{2,0},{3,7},{4,6},{5,1},{6,4},{7,3},{8,10},{9,13},{10,... | collective-permute-start | bytes 663560 | tf_op jit(solution)/shard_map/ppermute | solution.py:278
  17.6 0.2 collective-permute-start.3
  17.8 1.6 %shard_map.79 = (f32[512,128]{1,0:T(8,128)S(1)}, f32[512,128]{1,0:T(8,128)S(1)}) custom-call(bf16[4,128,128]{2,1,0:T(8,128)(2,1)S(1)} %get-tuple-element.48.refs_0_, bf16[4,128,128]{2,1,0:T(8,128)(2,1)S(1)} %get-tuple-element.49.refs_1_, bf16[3456,128]{1,0:T(8,128)(2,1)S(1)} %copy-done, bf16[3456,128]{1,0:T(8,128)(2,1)S(1)} %copy-done.1), custom_call_target="tpu_custom_call" | custom-call | flops 679477248 | bytes 2555904 | tf_op jit(solution)/shard_map/pallas_call | solution.py:255
  19.4 2.3 %collective-permute-done.4 = bf16[4,216,128]{2,1,0:T(8,128)(2,1)S(1)} collective-permute-done((bf16[4,216,128]{2,1,0:T(8,128)(2,1)S(1)}, bf16[4,216,128]{2,1,0:T(8,128)(2,1)S(1)}, u32[]{:S(2)}, u32[]{:S(2)}) %collective-permute-start.4) | collective-permute-done | bytes 221216 | tf_op jit(solution)/shard_map/ppermute | solution.py:278
  21.8 1.2 %collective-permute-start.5 = (bf16[4,216,128]{2,1,0:T(8,128)(2,1)S(1)}, bf16[4,216,128]{2,1,0:T(8,128)(2,1)S(1)}, u32[]{:S(2)}, u32[]{:S(2)}) collective-permute-start(bf16[4,216,128]{2,1,0:T(8,128)(2,1)S(1)} %add_convert_fusion), channel_id=1, source_target_pairs={{0,4},{1,3},{2,6},{3,1},{4,0},{5,7},{6,2},{7,5},{8,12},{9,11},{10,... | collective-permute-start | bytes 663560 | tf_op jit(solution)/shard_map/ppermute | solution.py:278
  22.9 0.7 %collective-permute-start.10 = (bf16[2,128,128]{2,1,0:T(8,128)(2,1)S(1)}, bf16[2,128,128]{2,1,0:T(8,128)(2,1)S(1)}, u32[]{:S(2)}, u32[]{:S(2)}) collective-permute-start(bf16[2,128,128]{2,1,0:T(8,128)(2,1)S(1)} %get-tuple-element.54), channel_id=1, source_target_pairs={{2,4},{6,8},{10,12},{14,16},{18,20},{22,24},{26,28},{4,2},{8,6},{1... | collective-permute-start | bytes 196616 | tf_op jit(solution)/shard_map/ppermute | solution.py:268
  23.6 3.7 %collective-permute-start.9 = (bf16[2,128,128]{2,1,0:T(8,128)(2,1)S(1)}, bf16[2,128,128]{2,1,0:T(8,128)(2,1)S(1)}, u32[]{:S(2)}, u32[]{:S(2)}) collective-permute-start(bf16[2,128,128]{2,1,0:T(8,128)(2,1)S(1)} %get-tuple-element.53), channel_id=1, source_target_pairs={{0,2},{4,6},{8,10},{12,14},{16,18},{20,22},{24,26},{28,30},{2,0},{... | collective-permute-start | bytes 196616 | tf_op jit(solution)/shard_map/ppermute | solution.py:268
  27.3 0.0 collective-permute-done.3
  27.3 0.5 %collective-permute-done.5 = bf16[4,216,128]{2,1,0:T(8,128)(2,1)S(1)} collective-permute-done((bf16[4,216,128]{2,1,0:T(8,128)(2,1)S(1)}, bf16[4,216,128]{2,1,0:T(8,128)(2,1)S(1)}, u32[]{:S(2)}, u32[]{:S(2)}) %collective-permute-start.5) | collective-permute-done | bytes 221216 | tf_op jit(solution)/shard_map/ppermute | solution.py:278
  27.8 0.1 fusion.3
  27.9 3.1 %collective-permute-start.6 = (bf16[216,128]{1,0:T(8,128)(2,1)S(1)}, bf16[216,128]{1,0:T(8,128)(2,1)S(1)}, u32[]{:S(2)}, u32[]{:S(2)}) collective-permute-start(bf16[216,128]{1,0:T(8,128)(2,1)S(1)} %get-tuple-element.70), channel_id=1, source_target_pairs={{0,16},{1,17},{2,18},{3,19},{4,20},{5,21},{6,22},{7,23},{8,24},{9,... | collective-permute-start | bytes 165896 | tf_op jit(solution)/shard_map/ppermute | solution.py:278
  31.0 1.3 %collective-permute-start.7 = (bf16[216,128]{1,0:T(8,128)(2,1)S(1)}, bf16[216,128]{1,0:T(8,128)(2,1)S(1)}, u32[]{:S(2)}, u32[]{:S(2)}) collective-permute-start(bf16[216,128]{1,0:T(8,128)(2,1)S(1)} %get-tuple-element.69), channel_id=1, source_target_pairs={{0,24},{1,25},{2,26},{3,27},{4,28},{5,29},{6,30},{7,31},{8,16},{9,... | collective-permute-start | bytes 165896 | tf_op jit(solution)/shard_map/ppermute | solution.py:278
  32.4 0.2 collective-permute-start.8
  32.6 0.0 collective-permute-done.10.refs_3_
  32.6 0.0 collective-permute-done.9.refs_2_
  32.6 1.3 %shard_map.80 = (bf16[4,128,128]{2,1,0:T(8,128)(2,1)}, bf16[4,128,128]{2,1,0:T(8,128)(2,1)}) custom-call(bf16[4,128,128]{2,1,0:T(8,128)(2,1)S(1)} %bitcast.24, bf16[4,128,128]{2,1,0:T(8,128)(2,1)S(1)} %bitcast.21, bf16[2,128,128]{2,1,0:T(8,128)(2,1)S(1)} %collective-permute-done.9.refs_2_, bf16[2,128,128]{2,1,0:T(8,128)(2,1)S(1)} %collective-permute-done.10.refs_3_, ...), custom_call_target="tpu_custom_call" | custom-call | flops 226492416 | bytes 2949120 | tf_op jit(solution)/shard_map/pallas_call | solution.py:255
  33.9 0.0 collective-permute-done.6
  33.9 3.1 %collective-permute-done.7 = bf16[216,128]{1,0:T(8,128)(2,1)S(1)} collective-permute-done((bf16[216,128]{1,0:T(8,128)(2,1)S(1)}, bf16[216,128]{1,0:T(8,128)(2,1)S(1)}, u32[]{:S(2)}, u32[]{:S(2)}) %collective-permute-start.7) | collective-permute-done | bytes 55328 | tf_op jit(solution)/shard_map/ppermute | solution.py:278
  37.1 0.0 collective-permute-done.8
  37.1 0.1 collective-permute-start.11
  37.2 1.3 %collective-permute-done.11 = f32[216,128]{1,0:T(8,128)S(1)} collective-permute-done((f32[216,128]{1,0:T(8,128)S(1)}, f32[216,128]{1,0:T(8,128)S(1)}, u32[]{:S(2)}, u32[]{:S(2)}) %collective-permute-start.11) | collective-permute-done | bytes 110624 | tf_op jit(solution)/shard_map/ppermute | solution.py:272
  38.5 0.7 %broadcast_select_fusion = (f32[216,128]{1,0:T(8,128)}, f32[216,128]{1,0:T(8,128)}) fusion(f32[216,128]{1,0:T(8,128)S(1)} %collective-permute-done.11, f32[216,128]{1,0:T(8,128)S(1)} %fusion.2, pred[]{:T(512)S(6)} %eq.5), kind=kLoop, calls=%fused_computation.9 | loop fusion | flops 55296 | bytes 442369 | tf_op jit(solution)/shard_map/jit(_where)/select_n | solution.py:400
  (11 shorter events, 0.1 us)
Async XLA Ops:
  0.6 7.5 %copy-start = (bf16[3456,128]{1,0:T(8,128)(2,1)S(1)}, bf16[3456,128]{1,0:T(8,128)(2,1)}, u32[]{:S(2)}) copy-start(bf16[3456,128]{1,0:T(8,128)(2,1)} %refs_6_.3) | copy-start | bytes 2654212
  0.6 7.5 %copy-start.1 = (bf16[3456,128]{1,0:T(8,128)(2,1)S(1)}, bf16[3456,128]{1,0:T(8,128)(2,1)}, u32[]{:S(2)}) copy-start(bf16[3456,128]{1,0:T(8,128)(2,1)} %refs_7_.3) | copy-start | bytes 2654212
  0.7 7.5 %copy-start.2 = (bf16[1,4,8,16,128]{4,3,2,1,0:T(8,128)(2,1)S(1)}, bf16[1,4,8,16,128]{4,3,2,1,0:T(8,128)(2,1)}, u32[]{:S(2)}) copy-start(bf16[1,4,8,16,128]{4,3,2,1,0:T(8,128)(2,1)} %param.7) | copy-start | bytes 393220
  0.7 7.5 %copy-start.3 = (bf16[1,4,8,16,128]{4,3,2,1,0:T(8,128)(2,1)S(1)}, bf16[1,4,8,16,128]{4,3,2,1,0:T(8,128)(2,1)}, u32[]{:S(2)}) copy-start(bf16[1,4,8,16,128]{4,3,2,1,0:T(8,128)(2,1)} %param.4) | copy-start | bytes 393220
  1.7 8.1 %collective-permute-start = (bf16[2,128,128]{2,1,0:T(8,128)(2,1)S(1)}, bf16[2,128,128]{2,1,0:T(8,128)(2,1)S(1)}, u32[]{:S(2)}, u32[]{:S(2)}) collective-permute-start(bf16[2,128,128]{2,1,0:T(8,128)(2,1)S(1)} %get-tuple-element.34), channel_id=1, source_target_pairs={{2,4},{6,8},{10,12},{14,16},{18,20},{22,24},{26,28},{4,2},{8,6},{1... | collective-permute-start | bytes 196616 | tf_op jit(solution)/shard_map/ppermute | solution.py:268
  2.4 8.9 %collective-permute-start.1 = (bf16[2,128,128]{2,1,0:T(8,128)(2,1)S(1)}, bf16[2,128,128]{2,1,0:T(8,128)(2,1)S(1)}, u32[]{:S(2)}, u32[]{:S(2)}) collective-permute-start(bf16[2,128,128]{2,1,0:T(8,128)(2,1)S(1)} %get-tuple-element.35), channel_id=1, source_target_pairs={{0,2},{4,6},{8,10},{12,14},{16,18},{20,22},{24,26},{28,30},{2,0},{... | collective-permute-start | bytes 196616 | tf_op jit(solution)/shard_map/ppermute | solution.py:268
  12.0 1.7 %collective-permute-start.2 = (bf16[10,128,128]{2,1,0:T(8,128)(2,1)S(1)}, bf16[10,128,128]{2,1,0:T(8,128)(2,1)S(1)}, u32[]{:S(2)}, u32[]{:S(2)}) collective-permute-start(bf16[10,128,128]{2,1,0:T(8,128)(2,1)S(1)} %get-tuple-element.40), channel_id=1, source_target_pairs={{0,1},{1,0},{2,3},{3,2},{4,5},{5,4},{6,7},{7,6},{8,9},{9,8},{10,11... | collective-permute-start | bytes 983048 | tf_op jit(solution)/shard_map/ppermute | solution.py:272
  15.7 6.0 %collective-permute-start.4 = (bf16[4,216,128]{2,1,0:T(8,128)(2,1)S(1)}, bf16[4,216,128]{2,1,0:T(8,128)(2,1)S(1)}, u32[]{:S(2)}, u32[]{:S(2)}) collective-permute-start(bf16[4,216,128]{2,1,0:T(8,128)(2,1)S(1)} %get-tuple-element.47), channel_id=1, source_target_pairs={{0,2},{1,5},{2,0},{3,7},{4,6},{5,1},{6,4},{7,3},{8,10},{9,13},{10,... | collective-permute-start | bytes 663560 | tf_op jit(solution)/shard_map/ppermute | solution.py:278
  17.6 9.7 %collective-permute-start.3 = (bf16[4,216,128]{2,1,0:T(8,128)(2,1)S(1)}, bf16[4,216,128]{2,1,0:T(8,128)(2,1)S(1)}, u32[]{:S(2)}, u32[]{:S(2)}) collective-permute-start(bf16[4,216,128]{2,1,0:T(8,128)(2,1)S(1)} %get-tuple-element.42), channel_id=1, source_target_pairs={{0,2},{1,5},{2,0},{3,7},{4,6},{5,1},{6,4},{7,3},{8,10},{9,13},{10,... | collective-permute-start | bytes 663560 | tf_op jit(solution)/shard_map/ppermute | solution.py:278
  21.8 6.0 %collective-permute-start.5 = (bf16[4,216,128]{2,1,0:T(8,128)(2,1)S(1)}, bf16[4,216,128]{2,1,0:T(8,128)(2,1)S(1)}, u32[]{:S(2)}, u32[]{:S(2)}) collective-permute-start(bf16[4,216,128]{2,1,0:T(8,128)(2,1)S(1)} %add_convert_fusion), channel_id=1, source_target_pairs={{0,4},{1,3},{2,6},{3,1},{4,0},{5,7},{6,2},{7,5},{8,12},{9,11},{10,... | collective-permute-start | bytes 663560 | tf_op jit(solution)/shard_map/ppermute | solution.py:278
  22.9 9.7 %collective-permute-start.10 = (bf16[2,128,128]{2,1,0:T(8,128)(2,1)S(1)}, bf16[2,128,128]{2,1,0:T(8,128)(2,1)S(1)}, u32[]{:S(2)}, u32[]{:S(2)}) collective-permute-start(bf16[2,128,128]{2,1,0:T(8,128)(2,1)S(1)} %get-tuple-element.54), channel_id=1, source_target_pairs={{2,4},{6,8},{10,12},{14,16},{18,20},{22,24},{26,28},{4,2},{8,6},{1... | collective-permute-start | bytes 196616 | tf_op jit(solution)/shard_map/ppermute | solution.py:268
  23.6 9.0 %collective-permute-start.9 = (bf16[2,128,128]{2,1,0:T(8,128)(2,1)S(1)}, bf16[2,128,128]{2,1,0:T(8,128)(2,1)S(1)}, u32[]{:S(2)}, u32[]{:S(2)}) collective-permute-start(bf16[2,128,128]{2,1,0:T(8,128)(2,1)S(1)} %get-tuple-element.53), channel_id=1, source_target_pairs={{0,2},{4,6},{8,10},{12,14},{16,18},{20,22},{24,26},{28,30},{2,0},{... | collective-permute-start | bytes 196616 | tf_op jit(solution)/shard_map/ppermute | solution.py:268
  27.9 6.1 %collective-permute-start.6 = (bf16[216,128]{1,0:T(8,128)(2,1)S(1)}, bf16[216,128]{1,0:T(8,128)(2,1)S(1)}, u32[]{:S(2)}, u32[]{:S(2)}) collective-permute-start(bf16[216,128]{1,0:T(8,128)(2,1)S(1)} %get-tuple-element.70), channel_id=1, source_target_pairs={{0,16},{1,17},{2,18},{3,19},{4,20},{5,21},{6,22},{7,23},{8,24},{9,... | collective-permute-start | bytes 165896 | tf_op jit(solution)/shard_map/ppermute | solution.py:278
  31.0 6.1 %collective-permute-start.7 = (bf16[216,128]{1,0:T(8,128)(2,1)S(1)}, bf16[216,128]{1,0:T(8,128)(2,1)S(1)}, u32[]{:S(2)}, u32[]{:S(2)}) collective-permute-start(bf16[216,128]{1,0:T(8,128)(2,1)S(1)} %get-tuple-element.69), channel_id=1, source_target_pairs={{0,24},{1,25},{2,26},{3,27},{4,28},{5,29},{6,30},{7,31},{8,16},{9,... | collective-permute-start | bytes 165896 | tf_op jit(solution)/shard_map/ppermute | solution.py:278
  32.4 4.7 %collective-permute-start.8 = (bf16[216,128]{1,0:T(8,128)(2,1)S(1)}, bf16[216,128]{1,0:T(8,128)(2,1)S(1)}, u32[]{:S(2)}, u32[]{:S(2)}) collective-permute-start(bf16[216,128]{1,0:T(8,128)(2,1)S(1)} %get-tuple-element.68), channel_id=1, source_target_pairs={{0,8},{1,9},{2,10},{3,11},{4,12},{5,13},{6,14},{7,15},{8,0},{9,1},... | collective-permute-start | bytes 165896 | tf_op jit(solution)/shard_map/ppermute | solution.py:278
  37.1 1.4 %collective-permute-start.11 = (f32[216,128]{1,0:T(8,128)S(1)}, f32[216,128]{1,0:T(8,128)S(1)}, u32[]{:S(2)}, u32[]{:S(2)}) collective-permute-start(f32[216,128]{1,0:T(8,128)S(1)} %fusion.2), channel_id=1, source_target_pairs={{0,1},{1,0},{2,3},{3,2},{4,5},{5,4},{6,7},{7,6},{8,9},{9,8},{10,11... | collective-permute-start | bytes 331784 | tf_op jit(solution)/shard_map/ppermute | solution.py:272

commit v7 on v6

--- a/solution.py
+++ b/solution.py
@@ -173,52 +173,40 @@
         store(send, keep)
 
 
-def kernel_sums(width, own, other, acc, patches, turned):
-    chans = own.shape[2]
-    cells = own.shape[1]
+def kernel_sums(width, source, acc, patches, turned, before=None):
+    ext_frames, cells, chans = source.shape
     halo = TAPS - 1
-    frames = (own.shape[0] - halo) // 2
-    ext = frames + halo
+    frames = (ext_frames - halo) // 2
     odd = lax.axis_index("dp") % 2
-    for clip, source in enumerate((own, other)):
-        fill(patches, clip * ext, source[pl.ds(odd * frames, ext)], width, True)
-        for n in range(ext):
-            block = source[(1 - odd) * frames + n]
-            place = (clip * ext + n) * cells
-            turned[:, place : place + cells] = block.T
+    fill(patches, 0, source[pl.ds(odd * frames, frames + halo)], width, True)
+    for n in range(frames + halo):
+        turned[:, n * cells : (n + 1) * cells] = source[(1 - odd) * frames + n].T
     for kt in range(TAPS):
         l_start = (1 - odd) * kt
         r_start = odd * (halo - kt)
-        left = jnp.concatenate(
-            [
-                turned[:, pl.ds(pl.multiple_of((clip * ext + l_start) * cells, cells), frames * cells)]
-                for clip in range(2)
-            ],
-            axis=1,
-        )
+        left = turned[:, pl.ds(pl.multiple_of(l_start * cells, cells), frames * cells)]
         for ki in range(TAPS):
             low = (halo - ki) * width
-            right = jnp.concatenate(
-                [
-                    patches[pl.ds(clip * ext + r_start, frames), low : low + cells, :].reshape(
-                        frames * cells, TAPS * chans
-                    )
-                    for clip in range(2)
-                ],
-                axis=0,
-            )
+            right = patches[pl.ds(r_start, frames), low : low + cells, :].reshape(frames * cells, TAPS * chans)
             sums = jnp.dot(left, right, preferred_element_type=F32)
             for kj in range(TAPS):
                 row = ((kt * TAPS + ki) * TAPS + kj) * chans
-                acc[row : row + chans, :] = sums[:, kj * chans : (kj + 1) * chans]
-
-
-def plain_sums_kernel(width, own, other, acc, patches, turned):
-    kernel_sums(width, own, other, acc, patches, turned)
-
-
-def relative_sums_kernel(width, distance, own, other, stay, pass_on, send_stay, send_on, acc, patches, turned):
-    kernel_sums(width, own, other, acc, patches, turned)
+                part = sums[:, kj * chans : (kj + 1) * chans]
+                if before is not None:
+                    part = part + before[row : row + chans, :]
+                acc[row : row + chans, :] = part
+
+
+def own_sums_kernel(width, own, acc, patches, turned):
+    kernel_sums(width, own, acc, patches, turned)
+
+
+def plain_sums_kernel(width, own_sums, other, acc, patches, turned):
+    kernel_sums(width, other, acc, patches, turned, own_sums)
+
+
+def relative_sums_kernel(width, distance, own_sums, other, stay, pass_on, send_stay, send_on, acc, patches, turned):
+    kernel_sums(width, other, acc, patches, turned, own_sums)
     size, rows, _ = stay.shape
     odd = lax.axis_index("dp") % 2
     me = lax.axis_index("tm")
@@ -350,9 +338,16 @@
         )
 
     scratch = [
-        pltpu.VMEM((2 * ext, cells + 2 * width, TAPS * chans), BF16),
-        pltpu.VMEM((chans, 2 * ext * cells), BF16),
+        pltpu.VMEM((ext, cells + 2 * width, TAPS * chans), BF16),
+        pltpu.VMEM((chans, ext * cells), BF16),
     ]
+    (own_sums,) = call(
+        lambda *refs: own_sums_kernel(width, *refs),
+        [shape((krows, chans), F32)],
+        scratch,
+        conv_flops,
+        keep,
+    )
     if dp == 2 and tm >= 4 and tm & (tm - 1) == 0 and rows % 8 == 0:
         size = tm // 4
         orders = ((1, 2), (2, 1))
@@ -365,8 +360,8 @@
             lambda *refs: relative_sums_kernel(width, distance, *refs),
             [wide, wide, narrow, narrow],
             [pltpu.VMEM((krows, chans), F32)] + scratch,
-            2 * conv_flops,
-            keep, other,
+            conv_flops,
+            own_sums, other,
         )
         send_on, mid, grad = lax.optimization_barrier((send_on, mid, grad))
         parts = middle(mid, grad)
@@ -386,8 +381,8 @@
             lambda *refs: plain_sums_kernel(width, *refs),
             [shape((krows, chans), F32)],
             scratch,
-            2 * conv_flops,
-            keep, other,
+            conv_flops,
+            own_sums, other,
         )
         output, movie_grad = finish(near_mid, far_mid, *middle(mid, grad))
         mine = lax.psum_scatter(sums, "tm", scatter_dimension=0, tiled=True)

time: 39.4 us -> 38.6 us (0.980)
  waiting for transfers between devices: 10.3 us -> 9.25 us
    ppermute x2, waiting for transfers between devices: 2.91 us -> 1.87 us  [swapped(): lax.ppermute(block, 'dp', [(i, i ^ 1) for i in range(lax.axis_size('dp'))])]
    pallas_call x6 -> x7, Pallas kernels: 8.4 us -> 8.57 us  [call(): pl.pallas_call(body, out_shape=outs, in_specs=[anywhere if i in unplaced...]
  transfers between devices with their start and end apart: 12 -> 12, of which waited for: 6 -> 6; matrix products, arithmetic and copies ran while one was open for 0% -> 0% of each run, Pallas kernels for 12% -> 15%
where the time goes in v7:
time: 38.6 us; the launch traced here: 38.4 us
  starting transfers between devices  18.9 us (49%)
  waiting for transfers between devices  9.25 us (24%)
  Pallas kernels  8.57 us (22%)
  other arithmetic  0.86 us (2%)
  between operations  0.78 us (2%)
    ppermute x4, starting transfers between devices, paired(): return lax.ppermute(block, 'tm', pairs + [(j, i) for i, j in pairs])  10.7 us
    pallas_call x7, Pallas kernels, call(): pl.pallas_call(body, out_shape=outs, in_specs=[anywhere if i in unplaced...  8.57 us
    ppermute x6, starting transfers between devices, exchanged(): return lax.ppermute(send, ('tm', 'dp'), route)  8.02 us
    ppermute x6, waiting for transfers between devices, exchanged(): return lax.ppermute(send, ('tm', 'dp'), route)  5.95 us
    ppermute x2, waiting for transfers between devices, swapped(): lax.ppermute(block, 'dp', [(i, i ^ 1) for i in range(lax.axis_size('dp'))])  1.87 us
    ppermute x4, waiting for transfers between devices, paired(): return lax.ppermute(block, 'tm', pairs + [(j, i) for i, j in pairs])  1.43 us
  transfers between devices with their start and end apart: 12, of which 6 were waited for; matrix products, arithmetic and copies ran while one was open for 0% of the time, Pallas kernels for 15%

profile of v7, /device:TPU:0, one launch (start us, length us, event | category | flops | bytes accessed | tf_op | source)
XLA Modules:
  0.0 38.4 jit_solution(1930388312013096553)
XLA Ops:
  0.7 1.0 %shard_map.75 = (bf16[2,128,128]{2,1,0:T(8,128)(2,1)S(1)}, bf16[2,128,128]{2,1,0:T(8,128)(2,1)S(1)}) custom-call(bf16[4,128,128]{2,1,0:T(8,128)(2,1)} %bitcast.22, bf16[4,128,128]{2,1,0:T(8,128)(2,1)} %bitcast.18), custom_call_target="tpu_custom_call" | custom-call | flops 8000000000 | bytes 393216 | tf_op jit(solution)/shard_map/pallas_call | solution.py:243
  1.7 0.7 %collective-permute-start = (bf16[2,128,128]{2,1,0:T(8,128)(2,1)S(1)}, bf16[2,128,128]{2,1,0:T(8,128)(2,1)S(1)}, u32[]{:S(2)}, u32[]{:S(2)}) collective-permute-start(bf16[2,128,128]{2,1,0:T(8,128)(2,1)S(1)} %get-tuple-element.34), channel_id=1, source_target_pairs={{2,4},{6,8},{10,12},{14,16},{18,20},{22,24},{26,28},{4,2},{8,6},{1... | collective-permute-start | bytes 196616 | tf_op jit(solution)/shard_map/ppermute | solution.py:256
  2.4 5.7 %collective-permute-start.1 = (bf16[2,128,128]{2,1,0:T(8,128)(2,1)S(1)}, bf16[2,128,128]{2,1,0:T(8,128)(2,1)S(1)}, u32[]{:S(2)}, u32[]{:S(2)}) collective-permute-start(bf16[2,128,128]{2,1,0:T(8,128)(2,1)S(1)} %get-tuple-element.35), channel_id=1, source_target_pairs={{0,2},{4,6},{8,10},{12,14},{16,18},{20,22},{24,26},{28,30},{2,0},{... | collective-permute-start | bytes 196616 | tf_op jit(solution)/shard_map/ppermute | solution.py:256
  8.1 1.7 %shard_map.76 = (bf16[4,128,128]{2,1,0:T(8,128)(2,1)S(1)}, f32[512,128]{1,0:T(8,128)S(1)}, f32[512,128]{1,0:T(8,128)S(1)}) custom-call(bf16[4,128,128]{2,1,0:T(8,128)(2,1)S(1)} %bitcast.23, bf16[4,128,128]{2,1,0:T(8,128)(2,1)S(1)} %bitcast.19, bf16[3456,128]{1,0:T(8,128)(2,1)S(1)} %copy-done, bf16[3456,128]{1,0:T(8,128)(2,1)S(1)} %copy-done.1), custom_call_target="tpu_custom_call" | custom-call | flops 679477248 | bytes 2686976 | tf_op jit(solution)/shard_map/pallas_call | solution.py:243
  9.8 0.0 collective-permute-done.refs_0_
  9.8 1.4 %collective-permute-done.1.refs_1_ = bf16[2,128,128]{2,1,0:T(8,128)(2,1)S(1)} collective-permute-done((bf16[2,128,128]{2,1,0:T(8,128)(2,1)S(1)}, bf16[2,128,128]{2,1,0:T(8,128)(2,1)S(1)}, u32[]{:S(2)}, u32[]{:S(2)}) %collective-permute-start.1) | collective-permute-done | bytes 65568 | tf_op jit(solution)/shard_map/ppermute | solution.py:256
  11.3 0.7 %shard_map.77 = (bf16[10,128,128]{2,1,0:T(8,128)(2,1)S(1)}, bf16[10,128,128]{2,1,0:T(8,128)(2,1)S(1)}, bf16[4,128,128]{2,1,0:T(8,128)(2,1)S(1)}, bf16[4,128,128]...) custom-call(bf16[2,128,128]{2,1,0:T(8,128)(2,1)S(1)} %collective-permute-done.refs_0_, ...), custom_call_target="tpu_custom_call" | custom-call | flops 226492416 | bytes 3735552 | tf_op jit(solution)/shard_map/pallas_call | solution.py:243
  12.0 0.1 collective-permute-start.2
  12.1 1.0 %shard_map.78.refs_0_ = f32[3456,128]{1,0:T(8,128)S(1)} custom-call(bf16[10,128,128]{2,1,0:T(8,128)(2,1)S(1)} %get-tuple-element.39.refs_0_), custom_call_target="tpu_custom_call" | custom-call | flops 452984832 | bytes 2097152 | tf_op jit(solution)/shard_map/pallas_call | solution.py:243
  13.1 0.6 %collective-permute-done.2.refs_1_ = bf16[10,128,128]{2,1,0:T(8,128)(2,1)S(1)} collective-permute-done((bf16[10,128,128]{2,1,0:T(8,128)(2,1)S(1)}, bf16[10,128,128]{2,1,0:T(8,128)(2,1)S(1)}, u32[]{:S(2)}, u32[]{:S(2)}) %collective-permute-start.2) | collective-permute-done | bytes 327712 | tf_op jit(solution)/shard_map/ppermute | solution.py:260
  13.7 1.2 %shard_map.79 = (f32[4,216,128]{2,1,0:T(8,128)S(1)}, f32[4,216,128]{2,1,0:T(8,128)S(1)}, bf16[4,216,128]{2,1,0:T(8,128)(2,1)S(1)}, bf16[4,216,128]{2,1,0:T(8,128)(2,1)S(1)}) custom-call(f32[3456,128]{1,0:T(8,128)S(1)} %shard_map.78.refs_0_, bf16[10,128,128]{2,1,0:T(8,128)(2,1)S(1)} %collective-permute-done.2.refs_1_), custom_call_target="tpu_custom_call" | custom-call | flops 452984832 | bytes 3424256 | tf_op jit(solution)/shard_map/pallas_call | solution.py:243
  14.9 1.9 %collective-permute-start.4 = (bf16[4,216,128]{2,1,0:T(8,128)(2,1)S(1)}, bf16[4,216,128]{2,1,0:T(8,128)(2,1)S(1)}, u32[]{:S(2)}, u32[]{:S(2)}) collective-permute-start(bf16[4,216,128]{2,1,0:T(8,128)(2,1)S(1)} %get-tuple-element.47), channel_id=1, source_target_pairs={{0,2},{1,5},{2,0},{3,7},{4,6},{5,1},{6,4},{7,3},{8,10},{9,13},{10,... | collective-permute-start | bytes 663560 | tf_op jit(solution)/shard_map/ppermute | solution.py:266
  16.8 0.2 collective-permute-start.3
  17.0 1.6 %shard_map.80 = (f32[512,128]{1,0:T(8,128)S(1)}, f32[512,128]{1,0:T(8,128)S(1)}) custom-call(bf16[4,128,128]{2,1,0:T(8,128)(2,1)S(1)} %get-tuple-element.48.refs_0_, bf16[4,128,128]{2,1,0:T(8,128)(2,1)S(1)} %get-tuple-element.49.refs_1_, bf16[3456,128]{1,0:T(8,128)(2,1)S(1)} %copy-done, bf16[3456,128]{1,0:T(8,128)(2,1)S(1)} %copy-done.1), custom_call_target="tpu_custom_call" | custom-call | flops 679477248 | bytes 2555904 | tf_op jit(solution)/shard_map/pallas_call | solution.py:243
  18.6 2.3 %collective-permute-done.4 = bf16[4,216,128]{2,1,0:T(8,128)(2,1)S(1)} collective-permute-done((bf16[4,216,128]{2,1,0:T(8,128)(2,1)S(1)}, bf16[4,216,128]{2,1,0:T(8,128)(2,1)S(1)}, u32[]{:S(2)}, u32[]{:S(2)}) %collective-permute-start.4) | collective-permute-done | bytes 221216 | tf_op jit(solution)/shard_map/ppermute | solution.py:266
  20.9 1.2 %collective-permute-start.5 = (bf16[4,216,128]{2,1,0:T(8,128)(2,1)S(1)}, bf16[4,216,128]{2,1,0:T(8,128)(2,1)S(1)}, u32[]{:S(2)}, u32[]{:S(2)}) collective-permute-start(bf16[4,216,128]{2,1,0:T(8,128)(2,1)S(1)} %add_convert_fusion), channel_id=1, source_target_pairs={{0,4},{1,3},{2,6},{3,1},{4,0},{5,7},{6,2},{7,5},{8,12},{9,11},{10,... | collective-permute-start | bytes 663560 | tf_op jit(solution)/shard_map/ppermute | solution.py:266
  22.1 0.7 %collective-permute-start.10 = (bf16[2,128,128]{2,1,0:T(8,128)(2,1)S(1)}, bf16[2,128,128]{2,1,0:T(8,128)(2,1)S(1)}, u32[]{:S(2)}, u32[]{:S(2)}) collective-permute-start(bf16[2,128,128]{2,1,0:T(8,128)(2,1)S(1)} %get-tuple-element.54), channel_id=1, source_target_pairs={{2,4},{6,8},{10,12},{14,16},{18,20},{22,24},{26,28},{4,2},{8,6},{1... | collective-permute-start | bytes 196616 | tf_op jit(solution)/shard_map/ppermute | solution.py:256
  22.8 3.7 %collective-permute-start.9 = (bf16[2,128,128]{2,1,0:T(8,128)(2,1)S(1)}, bf16[2,128,128]{2,1,0:T(8,128)(2,1)S(1)}, u32[]{:S(2)}, u32[]{:S(2)}) collective-permute-start(bf16[2,128,128]{2,1,0:T(8,128)(2,1)S(1)} %get-tuple-element.53), channel_id=1, source_target_pairs={{0,2},{4,6},{8,10},{12,14},{16,18},{20,22},{24,26},{28,30},{2,0},{... | collective-permute-start | bytes 196616 | tf_op jit(solution)/shard_map/ppermute | solution.py:256
  26.4 0.0 collective-permute-done.3
  26.4 0.5 %collective-permute-done.5 = bf16[4,216,128]{2,1,0:T(8,128)(2,1)S(1)} collective-permute-done((bf16[4,216,128]{2,1,0:T(8,128)(2,1)S(1)}, bf16[4,216,128]{2,1,0:T(8,128)(2,1)S(1)}, u32[]{:S(2)}, u32[]{:S(2)}) %collective-permute-start.5) | collective-permute-done | bytes 221216 | tf_op jit(solution)/shard_map/ppermute | solution.py:266
  26.9 0.1 fusion.3
  27.0 3.2 %collective-permute-start.6 = (bf16[216,128]{1,0:T(8,128)(2,1)S(1)}, bf16[216,128]{1,0:T(8,128)(2,1)S(1)}, u32[]{:S(2)}, u32[]{:S(2)}) collective-permute-start(bf16[216,128]{1,0:T(8,128)(2,1)S(1)} %get-tuple-element.70), channel_id=1, source_target_pairs={{0,16},{1,17},{2,18},{3,19},{4,20},{5,21},{6,22},{7,23},{8,24},{9,... | collective-permute-start | bytes 165896 | tf_op jit(solution)/shard_map/ppermute | solution.py:266
  30.2 1.3 %collective-permute-start.7 = (bf16[216,128]{1,0:T(8,128)(2,1)S(1)}, bf16[216,128]{1,0:T(8,128)(2,1)S(1)}, u32[]{:S(2)}, u32[]{:S(2)}) collective-permute-start(bf16[216,128]{1,0:T(8,128)(2,1)S(1)} %get-tuple-element.69), channel_id=1, source_target_pairs={{0,24},{1,25},{2,26},{3,27},{4,28},{5,29},{6,30},{7,31},{8,16},{9,... | collective-permute-start | bytes 165896 | tf_op jit(solution)/shard_map/ppermute | solution.py:266
  31.5 0.2 collective-permute-start.8
  31.8 0.0 collective-permute-done.10.refs_3_
  31.8 1.3 %shard_map.81 = (bf16[4,128,128]{2,1,0:T(8,128)(2,1)}, bf16[4,128,128]{2,1,0:T(8,128)(2,1)}) custom-call(bf16[4,128,128]{2,1,0:T(8,128)(2,1)S(1)} %bitcast.24, bf16[4,128,128]{2,1,0:T(8,128)(2,1)S(1)} %bitcast.21, bf16[2,128,128]{2,1,0:T(8,128)(2,1)S(1)} %collective-permute-done.9.refs_2_, bf16[2,128,128]{2,1,0:T(8,128)(2,1)S(1)} %collective-permute-done.10.refs_3_, ...), custom_call_target="tpu_custom_call" | custom-call | flops 226492416 | bytes 2949120 | tf_op jit(solution)/shard_map/pallas_call | solution.py:243
  33.1 0.0 collective-permute-done.6
  33.1 3.1 %collective-permute-done.7 = bf16[216,128]{1,0:T(8,128)(2,1)S(1)} collective-permute-done((bf16[216,128]{1,0:T(8,128)(2,1)S(1)}, bf16[216,128]{1,0:T(8,128)(2,1)S(1)}, u32[]{:S(2)}, u32[]{:S(2)}) %collective-permute-start.7) | collective-permute-done | bytes 55328 | tf_op jit(solution)/shard_map/ppermute | solution.py:266
  36.2 0.0 collective-permute-done.8
  36.3 0.1 collective-permute-start.11
  36.4 1.3 %collective-permute-done.11 = f32[216,128]{1,0:T(8,128)S(1)} collective-permute-done((f32[216,128]{1,0:T(8,128)S(1)}, f32[216,128]{1,0:T(8,128)S(1)}, u32[]{:S(2)}, u32[]{:S(2)}) %collective-permute-start.11) | collective-permute-done | bytes 110624 | tf_op jit(solution)/shard_map/ppermute | solution.py:260
  37.7 0.7 %broadcast_select_fusion = (f32[216,128]{1,0:T(8,128)}, f32[216,128]{1,0:T(8,128)}) fusion(f32[216,128]{1,0:T(8,128)S(1)} %collective-permute-done.11, f32[216,128]{1,0:T(8,128)S(1)} %fusion.2, pred[]{:T(512)S(6)} %eq.5), kind=kLoop, calls=%fused_computation.9 | loop fusion | flops 55296 | bytes 442369 | tf_op jit(solution)/shard_map/jit(_where)/select_n | solution.py:395
  (12 shorter events, 0.1 us)
Async XLA Ops:
  0.6 7.5 %copy-start = (bf16[3456,128]{1,0:T(8,128)(2,1)S(1)}, bf16[3456,128]{1,0:T(8,128)(2,1)}, u32[]{:S(2)}) copy-start(bf16[3456,128]{1,0:T(8,128)(2,1)} %refs_6_.3) | copy-start | bytes 2654212
  0.6 7.5 %copy-start.1 = (bf16[3456,128]{1,0:T(8,128)(2,1)S(1)}, bf16[3456,128]{1,0:T(8,128)(2,1)}, u32[]{:S(2)}) copy-start(bf16[3456,128]{1,0:T(8,128)(2,1)} %refs_7_.3) | copy-start | bytes 2654212
  0.7 7.5 %copy-start.2 = (bf16[1,4,8,16,128]{4,3,2,1,0:T(8,128)(2,1)S(1)}, bf16[1,4,8,16,128]{4,3,2,1,0:T(8,128)(2,1)}, u32[]{:S(2)}) copy-start(bf16[1,4,8,16,128]{4,3,2,1,0:T(8,128)(2,1)} %param.7) | copy-start | bytes 393220
  0.7 7.5 %copy-start.3 = (bf16[1,4,8,16,128]{4,3,2,1,0:T(8,128)(2,1)S(1)}, bf16[1,4,8,16,128]{4,3,2,1,0:T(8,128)(2,1)}, u32[]{:S(2)}) copy-start(bf16[1,4,8,16,128]{4,3,2,1,0:T(8,128)(2,1)} %param.4) | copy-start | bytes 393220
  1.7 8.1 %collective-permute-start = (bf16[2,128,128]{2,1,0:T(8,128)(2,1)S(1)}, bf16[2,128,128]{2,1,0:T(8,128)(2,1)S(1)}, u32[]{:S(2)}, u32[]{:S(2)}) collective-permute-start(bf16[2,128,128]{2,1,0:T(8,128)(2,1)S(1)} %get-tuple-element.34), channel_id=1, source_target_pairs={{2,4},{6,8},{10,12},{14,16},{18,20},{22,24},{26,28},{4,2},{8,6},{1... | collective-permute-start | bytes 196616 | tf_op jit(solution)/shard_map/ppermute | solution.py:256
  2.4 8.9 %collective-permute-start.1 = (bf16[2,128,128]{2,1,0:T(8,128)(2,1)S(1)}, bf16[2,128,128]{2,1,0:T(8,128)(2,1)S(1)}, u32[]{:S(2)}, u32[]{:S(2)}) collective-permute-start(bf16[2,128,128]{2,1,0:T(8,128)(2,1)S(1)} %get-tuple-element.35), channel_id=1, source_target_pairs={{0,2},{4,6},{8,10},{12,14},{16,18},{20,22},{24,26},{28,30},{2,0},{... | collective-permute-start | bytes 196616 | tf_op jit(solution)/shard_map/ppermute | solution.py:256
  12.0 1.7 %collective-permute-start.2 = (bf16[10,128,128]{2,1,0:T(8,128)(2,1)S(1)}, bf16[10,128,128]{2,1,0:T(8,128)(2,1)S(1)}, u32[]{:S(2)}, u32[]{:S(2)}) collective-permute-start(bf16[10,128,128]{2,1,0:T(8,128)(2,1)S(1)} %get-tuple-element.40), channel_id=1, source_target_pairs={{0,1},{1,0},{2,3},{3,2},{4,5},{5,4},{6,7},{7,6},{8,9},{9,8},{10,11... | collective-permute-start | bytes 983048 | tf_op jit(solution)/shard_map/ppermute | solution.py:260
  14.9 6.0 %collective-permute-start.4 = (bf16[4,216,128]{2,1,0:T(8,128)(2,1)S(1)}, bf16[4,216,128]{2,1,0:T(8,128)(2,1)S(1)}, u32[]{:S(2)}, u32[]{:S(2)}) collective-permute-start(bf16[4,216,128]{2,1,0:T(8,128)(2,1)S(1)} %get-tuple-element.47), channel_id=1, source_target_pairs={{0,2},{1,5},{2,0},{3,7},{4,6},{5,1},{6,4},{7,3},{8,10},{9,13},{10,... | collective-permute-start | bytes 663560 | tf_op jit(solution)/shard_map/ppermute | solution.py:266
  16.8 9.7 %collective-permute-start.3 = (bf16[4,216,128]{2,1,0:T(8,128)(2,1)S(1)}, bf16[4,216,128]{2,1,0:T(8,128)(2,1)S(1)}, u32[]{:S(2)}, u32[]{:S(2)}) collective-permute-start(bf16[4,216,128]{2,1,0:T(8,128)(2,1)S(1)} %get-tuple-element.42), channel_id=1, source_target_pairs={{0,2},{1,5},{2,0},{3,7},{4,6},{5,1},{6,4},{7,3},{8,10},{9,13},{10,... | collective-permute-start | bytes 663560 | tf_op jit(solution)/shard_map/ppermute | solution.py:266
  20.9 6.0 %collective-permute-start.5 = (bf16[4,216,128]{2,1,0:T(8,128)(2,1)S(1)}, bf16[4,216,128]{2,1,0:T(8,128)(2,1)S(1)}, u32[]{:S(2)}, u32[]{:S(2)}) collective-permute-start(bf16[4,216,128]{2,1,0:T(8,128)(2,1)S(1)} %add_convert_fusion), channel_id=1, source_target_pairs={{0,4},{1,3},{2,6},{3,1},{4,0},{5,7},{6,2},{7,5},{8,12},{9,11},{10,... | collective-permute-start | bytes 663560 | tf_op jit(solution)/shard_map/ppermute | solution.py:266
  22.1 9.7 %collective-permute-start.10 = (bf16[2,128,128]{2,1,0:T(8,128)(2,1)S(1)}, bf16[2,128,128]{2,1,0:T(8,128)(2,1)S(1)}, u32[]{:S(2)}, u32[]{:S(2)}) collective-permute-start(bf16[2,128,128]{2,1,0:T(8,128)(2,1)S(1)} %get-tuple-element.54), channel_id=1, source_target_pairs={{2,4},{6,8},{10,12},{14,16},{18,20},{22,24},{26,28},{4,2},{8,6},{1... | collective-permute-start | bytes 196616 | tf_op jit(solution)/shard_map/ppermute | solution.py:256
  22.8 9.0 %collective-permute-start.9 = (bf16[2,128,128]{2,1,0:T(8,128)(2,1)S(1)}, bf16[2,128,128]{2,1,0:T(8,128)(2,1)S(1)}, u32[]{:S(2)}, u32[]{:S(2)}) collective-permute-start(bf16[2,128,128]{2,1,0:T(8,128)(2,1)S(1)} %get-tuple-element.53), channel_id=1, source_target_pairs={{0,2},{4,6},{8,10},{12,14},{16,18},{20,22},{24,26},{28,30},{2,0},{... | collective-permute-start | bytes 196616 | tf_op jit(solution)/shard_map/ppermute | solution.py:256
  27.0 6.1 %collective-permute-start.6 = (bf16[216,128]{1,0:T(8,128)(2,1)S(1)}, bf16[216,128]{1,0:T(8,128)(2,1)S(1)}, u32[]{:S(2)}, u32[]{:S(2)}) collective-permute-start(bf16[216,128]{1,0:T(8,128)(2,1)S(1)} %get-tuple-element.70), channel_id=1, source_target_pairs={{0,16},{1,17},{2,18},{3,19},{4,20},{5,21},{6,22},{7,23},{8,24},{9,... | collective-permute-start | bytes 165896 | tf_op jit(solution)/shard_map/ppermute | solution.py:266
  30.2 6.1 %collective-permute-start.7 = (bf16[216,128]{1,0:T(8,128)(2,1)S(1)}, bf16[216,128]{1,0:T(8,128)(2,1)S(1)}, u32[]{:S(2)}, u32[]{:S(2)}) collective-permute-start(bf16[216,128]{1,0:T(8,128)(2,1)S(1)} %get-tuple-element.69), channel_id=1, source_target_pairs={{0,24},{1,25},{2,26},{3,27},{4,28},{5,29},{6,30},{7,31},{8,16},{9,... | collective-permute-start | bytes 165896 | tf_op jit(solution)/shard_map/ppermute | solution.py:266
  31.5 4.7 %collective-permute-start.8 = (bf16[216,128]{1,0:T(8,128)(2,1)S(1)}, bf16[216,128]{1,0:T(8,128)(2,1)S(1)}, u32[]{:S(2)}, u32[]{:S(2)}) collective-permute-start(bf16[216,128]{1,0:T(8,128)(2,1)S(1)} %get-tuple-element.68), channel_id=1, source_target_pairs={{0,8},{1,9},{2,10},{3,11},{4,12},{5,13},{6,14},{7,15},{8,0},{9,1},... | collective-permute-start | bytes 165896 | tf_op jit(solution)/shard_map/ppermute | solution.py:266
  36.3 1.4 %collective-permute-start.11 = (f32[216,128]{1,0:T(8,128)S(1)}, f32[216,128]{1,0:T(8,128)S(1)}, u32[]{:S(2)}, u32[]{:S(2)}) collective-permute-start(f32[216,128]{1,0:T(8,128)S(1)} %fusion.2), channel_id=1, source_target_pairs={{0,1},{1,0},{2,3},{3,2},{4,5},{5,4},{6,7},{7,6},{8,9},{9,8},{10,11... | collective-permute-start | bytes 331784 | tf_op jit(solution)/shard_map/ppermute | solution.py:260

commit v8 on v7

--- a/solution.py
+++ b/solution.py
@@ -205,17 +205,25 @@
     kernel_sums(width, other, acc, patches, turned, own_sums)
 
 
-def relative_sums_kernel(width, distance, own_sums, other, stay, pass_on, send_stay, send_on, acc, patches, turned):
-    kernel_sums(width, other, acc, patches, turned, own_sums)
-    size, rows, _ = stay.shape
+def pick_blocks(acc, quarter, distance, first):
+    size, rows, _ = quarter.shape
     odd = lax.axis_index("dp") % 2
     me = lax.axis_index("tm")
-    for n, quarter in enumerate((stay, pass_on, send_stay, send_on)):
-        for r in range(size):
-            far = jnp.where(odd == 1, distance[1][n * size + r], distance[0][n * size + r])
-            block = jnp.bitwise_xor(me, far)
-            part = acc[pl.ds(pl.multiple_of(block * rows, 8), rows), :]
-            quarter[r] = part.astype(quarter.dtype)
+    for r in range(size):
+        far = jnp.where(odd == 1, distance[1][first + r], distance[0][first + r])
+        block = jnp.bitwise_xor(me, far)
+        part = acc[pl.ds(pl.multiple_of(block * rows, 8), rows), :]
+        quarter[r] = part.astype(quarter.dtype)
+
+
+def relative_sums_kernel(width, distance, own_sums, other, acc, send_on, patches, turned):
+    kernel_sums(width, other, acc, patches, turned, own_sums)
+    pick_blocks(acc, send_on, distance, 3 * send_on.shape[0])
+
+
+def rest_kernel(distance, acc, stay, pass_on, send_stay):
+    for n, quarter in enumerate((stay, pass_on, send_stay)):
+        pick_blocks(acc, quarter, distance, n * quarter.shape[0])
 
 
 def middle_kernel(width, mid, grad, one, two, out_part, in_part, mid_patches, grad_patches):
@@ -356,12 +364,15 @@
             for first, second in orders
         ]
         wide, narrow = shape((size, rows, chans), F32), shape((size, rows, chans), BF16)
-        stay, pass_on, send_stay, send_on = call(
+        sums, send_on = call(
             lambda *refs: relative_sums_kernel(width, distance, *refs),
-            [wide, wide, narrow, narrow],
-            [pltpu.VMEM((krows, chans), F32)] + scratch,
+            [shape((krows, chans), F32), narrow],
+            scratch,
             conv_flops,
             own_sums, other,
+        )
+        stay, pass_on, send_stay = call(
+            lambda *refs: rest_kernel(distance, *refs), [wide, wide, narrow], [], conv_flops // 4, sums
         )
         send_on, mid, grad = lax.optimization_barrier((send_on, mid, grad))
         parts = middle(mid, grad)

time: 38.6 us -> 38.5 us (level)
    pallas_call x7 -> x8, Pallas kernels: 8.57 us -> 8.57 us  [call(): pl.pallas_call(body, out_shape=outs, in_specs=[anywhere if i in unplaced...]
where the time goes in v8:
time: 38.5 us; the launch traced here: 38.3 us
  starting transfers between devices  19 us (49%)
  waiting for transfers between devices  9.1 us (24%)
  Pallas kernels  8.57 us (22%)
  other arithmetic  0.88 us (2%)
  between operations  0.79 us (2%)
    ppermute x4, starting transfers between devices, paired(): return lax.ppermute(block, 'tm', pairs + [(j, i) for i, j in pairs])  10.7 us
    pallas_call x8, Pallas kernels, call(): pl.pallas_call(body, out_shape=outs, in_specs=[anywhere if i in unplaced...  8.57 us
    ppermute x6, starting transfers between devices, exchanged(): return lax.ppermute(send, ('tm', 'dp'), route)  8.08 us
    ppermute x6, waiting for transfers between devices, exchanged(): return lax.ppermute(send, ('tm', 'dp'), route)  5.8 us
    ppermute x2, waiting for transfers between devices, swapped(): lax.ppermute(block, 'dp', [(i, i ^ 1) for i in range(lax.axis_size('dp'))])  1.87 us
    ppermute x4, waiting for transfers between devices, paired(): return lax.ppermute(block, 'tm', pairs + [(j, i) for i, j in pairs])  1.43 us
  transfers between devices with their start and end apart: 12, of which 6 were waited for; matrix products, arithmetic and copies ran while one was open for 0% of the time, Pallas kernels for 15%

profile of v8, /device:TPU:0, one launch (start us, length us, event | category | flops | bytes accessed | tf_op | source)
XLA Modules:
  0.0 38.3 jit_solution(7470781665190087901)
XLA Ops:
  0.7 1.0 %shard_map.75 = (bf16[2,128,128]{2,1,0:T(8,128)(2,1)S(1)}, bf16[2,128,128]{2,1,0:T(8,128)(2,1)S(1)}) custom-call(bf16[4,128,128]{2,1,0:T(8,128)(2,1)} %bitcast.22, bf16[4,128,128]{2,1,0:T(8,128)(2,1)} %bitcast.18), custom_call_target="tpu_custom_call" | custom-call | flops 8000000000 | bytes 393216 | tf_op jit(solution)/shard_map/pallas_call | solution.py:251
  1.7 0.7 %collective-permute-start = (bf16[2,128,128]{2,1,0:T(8,128)(2,1)S(1)}, bf16[2,128,128]{2,1,0:T(8,128)(2,1)S(1)}, u32[]{:S(2)}, u32[]{:S(2)}) collective-permute-start(bf16[2,128,128]{2,1,0:T(8,128)(2,1)S(1)} %get-tuple-element.35), channel_id=1, source_target_pairs={{2,4},{6,8},{10,12},{14,16},{18,20},{22,24},{26,28},{4,2},{8,6},{1... | collective-permute-start | bytes 196616 | tf_op jit(solution)/shard_map/ppermute | solution.py:264
  2.4 5.7 %collective-permute-start.1 = (bf16[2,128,128]{2,1,0:T(8,128)(2,1)S(1)}, bf16[2,128,128]{2,1,0:T(8,128)(2,1)S(1)}, u32[]{:S(2)}, u32[]{:S(2)}) collective-permute-start(bf16[2,128,128]{2,1,0:T(8,128)(2,1)S(1)} %get-tuple-element.36), channel_id=1, source_target_pairs={{0,2},{4,6},{8,10},{12,14},{16,18},{20,22},{24,26},{28,30},{2,0},{... | collective-permute-start | bytes 196616 | tf_op jit(solution)/shard_map/ppermute | solution.py:264
  8.1 1.7 %shard_map.76 = (bf16[4,128,128]{2,1,0:T(8,128)(2,1)S(1)}, f32[512,128]{1,0:T(8,128)S(1)}, f32[512,128]{1,0:T(8,128)S(1)}) custom-call(bf16[4,128,128]{2,1,0:T(8,128)(2,1)S(1)} %bitcast.23, bf16[4,128,128]{2,1,0:T(8,128)(2,1)S(1)} %bitcast.19, bf16[3456,128]{1,0:T(8,128)(2,1)S(1)} %copy-done, bf16[3456,128]{1,0:T(8,128)(2,1)S(1)} %copy-done.1), custom_call_target="tpu_custom_call" | custom-call | flops 679477248 | bytes 2686976 | tf_op jit(solution)/shard_map/pallas_call | solution.py:251
  9.8 1.4 %collective-permute-done.1.refs_1_ = bf16[2,128,128]{2,1,0:T(8,128)(2,1)S(1)} collective-permute-done((bf16[2,128,128]{2,1,0:T(8,128)(2,1)S(1)}, bf16[2,128,128]{2,1,0:T(8,128)(2,1)S(1)}, u32[]{:S(2)}, u32[]{:S(2)}) %collective-permute-start.1) | collective-permute-done | bytes 65568 | tf_op jit(solution)/shard_map/ppermute | solution.py:264
  11.3 0.7 %shard_map.77 = (bf16[10,128,128]{2,1,0:T(8,128)(2,1)S(1)}, bf16[10,128,128]{2,1,0:T(8,128)(2,1)S(1)}, bf16[4,128,128]{2,1,0:T(8,128)(2,1)S(1)}, bf16[4,128,128]...) custom-call(bf16[2,128,128]{2,1,0:T(8,128)(2,1)S(1)} %collective-permute-done.refs_0_, ...), custom_call_target="tpu_custom_call" | custom-call | flops 226492416 | bytes 3735552 | tf_op jit(solution)/shard_map/pallas_call | solution.py:251
  12.0 0.1 collective-permute-start.2
  12.1 1.0 %shard_map.78.refs_0_ = f32[3456,128]{1,0:T(8,128)S(1)} custom-call(bf16[10,128,128]{2,1,0:T(8,128)(2,1)S(1)} %get-tuple-element.40.refs_0_), custom_call_target="tpu_custom_call" | custom-call | flops 452984832 | bytes 2097152 | tf_op jit(solution)/shard_map/pallas_call | solution.py:251
  13.1 0.6 %collective-permute-done.2.refs_1_ = bf16[10,128,128]{2,1,0:T(8,128)(2,1)S(1)} collective-permute-done((bf16[10,128,128]{2,1,0:T(8,128)(2,1)S(1)}, bf16[10,128,128]{2,1,0:T(8,128)(2,1)S(1)}, u32[]{:S(2)}, u32[]{:S(2)}) %collective-permute-start.2) | collective-permute-done | bytes 327712 | tf_op jit(solution)/shard_map/ppermute | solution.py:268
  13.7 1.1 %shard_map.79 = (f32[3456,128]{1,0:T(8,128)S(1)}, bf16[4,216,128]{2,1,0:T(8,128)(2,1)S(1)}) custom-call(f32[3456,128]{1,0:T(8,128)S(1)} %shard_map.78.refs_0_, bf16[10,128,128]{2,1,0:T(8,128)(2,1)S(1)} %collective-permute-done.2.refs_1_), custom_call_target="tpu_custom_call" | custom-call | flops 452984832 | bytes 4087808 | tf_op jit(solution)/shard_map/pallas_call | solution.py:251
  14.8 1.9 %collective-permute-start.4 = (bf16[4,216,128]{2,1,0:T(8,128)(2,1)S(1)}, bf16[4,216,128]{2,1,0:T(8,128)(2,1)S(1)}, u32[]{:S(2)}, u32[]{:S(2)}) collective-permute-start(bf16[4,216,128]{2,1,0:T(8,128)(2,1)S(1)} %get-tuple-element.49), channel_id=1, source_target_pairs={{0,2},{1,5},{2,0},{3,7},{4,6},{5,1},{6,4},{7,3},{8,10},{9,13},{10,... | collective-permute-start | bytes 663560 | tf_op jit(solution)/shard_map/ppermute | solution.py:274
  16.7 0.1 shard_map.80
  16.8 0.2 collective-permute-start.3
  17.0 1.6 %shard_map.81 = (f32[512,128]{1,0:T(8,128)S(1)}, f32[512,128]{1,0:T(8,128)S(1)}) custom-call(bf16[4,128,128]{2,1,0:T(8,128)(2,1)S(1)} %get-tuple-element.50.refs_0_, bf16[4,128,128]{2,1,0:T(8,128)(2,1)S(1)} %get-tuple-element.51.refs_1_, bf16[3456,128]{1,0:T(8,128)(2,1)S(1)} %copy-done, bf16[3456,128]{1,0:T(8,128)(2,1)S(1)} %copy-done.1), custom_call_target="tpu_custom_call" | custom-call | flops 679477248 | bytes 2555904 | tf_op jit(solution)/shard_map/pallas_call | solution.py:251
  18.6 2.2 %collective-permute-done.4 = bf16[4,216,128]{2,1,0:T(8,128)(2,1)S(1)} collective-permute-done((bf16[4,216,128]{2,1,0:T(8,128)(2,1)S(1)}, bf16[4,216,128]{2,1,0:T(8,128)(2,1)S(1)}, u32[]{:S(2)}, u32[]{:S(2)}) %collective-permute-start.4) | collective-permute-done | bytes 221216 | tf_op jit(solution)/shard_map/ppermute | solution.py:274
  20.8 0.1 add_convert_fusion
  20.8 1.2 %collective-permute-start.5 = (bf16[4,216,128]{2,1,0:T(8,128)(2,1)S(1)}, bf16[4,216,128]{2,1,0:T(8,128)(2,1)S(1)}, u32[]{:S(2)}, u32[]{:S(2)}) collective-permute-start(bf16[4,216,128]{2,1,0:T(8,128)(2,1)S(1)} %add_convert_fusion), channel_id=1, source_target_pairs={{0,4},{1,3},{2,6},{3,1},{4,0},{5,7},{6,2},{7,5},{8,12},{9,11},{10,... | collective-permute-start | bytes 663560 | tf_op jit(solution)/shard_map/ppermute | solution.py:274
  22.0 0.7 %collective-permute-start.10 = (bf16[2,128,128]{2,1,0:T(8,128)(2,1)S(1)}, bf16[2,128,128]{2,1,0:T(8,128)(2,1)S(1)}, u32[]{:S(2)}, u32[]{:S(2)}) collective-permute-start(bf16[2,128,128]{2,1,0:T(8,128)(2,1)S(1)} %get-tuple-element.56), channel_id=1, source_target_pairs={{2,4},{6,8},{10,12},{14,16},{18,20},{22,24},{26,28},{4,2},{8,6},{1... | collective-permute-start | bytes 196616 | tf_op jit(solution)/shard_map/ppermute | solution.py:264
  22.7 3.7 %collective-permute-start.9 = (bf16[2,128,128]{2,1,0:T(8,128)(2,1)S(1)}, bf16[2,128,128]{2,1,0:T(8,128)(2,1)S(1)}, u32[]{:S(2)}, u32[]{:S(2)}) collective-permute-start(bf16[2,128,128]{2,1,0:T(8,128)(2,1)S(1)} %get-tuple-element.55), channel_id=1, source_target_pairs={{0,2},{4,6},{8,10},{12,14},{16,18},{20,22},{24,26},{28,30},{2,0},{... | collective-permute-start | bytes 196616 | tf_op jit(solution)/shard_map/ppermute | solution.py:264
  26.4 0.5 %collective-permute-done.5 = bf16[4,216,128]{2,1,0:T(8,128)(2,1)S(1)} collective-permute-done((bf16[4,216,128]{2,1,0:T(8,128)(2,1)S(1)}, bf16[4,216,128]{2,1,0:T(8,128)(2,1)S(1)}, u32[]{:S(2)}, u32[]{:S(2)}) %collective-permute-start.5) | collective-permute-done | bytes 221216 | tf_op jit(solution)/shard_map/ppermute | solution.py:274
  26.8 0.1 fusion.3
  27.0 3.1 %collective-permute-start.6 = (bf16[216,128]{1,0:T(8,128)(2,1)S(1)}, bf16[216,128]{1,0:T(8,128)(2,1)S(1)}, u32[]{:S(2)}, u32[]{:S(2)}) collective-permute-start(bf16[216,128]{1,0:T(8,128)(2,1)S(1)} %get-tuple-element.72), channel_id=1, source_target_pairs={{0,16},{1,17},{2,18},{3,19},{4,20},{5,21},{6,22},{7,23},{8,24},{9,... | collective-permute-start | bytes 165896 | tf_op jit(solution)/shard_map/ppermute | solution.py:274
  30.1 1.3 %collective-permute-start.7 = (bf16[216,128]{1,0:T(8,128)(2,1)S(1)}, bf16[216,128]{1,0:T(8,128)(2,1)S(1)}, u32[]{:S(2)}, u32[]{:S(2)}) collective-permute-start(bf16[216,128]{1,0:T(8,128)(2,1)S(1)} %get-tuple-element.71), channel_id=1, source_target_pairs={{0,24},{1,25},{2,26},{3,27},{4,28},{5,29},{6,30},{7,31},{8,16},{9,... | collective-permute-start | bytes 165896 | tf_op jit(solution)/shard_map/ppermute | solution.py:274
  31.5 0.2 collective-permute-start.8
  31.7 0.0 collective-permute-done.10.refs_3_
  31.7 0.0 collective-permute-done.9.refs_2_
  31.7 1.3 %shard_map.82 = (bf16[4,128,128]{2,1,0:T(8,128)(2,1)}, bf16[4,128,128]{2,1,0:T(8,128)(2,1)}) custom-call(bf16[4,128,128]{2,1,0:T(8,128)(2,1)S(1)} %bitcast.24, bf16[4,128,128]{2,1,0:T(8,128)(2,1)S(1)} %bitcast.21, bf16[2,128,128]{2,1,0:T(8,128)(2,1)S(1)} %collective-permute-done.9.refs_2_, bf16[2,128,128]{2,1,0:T(8,128)(2,1)S(1)} %collective-permute-done.10.refs_3_, ...), custom_call_target="tpu_custom_call" | custom-call | flops 226492416 | bytes 2949120 | tf_op jit(solution)/shard_map/pallas_call | solution.py:251
  33.0 3.1 %collective-permute-done.7 = bf16[216,128]{1,0:T(8,128)(2,1)S(1)} collective-permute-done((bf16[216,128]{1,0:T(8,128)(2,1)S(1)}, bf16[216,128]{1,0:T(8,128)(2,1)S(1)}, u32[]{:S(2)}, u32[]{:S(2)}) %collective-permute-start.7) | collective-permute-done | bytes 55328 | tf_op jit(solution)/shard_map/ppermute | solution.py:274
  36.2 0.0 collective-permute-done.8
  36.2 0.1 collective-permute-start.11
  36.3 1.3 %collective-permute-done.11 = f32[216,128]{1,0:T(8,128)S(1)} collective-permute-done((f32[216,128]{1,0:T(8,128)S(1)}, f32[216,128]{1,0:T(8,128)S(1)}, u32[]{:S(2)}, u32[]{:S(2)}) %collective-permute-start.11) | collective-permute-done | bytes 110624 | tf_op jit(solution)/shard_map/ppermute | solution.py:268
  37.6 0.7 %broadcast_select_fusion = (f32[216,128]{1,0:T(8,128)}, f32[216,128]{1,0:T(8,128)}) fusion(f32[216,128]{1,0:T(8,128)S(1)} %collective-permute-done.11, f32[216,128]{1,0:T(8,128)S(1)} %fusion.2, pred[]{:T(512)S(6)} %eq.5), kind=kLoop, calls=%fused_computation.9 | loop fusion | flops 55296 | bytes 442369 | tf_op jit(solution)/shard_map/jit(_where)/select_n | solution.py:406
  (13 shorter events, 0.1 us)
Async XLA Ops:
  0.6 7.5 %copy-start = (bf16[3456,128]{1,0:T(8,128)(2,1)S(1)}, bf16[3456,128]{1,0:T(8,128)(2,1)}, u32[]{:S(2)}) copy-start(bf16[3456,128]{1,0:T(8,128)(2,1)} %refs_6_.3) | copy-start | bytes 2654212
  0.6 7.5 %copy-start.1 = (bf16[3456,128]{1,0:T(8,128)(2,1)S(1)}, bf16[3456,128]{1,0:T(8,128)(2,1)}, u32[]{:S(2)}) copy-start(bf16[3456,128]{1,0:T(8,128)(2,1)} %refs_7_.3) | copy-start | bytes 2654212
  0.7 7.5 %copy-start.2 = (bf16[1,4,8,16,128]{4,3,2,1,0:T(8,128)(2,1)S(1)}, bf16[1,4,8,16,128]{4,3,2,1,0:T(8,128)(2,1)}, u32[]{:S(2)}) copy-start(bf16[1,4,8,16,128]{4,3,2,1,0:T(8,128)(2,1)} %param.7) | copy-start | bytes 393220
  0.7 7.5 %copy-start.3 = (bf16[1,4,8,16,128]{4,3,2,1,0:T(8,128)(2,1)S(1)}, bf16[1,4,8,16,128]{4,3,2,1,0:T(8,128)(2,1)}, u32[]{:S(2)}) copy-start(bf16[1,4,8,16,128]{4,3,2,1,0:T(8,128)(2,1)} %param.4) | copy-start | bytes 393220
  1.7 8.1 %collective-permute-start = (bf16[2,128,128]{2,1,0:T(8,128)(2,1)S(1)}, bf16[2,128,128]{2,1,0:T(8,128)(2,1)S(1)}, u32[]{:S(2)}, u32[]{:S(2)}) collective-permute-start(bf16[2,128,128]{2,1,0:T(8,128)(2,1)S(1)} %get-tuple-element.35), channel_id=1, source_target_pairs={{2,4},{6,8},{10,12},{14,16},{18,20},{22,24},{26,28},{4,2},{8,6},{1... | collective-permute-start | bytes 196616 | tf_op jit(solution)/shard_map/ppermute | solution.py:264
  2.4 8.9 %collective-permute-start.1 = (bf16[2,128,128]{2,1,0:T(8,128)(2,1)S(1)}, bf16[2,128,128]{2,1,0:T(8,128)(2,1)S(1)}, u32[]{:S(2)}, u32[]{:S(2)}) collective-permute-start(bf16[2,128,128]{2,1,0:T(8,128)(2,1)S(1)} %get-tuple-element.36), channel_id=1, source_target_pairs={{0,2},{4,6},{8,10},{12,14},{16,18},{20,22},{24,26},{28,30},{2,0},{... | collective-permute-start | bytes 196616 | tf_op jit(solution)/shard_map/ppermute | solution.py:264
  12.0 1.7 %collective-permute-start.2 = (bf16[10,128,128]{2,1,0:T(8,128)(2,1)S(1)}, bf16[10,128,128]{2,1,0:T(8,128)(2,1)S(1)}, u32[]{:S(2)}, u32[]{:S(2)}) collective-permute-start(bf16[10,128,128]{2,1,0:T(8,128)(2,1)S(1)} %get-tuple-element.41), channel_id=1, source_target_pairs={{0,1},{1,0},{2,3},{3,2},{4,5},{5,4},{6,7},{7,6},{8,9},{9,8},{10,11... | collective-permute-start | bytes 983048 | tf_op jit(solution)/shard_map/ppermute | solution.py:268
  14.8 6.0 %collective-permute-start.4 = (bf16[4,216,128]{2,1,0:T(8,128)(2,1)S(1)}, bf16[4,216,128]{2,1,0:T(8,128)(2,1)S(1)}, u32[]{:S(2)}, u32[]{:S(2)}) collective-permute-start(bf16[4,216,128]{2,1,0:T(8,128)(2,1)S(1)} %get-tuple-element.49), channel_id=1, source_target_pairs={{0,2},{1,5},{2,0},{3,7},{4,6},{5,1},{6,4},{7,3},{8,10},{9,13},{10,... | collective-permute-start | bytes 663560 | tf_op jit(solution)/shard_map/ppermute | solution.py:274
  16.8 9.6 %collective-permute-start.3 = (bf16[4,216,128]{2,1,0:T(8,128)(2,1)S(1)}, bf16[4,216,128]{2,1,0:T(8,128)(2,1)S(1)}, u32[]{:S(2)}, u32[]{:S(2)}) collective-permute-start(bf16[4,216,128]{2,1,0:T(8,128)(2,1)S(1)} %get-tuple-element.44), channel_id=1, source_target_pairs={{0,2},{1,5},{2,0},{3,7},{4,6},{5,1},{6,4},{7,3},{8,10},{9,13},{10,... | collective-permute-start | bytes 663560 | tf_op jit(solution)/shard_map/ppermute | solution.py:274
  20.8 6.0 %collective-permute-start.5 = (bf16[4,216,128]{2,1,0:T(8,128)(2,1)S(1)}, bf16[4,216,128]{2,1,0:T(8,128)(2,1)S(1)}, u32[]{:S(2)}, u32[]{:S(2)}) collective-permute-start(bf16[4,216,128]{2,1,0:T(8,128)(2,1)S(1)} %add_convert_fusion), channel_id=1, source_target_pairs={{0,4},{1,3},{2,6},{3,1},{4,0},{5,7},{6,2},{7,5},{8,12},{9,11},{10,... | collective-permute-start | bytes 663560 | tf_op jit(solution)/shard_map/ppermute | solution.py:274
  22.0 9.7 %collective-permute-start.10 = (bf16[2,128,128]{2,1,0:T(8,128)(2,1)S(1)}, bf16[2,128,128]{2,1,0:T(8,128)(2,1)S(1)}, u32[]{:S(2)}, u32[]{:S(2)}) collective-permute-start(bf16[2,128,128]{2,1,0:T(8,128)(2,1)S(1)} %get-tuple-element.56), channel_id=1, source_target_pairs={{2,4},{6,8},{10,12},{14,16},{18,20},{22,24},{26,28},{4,2},{8,6},{1... | collective-permute-start | bytes 196616 | tf_op jit(solution)/shard_map/ppermute | solution.py:264
  22.7 9.0 %collective-permute-start.9 = (bf16[2,128,128]{2,1,0:T(8,128)(2,1)S(1)}, bf16[2,128,128]{2,1,0:T(8,128)(2,1)S(1)}, u32[]{:S(2)}, u32[]{:S(2)}) collective-permute-start(bf16[2,128,128]{2,1,0:T(8,128)(2,1)S(1)} %get-tuple-element.55), channel_id=1, source_target_pairs={{0,2},{4,6},{8,10},{12,14},{16,18},{20,22},{24,26},{28,30},{2,0},{... | collective-permute-start | bytes 196616 | tf_op jit(solution)/shard_map/ppermute | solution.py:264
  27.0 6.1 %collective-permute-start.6 = (bf16[216,128]{1,0:T(8,128)(2,1)S(1)}, bf16[216,128]{1,0:T(8,128)(2,1)S(1)}, u32[]{:S(2)}, u32[]{:S(2)}) collective-permute-start(bf16[216,128]{1,0:T(8,128)(2,1)S(1)} %get-tuple-element.72), channel_id=1, source_target_pairs={{0,16},{1,17},{2,18},{3,19},{4,20},{5,21},{6,22},{7,23},{8,24},{9,... | collective-permute-start | bytes 165896 | tf_op jit(solution)/shard_map/ppermute | solution.py:274
  30.1 6.1 %collective-permute-start.7 = (bf16[216,128]{1,0:T(8,128)(2,1)S(1)}, bf16[216,128]{1,0:T(8,128)(2,1)S(1)}, u32[]{:S(2)}, u32[]{:S(2)}) collective-permute-start(bf16[216,128]{1,0:T(8,128)(2,1)S(1)} %get-tuple-element.71), channel_id=1, source_target_pairs={{0,24},{1,25},{2,26},{3,27},{4,28},{5,29},{6,30},{7,31},{8,16},{9,... | collective-permute-start | bytes 165896 | tf_op jit(solution)/shard_map/ppermute | solution.py:274
  31.5 4.7 %collective-permute-start.8 = (bf16[216,128]{1,0:T(8,128)(2,1)S(1)}, bf16[216,128]{1,0:T(8,128)(2,1)S(1)}, u32[]{:S(2)}, u32[]{:S(2)}) collective-permute-start(bf16[216,128]{1,0:T(8,128)(2,1)S(1)} %get-tuple-element.70), channel_id=1, source_target_pairs={{0,8},{1,9},{2,10},{3,11},{4,12},{5,13},{6,14},{7,15},{8,0},{9,1},... | collective-permute-start | bytes 165896 | tf_op jit(solution)/shard_map/ppermute | solution.py:274
  36.2 1.4 %collective-permute-start.11 = (f32[216,128]{1,0:T(8,128)S(1)}, f32[216,128]{1,0:T(8,128)S(1)}, u32[]{:S(2)}, u32[]{:S(2)}) collective-permute-start(f32[216,128]{1,0:T(8,128)S(1)} %fusion.2), channel_id=1, source_target_pairs={{0,1},{1,0},{2,3},{3,2},{4,5},{5,4},{6,7},{7,6},{8,9},{9,8},{10,11... | collective-permute-start | bytes 331784 | tf_op jit(solution)/shard_map/ppermute | solution.py:268
